TPU v7x, 512 devices: a whole 4x8x8 slice. The times are simulated.
512 devices in a mesh: wave: 8 (over y_hi, x), tile: 64 (over z, y_lo, core).
Axes of the slice: x: 4, y: 8 (y_hi: 2, y_lo: 4; y = y_hi * 4 + y_lo), z: 8, core: 2. Of those that a mesh axis runs over, the one named last changes fastest.
Arguments:
- e_forward: float32 [8, 3, 1024, 16, 128], P('wave', None, 'tile'), may hold values from -6 to 6
- h_forward: float32 [8, 3, 1024, 16, 128], P('wave', None, 'tile'), may hold values from -6 to 6
- e_adjoint: float32 [8, 3, 1024, 16, 128], P('wave', None, 'tile'), may hold values from -6 to 6
- h_adjoint: float32 [8, 3, 1024, 16, 128], P('wave', None, 'tile'), may hold values from -6 to 6
- eps_table: float32 [8, 4], P('wave'), may hold values from 1 to 6
- material: int32 [1024, 16, 128], P('tile'), may hold values from 0 to 3
- pml_depth: int32 [1024, 16, 128], P('tile'), may hold values from 0 to 4
- design_start: int32 [64], P('tile'), may hold values from 0 to 112
Outputs:
- e_forward_out: float32 [8, 3, 1024, 16, 128], P('wave', None, 'tile')
- h_forward_out: float32 [8, 3, 1024, 16, 128], P('wave', None, 'tile')
- e_adjoint_out: float32 [8, 3, 1024, 16, 128], P('wave', None, 'tile')
- h_adjoint_out: float32 [8, 3, 1024, 16, 128], P('wave', None, 'tile')
- gradient: float32 [1024, 16, 16], P('tile')
All inputs are finite; a program needn't handle non-finite values.
Results may differ from a plain program's by a relative error of at most 0.0003.
Values sent between devices are 32-bit elements; how exact they have to be, the bound alone decides.
No kernel may reach another device: no remote copies, remote signals or barrier semaphores. Data moves between devices by JAX's collectives and lax.ppermute only.
A program may use at most 64 MiB of HBM per device.

v0:
```python
import jax
import jax.numpy as jnp
from jax import lax
from jax.sharding import PartitionSpec as P

STEPS = 4
DZ = 16
TILE_COLS = 8


dt_step = 0.5
depth_scale = 4.0


def from_behind(value, axis, steps):
    count = lax.axis_size(axis)
    initial, last = (max(0, -steps), min(count, count - steps))
    return lax.ppermute(value, axis, [(source, source + steps) for source in range(initial, last)])


def ahead(field, after, axis):
    moved = jnp.concatenate(
        [lax.slice_in_dim(field, 1, field.shape[axis], axis=axis), after], axis=axis
    )
    return moved - field


def behind(field, before, axis):
    moved = jnp.concatenate(
        [before, lax.slice_in_dim(field, 0, field.shape[axis] - 1, axis=axis)], axis=axis
    )
    return field - moved


def curl_ahead(vector, next_x, next_y):
    flat = jnp.zeros(vector.shape[1:3] + (1,), vector.dtype)
    return jnp.stack(
        [
            ahead(vector[2], next_y[1], 1) - ahead(vector[1], flat, 2),
            ahead(vector[0], flat, 2) - ahead(vector[2], next_x[1], 0),
            ahead(vector[1], next_x[0], 0) - ahead(vector[0], next_y[0], 1),
        ]
    )


def curl_behind(vector, prev_x, prev_y):
    flat = jnp.zeros(vector.shape[1:3] + (1,), vector.dtype)
    return jnp.stack(
        [
            behind(vector[2], prev_y[1], 1) - behind(vector[1], flat, 2),
            behind(vector[0], flat, 2) - behind(vector[2], prev_x[1], 0),
            behind(vector[1], prev_x[0], 0) - behind(vector[0], prev_y[0], 1),
        ]
    )


def electric_faces(first, second, cols, keep_next):
    faces_x = jnp.concatenate([first[1:3, :1], second[1:3, :1]])
    faces_y = jnp.concatenate([first[::2, :, :1], second[::2, :, :1]])
    got_x = from_behind(faces_x, "tile", -cols)
    got_y = from_behind(faces_y, "tile", -1) * keep_next
    return (got_x, got_y)


def magnetic_faces(first, second, cols, keep_prev):
    faces_x = jnp.concatenate([first[1:3, -1:], second[1:3, -1:]])
    faces_y = jnp.concatenate([first[::2, :, -1:], second[::2, :, -1:]])
    got_x = from_behind(faces_x, "tile", cols)
    got_y = from_behind(faces_y, "tile", 1) * keep_prev
    return (got_x, got_y)


def coefficients(table, kind, depth):
    kinds = jnp.arange(table.shape[0], dtype=jnp.int32)
    onehot = (kind[None] == kinds[:, None, None, None]).astype(jnp.float32)
    eps = jnp.sum(onehot * table[:, None, None, None], axis=0)
    ramp = depth.astype(jnp.float32) / depth_scale
    sigma = ramp * ramp
    s_e = sigma * dt_step / (2.0 * eps)
    s_h = sigma * dt_step / 2.0
    return (
        (1.0 - s_e) / (1.0 + s_e),
        dt_step / (eps * (1.0 + s_e)),
        (1.0 - s_h) / (1.0 + s_h),
        dt_step / (1.0 + s_h),
    )


def add_term(gradient, term):
    return gradient + term


def per_device(
    e_forward, h_forward, e_adjoint, h_adjoint, eps_table, material, pml_depth, design_start
):
    cols = TILE_COLS
    column = lax.axis_index("tile") % cols
    keep_next = (column < cols - 1).astype(jnp.float32)
    keep_prev = (column > 0).astype(jnp.float32)
    ca, cb, da, db = coefficients(eps_table[0], material, pml_depth)
    start = design_start[0]
    ef, hf, ea, ha = (e_forward[0], h_forward[0], e_adjoint[0], h_adjoint[0])
    gradient = jnp.zeros(material.shape[:2] + (DZ,), jnp.float32)
    for step in range(STEPS):
        got_x, got_y = electric_faces(ef, ea, cols, keep_next)
        hf = da * hf - db * curl_ahead(ef, got_x[:2], got_y[:2])
        ha = da * ha - db * curl_ahead(ea, got_x[2:], got_y[2:])
        got_x, got_y = magnetic_faces(hf, ha, cols, keep_prev)
        ef = ca * ef + cb * curl_behind(hf, got_x[:2], got_y[:2])
        ea = ca * ea + cb * curl_behind(ha, got_x[2:], got_y[2:])
        term = lax.dynamic_slice_in_dim(jnp.sum(ef * ea, axis=0), start, DZ, 2)
        gradient = add_term(gradient, term)
    gradient = lax.psum(gradient, "wave")
    return (ef[None], hf[None], ea[None], ha[None], gradient)


def solution(mesh):
    return jax.shard_map(
        per_device,
        mesh=mesh,
        in_specs=(
            P("wave", None, "tile", None, None),
            P("wave", None, "tile", None, None),
            P("wave", None, "tile", None, None),
            P("wave", None, "tile", None, None),
            P("wave", None),
            P("tile", None, None),
            P("tile", None, None),
            P("tile"),
        ),
        out_specs=(
            P("wave", None, "tile", None, None),
            P("wave", None, "tile", None, None),
            P("wave", None, "tile", None, None),
            P("wave", None, "tile", None, None),
            P("tile", None, None),
        ),
        check_vma=False,
    )
```

profile of v0, /device:TPU:192, one launch (start us, length us, event | category | flops | bytes accessed | tf_op | source)
XLA Modules:
  0.0 153.9 jit_solution(3697820240986314225)
XLA Ops:
  0.7 1.0 slice.969
  1.6 0.9 slice.968
  2.6 4.0 %collective-permute-start = (f32[4,16,1,128]{3,2,1,0:T(1,128)S(1)}, f32[4,16,1,128]{3,2,1,0:T(1,128)S(1)}, u32[]{:S(2)}, u32[]{:S(2)}) collective-permute-start(f32[4,16,1,128]{3,2,1,0:T(1,128)S(1)} %pad_maximum_fusion), channel_id=1, source_target_pairs={{1,0},{2,1},{3,2},{4,3},{5,4},{6,5},{7,6},{8,7},{9,8},{10,9},{11,1... | collective-permute-start | bytes 98312 | tf_op jit(solution)/shard_map/ppermute | solution.py:18
  8.1 1.9 %collective-permute-start.1 = (f32[4,1,16,128]{3,2,1,0:T(8,128)S(1)}, f32[4,1,16,128]{3,2,1,0:T(8,128)S(1)}, u32[]{:S(2)}, u32[]{:S(2)}) collective-permute-start(f32[4,1,16,128]{3,2,1,0:T(8,128)S(1)} %pad_maximum_fusion.1), channel_id=1, source_target_pairs={{8,0},{9,1},{10,2},{11,3},{12,4},{13,5},{14,6},{15,7},{16,8},{17,9... | collective-permute-start | bytes 98312 | tf_op jit(solution)/shard_map/ppermute | solution.py:18
  10.0 0.9 slice_bitcast_fusion.80
  14.6 0.9 collective-permute-done.1
  18.3 1.9 %collective-permute-start.2 = (f32[4,16,1,128]{3,2,1,0:T(1,128)S(1)}, f32[4,16,1,128]{3,2,1,0:T(1,128)S(1)}, u32[]{:S(2)}, u32[]{:S(2)}) collective-permute-start(f32[4,16,1,128]{3,2,1,0:T(1,128)S(1)} %pad_maximum_fusion.2), channel_id=1, source_target_pairs={{0,1},{1,2},{2,3},{3,4},{4,5},{5,6},{6,7},{7,8},{8,9},{9,10},{10,1... | collective-permute-start | bytes 98312 | tf_op jit(solution)/shard_map/ppermute | solution.py:18
  20.2 4.6 %collective-permute-start.3 = (f32[4,1,16,128]{3,2,1,0:T(8,128)S(1)}, f32[4,1,16,128]{3,2,1,0:T(8,128)S(1)}, u32[]{:S(2)}, u32[]{:S(2)}) collective-permute-start(f32[4,1,16,128]{3,2,1,0:T(8,128)S(1)} %pad_maximum_fusion.3), channel_id=1, source_target_pairs={{0,8},{1,9},{2,10},{3,11},{4,12},{5,13},{6,14},{7,15},{8,16},{9,17... | collective-permute-start | bytes 98312 | tf_op jit(solution)/shard_map/ppermute | solution.py:18
  24.8 1.5 collective-permute-done.2
  27.5 5.5 %collective-permute-start.4 = (f32[4,16,1,128]{3,1,2,0:T(8,128)S(1)}, f32[4,16,1,128]{3,1,2,0:T(8,128)S(1)}, u32[]{:S(2)}, u32[]{:S(2)}) collective-permute-start(f32[4,16,1,128]{3,1,2,0:T(8,128)S(1)} %pad_maximum_fusion.4), channel_id=1, source_target_pairs={{1,0},{2,1},{3,2},{4,3},{5,4},{6,5},{7,6},{8,7},{9,8},{10,9},{11,1... | collective-permute-start | bytes 98312 | tf_op jit(solution)/shard_map/ppermute | solution.py:18
  33.3 1.9 %collective-permute-start.5 = (f32[4,1,16,128]{3,2,1,0:T(8,128)S(1)}, f32[4,1,16,128]{3,2,1,0:T(8,128)S(1)}, u32[]{:S(2)}, u32[]{:S(2)}) collective-permute-start(f32[4,1,16,128]{3,2,1,0:T(8,128)S(1)} %pad_maximum_fusion.5), channel_id=1, source_target_pairs={{8,0},{9,1},{10,2},{11,3},{12,4},{13,5},{14,6},{15,7},{16,8},{17,9... | collective-permute-start | bytes 98312 | tf_op jit(solution)/shard_map/ppermute | solution.py:18
  35.3 5.4 %collective-permute-done.5 = f32[4,1,16,128]{3,2,1,0:T(8,128)S(1)} collective-permute-done((f32[4,1,16,128]{3,2,1,0:T(8,128)S(1)}, f32[4,1,16,128]{3,2,1,0:T(8,128)S(1)}, u32[]{:S(2)}, u32[]{:S(2)}) %collective-permute-start.5) | collective-permute-done | bytes 32800 | tf_op jit(solution)/shard_map/ppermute | solution.py:18
  41.4 1.9 %collective-permute-start.6 = (f32[4,16,1,128]{3,1,2,0:T(8,128)S(1)}, f32[4,16,1,128]{3,1,2,0:T(8,128)S(1)}, u32[]{:S(2)}, u32[]{:S(2)}) collective-permute-start(f32[4,16,1,128]{3,1,2,0:T(8,128)S(1)} %pad_maximum_fusion.6), channel_id=1, source_target_pairs={{0,1},{1,2},{2,3},{3,4},{4,5},{5,6},{6,7},{7,8},{8,9},{9,10},{10,1... | collective-permute-start | bytes 98312 | tf_op jit(solution)/shard_map/ppermute | solution.py:18
  43.4 3.9 %collective-permute-start.7 = (f32[4,1,16,128]{3,2,1,0:T(8,128)S(1)}, f32[4,1,16,128]{3,2,1,0:T(8,128)S(1)}, u32[]{:S(2)}, u32[]{:S(2)}) collective-permute-start(f32[4,1,16,128]{3,2,1,0:T(8,128)S(1)} %pad_maximum_fusion.7), channel_id=1, source_target_pairs={{0,8},{1,9},{2,10},{3,11},{4,12},{5,13},{6,14},{7,15},{8,16},{9,17... | collective-permute-start | bytes 98312 | tf_op jit(solution)/shard_map/ppermute | solution.py:18
  47.4 2.1 %collective-permute-done.6 = f32[4,16,1,128]{3,1,2,0:T(8,128)S(1)} collective-permute-done((f32[4,16,1,128]{3,1,2,0:T(8,128)S(1)}, f32[4,16,1,128]{3,1,2,0:T(8,128)S(1)}, u32[]{:S(2)}, u32[]{:S(2)}) %collective-permute-start.6) | collective-permute-done | bytes 32800 | tf_op jit(solution)/shard_map/ppermute | solution.py:18
  50.9 4.8 %collective-permute-start.8 = (f32[4,16,1,128]{3,2,1,0:T(1,128)S(1)}, f32[4,16,1,128]{3,2,1,0:T(1,128)S(1)}, u32[]{:S(2)}, u32[]{:S(2)}) collective-permute-start(f32[4,16,1,128]{3,2,1,0:T(1,128)S(1)} %pad_maximum_fusion.8), channel_id=1, source_target_pairs={{1,0},{2,1},{3,2},{4,3},{5,4},{6,5},{7,6},{8,7},{9,8},{10,9},{11,1... | collective-permute-start | bytes 98312 | tf_op jit(solution)/shard_map/ppermute | solution.py:18
  56.0 1.9 %collective-permute-start.9 = (f32[4,1,16,128]{3,2,1,0:T(8,128)S(1)}, f32[4,1,16,128]{3,2,1,0:T(8,128)S(1)}, u32[]{:S(2)}, u32[]{:S(2)}) collective-permute-start(f32[4,1,16,128]{3,2,1,0:T(8,128)S(1)} %pad_maximum_fusion.9), channel_id=1, source_target_pairs={{8,0},{9,1},{10,2},{11,3},{12,4},{13,5},{14,6},{15,7},{16,8},{17,9... | collective-permute-start | bytes 98312 | tf_op jit(solution)/shard_map/ppermute | solution.py:18
  58.0 5.1 %collective-permute-done.9 = f32[4,1,16,128]{3,2,1,0:T(8,128)S(1)} collective-permute-done((f32[4,1,16,128]{3,2,1,0:T(8,128)S(1)}, f32[4,1,16,128]{3,2,1,0:T(8,128)S(1)}, u32[]{:S(2)}, u32[]{:S(2)}) %collective-permute-start.9) | collective-permute-done | bytes 32800 | tf_op jit(solution)/shard_map/ppermute | solution.py:18
  63.9 1.9 %collective-permute-start.10 = (f32[4,16,1,128]{3,2,1,0:T(1,128)S(1)}, f32[4,16,1,128]{3,2,1,0:T(1,128)S(1)}, u32[]{:S(2)}, u32[]{:S(2)}) collective-permute-start(f32[4,16,1,128]{3,2,1,0:T(1,128)S(1)} %pad_maximum_fusion.10), channel_id=1, source_target_pairs={{0,1},{1,2},{2,3},{3,4},{4,5},{5,6},{6,7},{7,8},{8,9},{9,10},{10,1... | collective-permute-start | bytes 98312 | tf_op jit(solution)/shard_map/ppermute | solution.py:18
  65.8 3.9 %collective-permute-start.11 = (f32[4,1,16,128]{3,2,1,0:T(8,128)S(1)}, f32[4,1,16,128]{3,2,1,0:T(8,128)S(1)}, u32[]{:S(2)}, u32[]{:S(2)}) collective-permute-start(f32[4,1,16,128]{3,2,1,0:T(8,128)S(1)} %pad_maximum_fusion.11), channel_id=1, source_target_pairs={{0,8},{1,9},{2,10},{3,11},{4,12},{5,13},{6,14},{7,15},{8,16},{9,17... | collective-permute-start | bytes 98312 | tf_op jit(solution)/shard_map/ppermute | solution.py:18
  69.8 2.1 %collective-permute-done.10 = f32[4,16,1,128]{3,2,1,0:T(1,128)S(1)} collective-permute-done((f32[4,16,1,128]{3,2,1,0:T(1,128)S(1)}, f32[4,16,1,128]{3,2,1,0:T(1,128)S(1)}, u32[]{:S(2)}, u32[]{:S(2)}) %collective-permute-start.10) | collective-permute-done | bytes 32800 | tf_op jit(solution)/shard_map/ppermute | solution.py:18
  72.8 4.8 %collective-permute-start.12 = (f32[4,16,1,128]{3,2,1,0:T(1,128)S(1)}, f32[4,16,1,128]{3,2,1,0:T(1,128)S(1)}, u32[]{:S(2)}, u32[]{:S(2)}) collective-permute-start(f32[4,16,1,128]{3,2,1,0:T(1,128)S(1)} %pad_maximum_fusion.12), channel_id=1, source_target_pairs={{1,0},{2,1},{3,2},{4,3},{5,4},{6,5},{7,6},{8,7},{9,8},{10,9},{11,1... | collective-permute-start | bytes 98312 | tf_op jit(solution)/shard_map/ppermute | solution.py:18
  77.9 1.9 %collective-permute-start.13 = (f32[4,1,16,128]{3,2,1,0:T(8,128)S(1)}, f32[4,1,16,128]{3,2,1,0:T(8,128)S(1)}, u32[]{:S(2)}, u32[]{:S(2)}) collective-permute-start(f32[4,1,16,128]{3,2,1,0:T(8,128)S(1)} %pad_maximum_fusion.13), channel_id=1, source_target_pairs={{8,0},{9,1},{10,2},{11,3},{12,4},{13,5},{14,6},{15,7},{16,8},{17,9... | collective-permute-start | bytes 98312 | tf_op jit(solution)/shard_map/ppermute | solution.py:18
  79.8 5.1 %collective-permute-done.13 = f32[4,1,16,128]{3,2,1,0:T(8,128)S(1)} collective-permute-done((f32[4,1,16,128]{3,2,1,0:T(8,128)S(1)}, f32[4,1,16,128]{3,2,1,0:T(8,128)S(1)}, u32[]{:S(2)}, u32[]{:S(2)}) %collective-permute-start.13) | collective-permute-done | bytes 32800 | tf_op jit(solution)/shard_map/ppermute | solution.py:18
  85.7 1.9 %collective-permute-start.14 = (f32[4,16,1,128]{3,2,1,0:T(1,128)S(1)}, f32[4,16,1,128]{3,2,1,0:T(1,128)S(1)}, u32[]{:S(2)}, u32[]{:S(2)}) collective-permute-start(f32[4,16,1,128]{3,2,1,0:T(1,128)S(1)} %pad_maximum_fusion.14), channel_id=1, source_target_pairs={{0,1},{1,2},{2,3},{3,4},{4,5},{5,6},{6,7},{7,8},{8,9},{9,10},{10,1... | collective-permute-start | bytes 98312 | tf_op jit(solution)/shard_map/ppermute | solution.py:18
  87.7 0.9 fusion.27
  88.6 0.9 fusion.41
  89.5 3.9 %collective-permute-start.15 = (f32[4,1,16,128]{3,2,1,0:T(8,128)S(1)}, f32[4,1,16,128]{3,2,1,0:T(8,128)S(1)}, u32[]{:S(2)}, u32[]{:S(2)}) collective-permute-start(f32[4,1,16,128]{3,2,1,0:T(8,128)S(1)} %pad_maximum_fusion.15), channel_id=1, source_target_pairs={{0,8},{1,9},{2,10},{3,11},{4,12},{5,13},{6,14},{7,15},{8,16},{9,17... | collective-permute-start | bytes 98312 | tf_op jit(solution)/shard_map/ppermute | solution.py:18
  93.7 1.6 %collective-permute-done.15 = f32[4,1,16,128]{3,2,1,0:T(8,128)S(1)} collective-permute-done((f32[4,1,16,128]{3,2,1,0:T(8,128)S(1)}, f32[4,1,16,128]{3,2,1,0:T(8,128)S(1)}, u32[]{:S(2)}, u32[]{:S(2)}) %collective-permute-start.15) | collective-permute-done | bytes 32800 | tf_op jit(solution)/shard_map/ppermute | solution.py:18
  96.8 54.2 %psum.7 = f32[16,16,16]{2,1,0:T(8,128)} all-reduce(f32[16,16,16]{2,1,0:T(8,128)} %dynamic-slice_add_fusion), channel_id=1, replica_groups=mesh['wave'=8,'tile'=64] {'wave'}, use_global_device_ids=true, to_apply=%region_5.6 | all-reduce | flops 4096 | bytes 32768 | tf_op jit(solution)/shard_map/psum | solution.py:113
  151.0 2.0 %fusion.34 = f32[1,3,16,16,128]{4,3,2,1,0:T(8,128)} fusion(f32[1,1,16,16,128]{4,3,2,1,0:T(8,128)} %bitcast.634, f32[1,1,16,16,128]{4,3,2,1,0:T(8,128)S(1)} %bitcast.624, f32[1,1,16,16,128]{4,3,2,1,0:T(8,128)S(1)} %bitcast.622, f32[1,1,16,16,128]{4,3,2,1,0:T(8,128)} %bitcast.636, f32[1,1,16,16,128]{4,3,2,1,0:T(8,128)} %bitcast.632, ...), kind=kLoop, calls=%fused_computation.59 | loop fusion | flops 1966080 | bytes 2621440 | tf_op jit(solution)/shard_map/add | solution.py:110
  153.0 0.9 fusion.8
  (224 shorter events, 14.7 us)
Async XLA Ops:
  0.6 10.3 %copy-start = (f32[1,3,16,16,128]{4,3,2,1,0:T(8,128)S(1)}, f32[1,3,16,16,128]{4,3,2,1,0:T(8,128)}, u32[]{:S(2)}) copy-start(f32[1,3,16,16,128]{4,3,2,1,0:T(8,128)} %param.10) | copy-start | bytes 1179652
  0.6 10.3 %copy-start.1 = (f32[1,3,16,16,128]{4,3,2,1,0:T(8,128)S(1)}, f32[1,3,16,16,128]{4,3,2,1,0:T(8,128)}, u32[]{:S(2)}) copy-start(f32[1,3,16,16,128]{4,3,2,1,0:T(8,128)} %param.8) | copy-start | bytes 1179652
  2.6 11.9 %collective-permute-start = (f32[4,16,1,128]{3,2,1,0:T(1,128)S(1)}, f32[4,16,1,128]{3,2,1,0:T(1,128)S(1)}, u32[]{:S(2)}, u32[]{:S(2)}) collective-permute-start(f32[4,16,1,128]{3,2,1,0:T(1,128)S(1)} %pad_maximum_fusion), channel_id=1, source_target_pairs={{1,0},{2,1},{3,2},{4,3},{5,4},{6,5},{7,6},{8,7},{9,8},{10,9},{11,1... | collective-permute-start | bytes 98312 | tf_op jit(solution)/shard_map/ppermute | solution.py:18
  8.1 7.4 %collective-permute-start.1 = (f32[4,1,16,128]{3,2,1,0:T(8,128)S(1)}, f32[4,1,16,128]{3,2,1,0:T(8,128)S(1)}, u32[]{:S(2)}, u32[]{:S(2)}) collective-permute-start(f32[4,1,16,128]{3,2,1,0:T(8,128)S(1)} %pad_maximum_fusion.1), channel_id=1, source_target_pairs={{8,0},{9,1},{10,2},{11,3},{12,4},{13,5},{14,6},{15,7},{16,8},{17,9... | collective-permute-start | bytes 98312 | tf_op jit(solution)/shard_map/ppermute | solution.py:18
  11.1 0.9 copy-start.12
  11.1 0.9 copy-start.14
  12.0 0.9 copy-start.13
  15.9 0.9 copy-start.11
  16.8 1.0 copy-start.2
  16.8 1.1 copy-start.3
  18.3 8.0 %collective-permute-start.2 = (f32[4,16,1,128]{3,2,1,0:T(1,128)S(1)}, f32[4,16,1,128]{3,2,1,0:T(1,128)S(1)}, u32[]{:S(2)}, u32[]{:S(2)}) collective-permute-start(f32[4,16,1,128]{3,2,1,0:T(1,128)S(1)} %pad_maximum_fusion.2), channel_id=1, source_target_pairs={{0,1},{1,2},{2,3},{3,4},{4,5},{5,6},{6,7},{7,8},{8,9},{9,10},{10,1... | collective-permute-start | bytes 98312 | tf_op jit(solution)/shard_map/ppermute | solution.py:18
  20.2 6.2 %collective-permute-start.3 = (f32[4,1,16,128]{3,2,1,0:T(8,128)S(1)}, f32[4,1,16,128]{3,2,1,0:T(8,128)S(1)}, u32[]{:S(2)}, u32[]{:S(2)}) collective-permute-start(f32[4,1,16,128]{3,2,1,0:T(8,128)S(1)} %pad_maximum_fusion.3), channel_id=1, source_target_pairs={{0,8},{1,9},{2,10},{3,11},{4,12},{5,13},{6,14},{7,15},{8,16},{9,17... | collective-permute-start | bytes 98312 | tf_op jit(solution)/shard_map/ppermute | solution.py:18
  26.5 0.6 copy-start.7
  26.5 0.7 copy-start.5
  27.5 7.7 %collective-permute-start.4 = (f32[4,16,1,128]{3,1,2,0:T(8,128)S(1)}, f32[4,16,1,128]{3,1,2,0:T(8,128)S(1)}, u32[]{:S(2)}, u32[]{:S(2)}) collective-permute-start(f32[4,16,1,128]{3,1,2,0:T(8,128)S(1)} %pad_maximum_fusion.4), channel_id=1, source_target_pairs={{1,0},{2,1},{3,2},{4,3},{5,4},{6,5},{7,6},{8,7},{9,8},{10,9},{11,1... | collective-permute-start | bytes 98312 | tf_op jit(solution)/shard_map/ppermute | solution.py:18
  33.3 7.4 %collective-permute-start.5 = (f32[4,1,16,128]{3,2,1,0:T(8,128)S(1)}, f32[4,1,16,128]{3,2,1,0:T(8,128)S(1)}, u32[]{:S(2)}, u32[]{:S(2)}) collective-permute-start(f32[4,1,16,128]{3,2,1,0:T(8,128)S(1)} %pad_maximum_fusion.5), channel_id=1, source_target_pairs={{8,0},{9,1},{10,2},{11,3},{12,4},{13,5},{14,6},{15,7},{16,8},{17,9... | collective-permute-start | bytes 98312 | tf_op jit(solution)/shard_map/ppermute | solution.py:18
  41.4 8.0 %collective-permute-start.6 = (f32[4,16,1,128]{3,1,2,0:T(8,128)S(1)}, f32[4,16,1,128]{3,1,2,0:T(8,128)S(1)}, u32[]{:S(2)}, u32[]{:S(2)}) collective-permute-start(f32[4,16,1,128]{3,1,2,0:T(8,128)S(1)} %pad_maximum_fusion.6), channel_id=1, source_target_pairs={{0,1},{1,2},{2,3},{3,4},{4,5},{5,6},{6,7},{7,8},{8,9},{9,10},{10,1... | collective-permute-start | bytes 98312 | tf_op jit(solution)/shard_map/ppermute | solution.py:18
  43.4 6.2 %collective-permute-start.7 = (f32[4,1,16,128]{3,2,1,0:T(8,128)S(1)}, f32[4,1,16,128]{3,2,1,0:T(8,128)S(1)}, u32[]{:S(2)}, u32[]{:S(2)}) collective-permute-start(f32[4,1,16,128]{3,2,1,0:T(8,128)S(1)} %pad_maximum_fusion.7), channel_id=1, source_target_pairs={{0,8},{1,9},{2,10},{3,11},{4,12},{5,13},{6,14},{7,15},{8,16},{9,17... | collective-permute-start | bytes 98312 | tf_op jit(solution)/shard_map/ppermute | solution.py:18
  49.6 0.7 copy-start.10
  49.7 0.7 copy-start.8
  49.9 0.6 copy-start.4
  50.9 7.0 %collective-permute-start.8 = (f32[4,16,1,128]{3,2,1,0:T(1,128)S(1)}, f32[4,16,1,128]{3,2,1,0:T(1,128)S(1)}, u32[]{:S(2)}, u32[]{:S(2)}) collective-permute-start(f32[4,16,1,128]{3,2,1,0:T(1,128)S(1)} %pad_maximum_fusion.8), channel_id=1, source_target_pairs={{1,0},{2,1},{3,2},{4,3},{5,4},{6,5},{7,6},{8,7},{9,8},{10,9},{11,1... | collective-permute-start | bytes 98312 | tf_op jit(solution)/shard_map/ppermute | solution.py:18
  56.0 7.0 %collective-permute-start.9 = (f32[4,1,16,128]{3,2,1,0:T(8,128)S(1)}, f32[4,1,16,128]{3,2,1,0:T(8,128)S(1)}, u32[]{:S(2)}, u32[]{:S(2)}) collective-permute-start(f32[4,1,16,128]{3,2,1,0:T(8,128)S(1)} %pad_maximum_fusion.9), channel_id=1, source_target_pairs={{8,0},{9,1},{10,2},{11,3},{12,4},{13,5},{14,6},{15,7},{16,8},{17,9... | collective-permute-start | bytes 98312 | tf_op jit(solution)/shard_map/ppermute | solution.py:18
  63.9 8.0 %collective-permute-start.10 = (f32[4,16,1,128]{3,2,1,0:T(1,128)S(1)}, f32[4,16,1,128]{3,2,1,0:T(1,128)S(1)}, u32[]{:S(2)}, u32[]{:S(2)}) collective-permute-start(f32[4,16,1,128]{3,2,1,0:T(1,128)S(1)} %pad_maximum_fusion.10), channel_id=1, source_target_pairs={{0,1},{1,2},{2,3},{3,4},{4,5},{5,6},{6,7},{7,8},{8,9},{9,10},{10,1... | collective-permute-start | bytes 98312 | tf_op jit(solution)/shard_map/ppermute | solution.py:18
  65.8 6.2 %collective-permute-start.11 = (f32[4,1,16,128]{3,2,1,0:T(8,128)S(1)}, f32[4,1,16,128]{3,2,1,0:T(8,128)S(1)}, u32[]{:S(2)}, u32[]{:S(2)}) collective-permute-start(f32[4,1,16,128]{3,2,1,0:T(8,128)S(1)} %pad_maximum_fusion.11), channel_id=1, source_target_pairs={{0,8},{1,9},{2,10},{3,11},{4,12},{5,13},{6,14},{7,15},{8,16},{9,17... | collective-permute-start | bytes 98312 | tf_op jit(solution)/shard_map/ppermute | solution.py:18
  72.8 7.0 %collective-permute-start.12 = (f32[4,16,1,128]{3,2,1,0:T(1,128)S(1)}, f32[4,16,1,128]{3,2,1,0:T(1,128)S(1)}, u32[]{:S(2)}, u32[]{:S(2)}) collective-permute-start(f32[4,16,1,128]{3,2,1,0:T(1,128)S(1)} %pad_maximum_fusion.12), channel_id=1, source_target_pairs={{1,0},{2,1},{3,2},{4,3},{5,4},{6,5},{7,6},{8,7},{9,8},{10,9},{11,1... | collective-permute-start | bytes 98312 | tf_op jit(solution)/shard_map/ppermute | solution.py:18
  77.9 7.0 %collective-permute-start.13 = (f32[4,1,16,128]{3,2,1,0:T(8,128)S(1)}, f32[4,1,16,128]{3,2,1,0:T(8,128)S(1)}, u32[]{:S(2)}, u32[]{:S(2)}) collective-permute-start(f32[4,1,16,128]{3,2,1,0:T(8,128)S(1)} %pad_maximum_fusion.13), channel_id=1, source_target_pairs={{8,0},{9,1},{10,2},{11,3},{12,4},{13,5},{14,6},{15,7},{16,8},{17,9... | collective-permute-start | bytes 98312 | tf_op jit(solution)/shard_map/ppermute | solution.py:18
  85.7 7.9 %collective-permute-start.14 = (f32[4,16,1,128]{3,2,1,0:T(1,128)S(1)}, f32[4,16,1,128]{3,2,1,0:T(1,128)S(1)}, u32[]{:S(2)}, u32[]{:S(2)}) collective-permute-start(f32[4,16,1,128]{3,2,1,0:T(1,128)S(1)} %pad_maximum_fusion.14), channel_id=1, source_target_pairs={{0,1},{1,2},{2,3},{3,4},{4,5},{5,6},{6,7},{7,8},{8,9},{9,10},{10,1... | collective-permute-start | bytes 98312 | tf_op jit(solution)/shard_map/ppermute | solution.py:18
  89.5 5.8 %collective-permute-start.15 = (f32[4,1,16,128]{3,2,1,0:T(8,128)S(1)}, f32[4,1,16,128]{3,2,1,0:T(8,128)S(1)}, u32[]{:S(2)}, u32[]{:S(2)}) collective-permute-start(f32[4,1,16,128]{3,2,1,0:T(8,128)S(1)} %pad_maximum_fusion.15), channel_id=1, source_target_pairs={{0,8},{1,9},{2,10},{3,11},{4,12},{5,13},{6,14},{7,15},{8,16},{9,17... | collective-permute-start | bytes 98312 | tf_op jit(solution)/shard_map/ppermute | solution.py:18
  151.0 2.0 %copy-start.6 = (f32[1,16,16,128]{3,2,1,0:T(8,128)S(1)}, f32[1,16,16,128]{3,2,1,0:T(8,128)}, u32[]{:S(2)}) copy-start(f32[1,16,16,128]{3,2,1,0:T(8,128)} %copy-done.5) | copy-start | bytes 393220
  151.0 2.0 %copy-start.9 = (f32[1,16,16,128]{3,2,1,0:T(8,128)S(1)}, f32[1,16,16,128]{3,2,1,0:T(8,128)}, u32[]{:S(2)}) copy-start(f32[1,16,16,128]{3,2,1,0:T(8,128)} %copy-done.8) | copy-start | bytes 393220
where the time goes:
time: 155 us; the launch traced here: 154 us
  blocking collectives  54.2 us (35%)
  starting transfers between devices  50.9 us (33%)
  waiting for transfers between devices  24.2 us (16%)
  local copies, waits for them, and re-layouts  11.8 us (8%)
  other arithmetic  9.93 us (6%)
  between operations  2.75 us (2%)
    psum x1, blocking collectives, per_device(): gradient = lax.psum(gradient, 'wave')  54.2 us
    ppermute x16, starting transfers between devices, from_behind(): lax.ppermute(value, axis, [(source, source + steps) for source in range(i...  50.9 us
    ppermute x16, waiting for transfers between devices, from_behind(): lax.ppermute(value, axis, [(source, source + steps) for source in range(i...  24.2 us
    unnamed x30, local copies, waits for them, and re-layouts  4.3 us
  transfers between devices with their start and end apart: 16, of which 11 were waited for; matrix products, arithmetic and copies ran while one was open for 4% of the time, Pallas kernels for 0%

commit v1 on v0

v1 whole, which is shorter than its diff:
```python
import functools

import jax
import jax.numpy as jnp
from jax import lax
from jax.experimental import pallas as pl
from jax.experimental.pallas import tpu as pltpu
from jax.sharding import PartitionSpec as P

STEPS = 4
DZ = 16
TILE_COLS = 8
HALO = STEPS
KINDS = 14

dt_step = 0.5
depth_scale = 4.0

VMEM = pl.BlockSpec(memory_space=pltpu.VMEM)
SMEM = pl.BlockSpec(memory_space=pltpu.SMEM)
ANY = pl.BlockSpec(memory_space=pl.ANY)


def swap_pairs(count, cols, along_x, odd):
    rows = count // cols
    pairs = []
    for row in range(rows):
        for col in range(cols):
            place, size = (row, rows) if along_x else (col, cols)
            other = place + 1 if place % 2 == odd else place - 1
            if 0 <= other < size:
                target = other * cols + col if along_x else row * cols + other
                pairs.append((row * cols + col, target))
    return pairs


def low_half(shape):
    return lax.broadcasted_iota(jnp.int32, shape, len(shape) - 2) < 4


def staggered(block, by):
    row = lax.broadcasted_iota(jnp.int32, block.shape, 0)
    for bit in range(3):
        moved = pltpu.roll(block, (by << bit) % 128, 1)
        block = jnp.where((row >> bit) % 2 == 1, moved, block)
    return block


def pack_kernel(meta, ef, hf, ea, ha, kind, depth, xa1, xb1, xa2, xb2, yb, ya):
    row_even = lax.rem(meta[1], 2) == 0
    col_even = lax.rem(meta[2], 2) == 0
    cells = ef.shape[1]
    at_a = jnp.where(row_even, cells - HALO, 0)
    at_b = jnp.where(row_even, 0, cells - HALO)
    fields = (ef, hf, ea, ha)
    low = low_half((HALO, 8, 128))

    def source(k, rows, ys):
        if k < 12:
            return fields[k // 3][k % 3, rows, ys, :]
        return (kind, depth)[k - 12][rows, ys, :].astype(jnp.float32)

    for k in range(KINDS):
        for at, first, second in ((at_a, xa1, xa2), (at_b, xb1, xb2)):
            rows = pl.ds(at, HALO)
            t0 = source(k, rows, slice(0, 8))
            t1 = source(k, rows, slice(8, 16))
            first[k] = jnp.where(low, t0, t1)
            second[k] = jnp.where(low, t1, t0)

    every = slice(None)

    @pl.when(col_even)
    def _():
        for k in range(KINDS):
            yb[k] = source(k, every, slice(0, 4))
            ya[k] = source(k, every, slice(12, 16))

    @pl.when(jnp.logical_not(col_even))
    def _():
        for k in range(KINDS):
            yb[k] = source(k, every, slice(12, 16))
            ya[k] = source(k, every, slice(0, 4))


def pack(meta, fields, kind, depth):
    cells = kind.shape[0]
    edge = jax.ShapeDtypeStruct((KINDS, HALO, 8, 128), jnp.float32)
    strip = jax.ShapeDtypeStruct((KINDS, cells, 4, 128), jnp.float32)
    return pl.pallas_call(
        pack_kernel,
        out_shape=(edge, edge, edge, edge, strip, strip),
        in_specs=[SMEM] + [VMEM] * 6,
        out_specs=[VMEM] * 6,
        compiler_params=pltpu.CompilerParams(vmem_limit_bytes=16 * 2**20),
        name="pack",
    )(meta, *fields, kind, depth)


def corner_kernel(meta, ra1, rb1, ya, cb, yac):
    col_even = lax.rem(meta[2], 2) == 0
    cells = ya.shape[1]
    yac[:, 0:cells] = ya[...]

    def put(to_a, to_b):
        for k in range(KINDS):
            yac[k, cells:cells + HALO] = ra1[k, :, to_a, :]
            yac[k, cells + HALO:cells + 2 * HALO] = rb1[k, :, to_a, :]
            cb[k, 0:HALO] = ra1[k, :, to_b, :]
            cb[k, HALO:2 * HALO] = rb1[k, :, to_b, :]

    @pl.when(col_even)
    def _():
        put(slice(4, 8), slice(0, 4))

    @pl.when(jnp.logical_not(col_even))
    def _():
        put(slice(0, 4), slice(4, 8))


def corners(meta, ra1, rb1, ya):
    cells = ya.shape[1]
    return pl.pallas_call(
        corner_kernel,
        out_shape=(
            jax.ShapeDtypeStruct((KINDS, 2 * HALO, 4, 128), jnp.float32),
            jax.ShapeDtypeStruct((KINDS, cells + 2 * HALO, 4, 128), jnp.float32),
        ),
        in_specs=[SMEM] + [VMEM] * 3,
        out_specs=[VMEM] * 2,
        compiler_params=pltpu.CompilerParams(vmem_limit_bytes=16 * 2**20),
        name="corners",
    )(meta, ra1, rb1, ya)


def steps_kernel(cols, rows, meta, table, ef, hf, ea, ha, kind, depth,
                 ra1, rb1, ra2, rb2, rb, rcb, rya,
                 ef_out, hf_out, ea_out, ha_out, send,
                 field, ca, cb, da, db, total, in_sems, out_sems):
    start, row, col = meta[0], meta[1], meta[2]
    row_even = lax.rem(row, 2) == 0
    col_even = lax.rem(col, 2) == 0
    cells = kind.shape[0]
    wide = cells + 2 * HALO
    own = slice(HALO, HALO + cells)

    loads = []
    for n, source in enumerate((ef, hf, ea, ha)):
        loads.append(pltpu.make_async_copy(
            source, field.at[pl.ds(3 * n, 3), pl.ds(HALO, cells), pl.ds(0, cells), :],
            in_sems.at[n]))
        loads[-1].start()

    off_a = jnp.where(row_even, HALO + cells, 0)
    off_b = jnp.where(row_even, 0, HALO + cells)
    low = low_half((HALO, 8, 128))
    for k in range(KINDS):
        for off, first, second in ((off_a, ra1, ra2), (off_b, rb1, rb2)):
            here = pl.ds(off, HALO)
            edge, mid = first[k], second[k]
            field[k, here, 0:8, :] = jnp.where(low, edge, mid)
            field[k, here, 8:16, :] = jnp.where(low, mid, edge)

    def columns(side_a, side_b):
        for k in range(KINDS):
            field[k, own, side_a, :] = rya[k, 0:cells]
            field[k, pl.ds(off_a, HALO), side_a, :] = rya[k, cells:cells + HALO]
            field[k, pl.ds(off_b, HALO), side_a, :] = rya[k, cells + HALO:wide]
            field[k, own, side_b, :] = rb[k]
            field[k, pl.ds(off_a, HALO), side_b, :] = rcb[k, 0:HALO]
            field[k, pl.ds(off_b, HALO), side_b, :] = rcb[k, HALO:2 * HALO]

    @pl.when(col_even)
    def _():
        columns(slice(16, 20), slice(20, 24))

    @pl.when(jnp.logical_not(col_even))
    def _():
        columns(slice(20, 24), slice(16, 20))

    field[12, own, 0:cells, :] = kind[...].astype(jnp.float32)
    field[13, own, 0:cells, :] = depth[...].astype(jnp.float32)

    eps = [table[0, m] for m in range(4)]
    place = lax.broadcasted_iota(jnp.int32, (wide, 128), 0)
    after = jnp.logical_and(place >= 16, place < 20)
    before = place >= 20
    outside_y = jnp.logical_or(jnp.logical_and(after, col == cols - 1),
                               jnp.logical_and(before, col == 0))

    def coefficient(x, _):
        m = field[12, x]
        ramp = field[13, x] / depth_scale
        e = jnp.where(m < 0.5, eps[0],
                      jnp.where(m < 1.5, eps[1], jnp.where(m < 2.5, eps[2], eps[3])))
        sigma = ramp * ramp
        s_e = sigma * dt_step / (2.0 * e)
        s_h = sigma * dt_step / 2.0
        outside_x = jnp.logical_or(jnp.logical_and(x < HALO, row == 0),
                                   jnp.logical_and(x >= HALO + cells, row == rows - 1))
        outside = jnp.logical_or(outside_y, outside_x)
        ca[x] = (1.0 - s_e) / (1.0 + s_e)
        cb[x] = jnp.where(outside, 0.0, dt_step / (e * (1.0 + s_e)))
        da[x] = (1.0 - s_h) / (1.0 + s_h)
        db[x] = jnp.where(outside, 0.0, dt_step / (1.0 + s_h))
        return 0

    lax.fori_loop(0, wide, coefficient, 0)

    for load in loads:
        load.wait()

    lane = lax.broadcasted_iota(jnp.int32, (wide, 128), 1)
    last_z, first_z = lane == 127, lane == 0

    def up_z(v):
        return jnp.where(last_z, 0.0, pltpu.roll(v, 127, 1))

    def down_z(v):
        return jnp.where(first_z, 0.0, pltpu.roll(v, 1, 1))

    def up_y(v):
        return pltpu.roll(v, wide - 1, 0)

    def down_y(v):
        return pltpu.roll(v, 1, 0)

    def h_row(x, _):
        dax, dbx = da[x], db[x]
        for e, h in ((0, 3), (6, 9)):
            ex, ey, ez = field[e, x], field[e + 1, x], field[e + 2, x]
            ey1, ez1 = field[e + 1, x + 1], field[e + 2, x + 1]
            field[h, x] = dax * field[h, x] - dbx * ((up_y(ez) - ez) - (up_z(ey) - ey))
            field[h + 1, x] = dax * field[h + 1, x] - dbx * ((up_z(ex) - ex) - (ez1 - ez))
            field[h + 2, x] = dax * field[h + 2, x] - dbx * ((ey1 - ey) - (up_y(ex) - ex))
        return 0

    def e_row(x, keep):
        cax, cbx = ca[x], cb[x]
        new = []
        for e, h in ((0, 3), (6, 9)):
            hx, hy, hz = field[h, x], field[h + 1, x], field[h + 2, x]
            hy1, hz1 = field[h + 1, x - 1], field[h + 2, x - 1]
            new.append((
                cax * field[e, x] + cbx * ((hz - down_y(hz)) - (hy - down_z(hy))),
                cax * field[e + 1, x] + cbx * ((hx - down_z(hx)) - (hz - hz1)),
                cax * field[e + 2, x] + cbx * ((hy - hy1) - (hx - down_y(hx))),
            ))
            for n in range(3):
                field[e + n, x] = new[-1][n]
        if keep is not None:
            term = sum(new[0][n][0:16] * new[1][n][0:16] for n in range(3))
            if keep == 0:
                total[x - HALO] = term
            else:
                total[x - HALO] = total[x - HALO] + term
        return 0

    stores = []
    for step in range(STEPS):
        lax.fori_loop(step, wide - 1 - step, h_row, 0)
        if step == STEPS - 1:
            stores += [(3, hf_out), (9, ha_out)]
            for n, (k, out) in enumerate(stores):
                pltpu.make_async_copy(
                    field.at[pl.ds(k, 3), pl.ds(HALO, cells), pl.ds(0, cells), :], out,
                    out_sems.at[n]).start()
        if step < STEPS - 1:
            lax.fori_loop(step + 1, HALO, lambda x, c: e_row(x, None), 0)
            lax.fori_loop(HALO + cells, wide - 1 - step, lambda x, c: e_row(x, None), 0)
        lax.fori_loop(HALO, HALO + cells, lambda x, c: e_row(x, step), 0)

    stores += [(0, ef_out), (6, ea_out)]
    for n, (k, out) in enumerate(stores):
        if n >= 2:
            pltpu.make_async_copy(
                field.at[pl.ds(k, 3), pl.ds(HALO, cells), pl.ds(0, cells), :], out,
                out_sems.at[n]).start()

    sub = lax.broadcasted_iota(jnp.int32, (8, 128), 0)
    mine = lax.broadcasted_iota(jnp.int32, (8, 128), 1) // DZ == sub
    for tile in range(cells * 2 // 8):
        block = jnp.zeros((8, 128), jnp.float32)
        for n in range(8):
            x, half = (tile * 8 + n) // 2, (tile * 8 + n) % 2
            moved = pltpu.roll(total[x, 8 * half:8 * half + 8, :], 128 - start, 1)
            moved = staggered(moved, DZ)
            line = jnp.sum(jnp.where(mine, moved, 0.0), axis=0, keepdims=True)
            block = jnp.where(sub == n, line, block)
        for peer in range(send.shape[0]):
            send[peer, tile * 8:tile * 8 + 8, :] = block

    for n, (k, out) in enumerate(stores):
        pltpu.make_async_copy(
            field.at[pl.ds(k, 3), pl.ds(HALO, cells), pl.ds(0, cells), :], out,
            out_sems.at[n]).wait()


def all_steps(cols, rows, waves, meta, table, fields, kind, depth, halos):
    cells = kind.shape[0]
    wide = cells + 2 * HALO
    out = jax.ShapeDtypeStruct(fields[0].shape, jnp.float32)
    plane = pltpu.VMEM((wide, wide, 128), jnp.float32)
    return pl.pallas_call(
        functools.partial(steps_kernel, cols, rows),
        out_shape=(out, out, out, out,
                   jax.ShapeDtypeStruct((waves, cells * 2, 128), jnp.float32)),
        in_specs=[SMEM, SMEM] + [ANY] * 4 + [VMEM] * 9,
        out_specs=[ANY] * 4 + [VMEM],
        scratch_shapes=[
            pltpu.VMEM((KINDS, wide, wide, 128), jnp.float32),
            plane, plane, plane, plane,
            pltpu.VMEM((cells, cells, 128), jnp.float32),
            pltpu.SemaphoreType.DMA((4,)),
            pltpu.SemaphoreType.DMA((4,)),
        ],
        compiler_params=pltpu.CompilerParams(vmem_limit_bytes=24 * 2**20),
        name="steps",
    )(meta, table, *fields, kind, depth, *halos)


def gradient_kernel(parts, out):
    waves, lines, _ = parts.shape
    whole = parts[0]
    for wave in range(1, waves):
        whole = whole + parts[wave]
    for n in range(lines):
        spread = jnp.broadcast_to(whole[n:n + 1, :], (8, 128))
        moved = staggered(spread, 128 - DZ)
        out[n // 2, 8 * (n % 2):8 * (n % 2) + 8, :] = moved[:, 0:DZ]


def gradient_of(parts):
    cells = parts.shape[1] // 2
    return pl.pallas_call(
        gradient_kernel,
        out_shape=jax.ShapeDtypeStruct((cells, cells, DZ), jnp.float32),
        in_specs=[VMEM],
        out_specs=VMEM,
        compiler_params=pltpu.CompilerParams(vmem_limit_bytes=8 * 2**20),
        name="gradient",
    )(parts)


def per_device(
    e_forward, h_forward, e_adjoint, h_adjoint, eps_table, material, pml_depth, design_start
):
    cols = TILE_COLS
    count = lax.axis_size("tile")
    rows = count // cols
    me = lax.axis_index("tile")
    meta = jnp.stack([design_start[0], me // cols, me % cols]).astype(jnp.int32)
    fields = (e_forward[0], h_forward[0], e_adjoint[0], h_adjoint[0])

    def swap(value, along_x, odd):
        return lax.ppermute(value, "tile", swap_pairs(count, cols, along_x, odd))

    xa1, xb1, xa2, xb2, yb, ya = pack(meta, fields, material, pml_depth)
    ra1 = swap(xa1, True, 0)
    rb1 = swap(xb1, True, 1)
    rb = swap(yb, False, 1)
    ra2 = swap(xa2, True, 0)
    rb2 = swap(xb2, True, 1)
    cb, yac = corners(meta, ra1, rb1, ya)
    rcb = swap(cb, False, 1)
    rya = swap(yac, False, 0)
    *outs, send = all_steps(cols, rows, lax.axis_size("wave"), meta, eps_table, fields,
                            material, pml_depth, (ra1, rb1, ra2, rb2, rb, rcb, rya))
    parts = lax.all_to_all(send, "wave", 0, 0)
    gradient = gradient_of(parts)
    return tuple(out[None] for out in outs) + (gradient,)


def solution(mesh):
    return jax.shard_map(
        per_device,
        mesh=mesh,
        in_specs=(
            P("wave", None, "tile", None, None),
            P("wave", None, "tile", None, None),
            P("wave", None, "tile", None, None),
            P("wave", None, "tile", None, None),
            P("wave", None),
            P("tile", None, None),
            P("tile", None, None),
            P("tile"),
        ),
        out_specs=(
            P("wave", None, "tile", None, None),
            P("wave", None, "tile", None, None),
            P("wave", None, "tile", None, None),
            P("wave", None, "tile", None, None),
            P("tile", None, None),
        ),
        check_vma=False,
    )
```

time: 155 us -> 81.3 us (0.52)
  the two profiles are of different devices: /device:TPU:192 before, /device:TPU:72 now
where the time goes in v1:
time: 81.3 us; the launch traced here: 80.8 us
  starting transfers between devices  24.4 us (30%)
  blocking collectives  20.5 us (25%)
  Pallas kernels  18.5 us (23%)
  waiting for transfers between devices  10.1 us (12%)
  local copies, waits for them, and re-layouts  5.82 us (7%)
  between operations  1.46 us (2%)
    ppermute x7, starting transfers between devices, swap(): return lax.ppermute(value, 'tile', swap_pairs(count, cols, along_x, odd))  24.4 us
    all_to_all x1, blocking collectives, per_device(): parts = lax.all_to_all(send, 'wave', 0, 0)  20.5 us
    pallas_call x1, Pallas kernels, all_steps(): pl.pallas_call(functools.partial(steps_kernel, cols, rows), out_shape=(ou...  16.2 us
    ppermute x7, waiting for transfers between devices, swap(): return lax.ppermute(value, 'tile', swap_pairs(count, cols, along_x, odd))  10.1 us
    unnamed x26, local copies, waits for them, and re-layouts  5.82 us
  transfers between devices with their start and end apart: 7, of which 4 were waited for; matrix products, arithmetic and copies ran while one was open for 0% of the time, Pallas kernels for 0%

profile of v1, /device:TPU:72, one launch (start us, length us, event | category | flops | bytes accessed | tf_op | source)
XLA Modules:
  0.0 80.8 jit_solution(14887382959012670576)
XLA Ops:
  1.3 0.1 pad_add_fusion.meta
  1.4 1.0 %copy-done = f32[1,3,16,16,128]{4,3,2,1,0:T(8,128)S(1)} copy-done((f32[1,3,16,16,128]{4,3,2,1,0:T(8,128)S(1)}, f32[1,3,16,16,128]{4,3,2,1,0:T(8,128)}, u32[]{:S(2)}) %copy-start) | copy-done | bytes 393240
  2.4 1.0 %copy-done.2 = f32[1,3,16,16,128]{4,3,2,1,0:T(8,128)S(1)} copy-done((f32[1,3,16,16,128]{4,3,2,1,0:T(8,128)S(1)}, f32[1,3,16,16,128]{4,3,2,1,0:T(8,128)}, u32[]{:S(2)}) %copy-start.2) | copy-done | bytes 393240
  3.4 1.0 %copy-done.4 = f32[1,3,16,16,128]{4,3,2,1,0:T(8,128)S(1)} copy-done((f32[1,3,16,16,128]{4,3,2,1,0:T(8,128)S(1)}, f32[1,3,16,16,128]{4,3,2,1,0:T(8,128)}, u32[]{:S(2)}) %copy-start.4) | copy-done | bytes 393240
  4.4 1.0 %copy-done.6 = f32[1,3,16,16,128]{4,3,2,1,0:T(8,128)S(1)} copy-done((f32[1,3,16,16,128]{4,3,2,1,0:T(8,128)S(1)}, f32[1,3,16,16,128]{4,3,2,1,0:T(8,128)}, u32[]{:S(2)}) %copy-start.6) | copy-done | bytes 393240
  5.4 0.9 %copy-done.8 = s32[16,16,128]{2,1,0:T(8,128)S(1)} copy-done((s32[16,16,128]{2,1,0:T(8,128)S(1)}, s32[16,16,128]{2,1,0:T(8,128)}, u32[]{:S(2)}) %copy-start.8) | copy-done | bytes 131096
  6.3 0.9 %copy-done.10 = s32[16,16,128]{2,1,0:T(8,128)S(1)} copy-done((s32[16,16,128]{2,1,0:T(8,128)S(1)}, s32[16,16,128]{2,1,0:T(8,128)}, u32[]{:S(2)}) %copy-start.10) | copy-done | bytes 131096
  7.2 0.8 pack.1
  8.0 1.9 %collective-permute-start = (f32[14,4,8,128]{3,2,1,0:T(8,128)S(1)}, f32[14,4,8,128]{3,2,1,0:T(8,128)S(1)}, u32[]{:S(2)}, u32[]{:S(2)}) collective-permute-start(f32[14,4,8,128]{3,2,1,0:T(8,128)S(1)} %get-tuple-element.18), channel_id=1, source_target_pairs={{0,8},{1,9},{2,10},{3,11},{4,12},{5,13},{6,14},{7,15},{8,0},{9,1},... | collective-permute-start | bytes 688136 | tf_op jit(solution)/shard_map/ppermute | solution.py:356
  9.9 6.6 %collective-permute-start.1 = (f32[14,4,8,128]{3,2,1,0:T(8,128)S(1)}, f32[14,4,8,128]{3,2,1,0:T(8,128)S(1)}, u32[]{:S(2)}, u32[]{:S(2)}) collective-permute-start(f32[14,4,8,128]{3,2,1,0:T(8,128)S(1)} %get-tuple-element.19), channel_id=1, source_target_pairs={{8,16},{9,17},{10,18},{11,19},{12,20},{13,21},{14,22},{15,23},{16,... | collective-permute-start | bytes 688136 | tf_op jit(solution)/shard_map/ppermute | solution.py:356
  16.5 0.7 collective-permute-done.ra1
  17.2 4.6 %collective-permute-done.1.rb1 = f32[14,4,8,128]{3,2,1,0:T(8,128)S(1)} collective-permute-done((f32[14,4,8,128]{3,2,1,0:T(8,128)S(1)}, f32[14,4,8,128]{3,2,1,0:T(8,128)S(1)}, u32[]{:S(2)}, u32[]{:S(2)}) %collective-permute-start.1) | collective-permute-done | bytes 229408 | tf_op jit(solution)/shard_map/ppermute | solution.py:356
  21.8 0.7 corners.1
  22.5 1.9 %collective-permute-start.6 = (f32[14,24,4,128]{3,2,1,0:T(4,128)S(1)}, f32[14,24,4,128]{3,2,1,0:T(4,128)S(1)}, u32[]{:S(2)}, u32[]{:S(2)}) collective-permute-start(f32[14,24,4,128]{3,2,1,0:T(4,128)S(1)} %get-tuple-element.25), channel_id=1, source_target_pairs={{0,1},{1,0},{2,3},{3,2},{4,5},{5,4},{6,7},{7,6},{8,9},{9,8},{10,11... | collective-permute-start | bytes 2064392 | tf_op jit(solution)/shard_map/ppermute | solution.py:356
  24.4 3.4 %collective-permute-start.4 = (f32[14,16,4,128]{3,2,1,0:T(4,128)S(1)}, f32[14,16,4,128]{3,2,1,0:T(4,128)S(1)}, u32[]{:S(2)}, u32[]{:S(2)}) collective-permute-start(f32[14,16,4,128]{3,2,1,0:T(4,128)S(1)} %get-tuple-element.22), channel_id=1, source_target_pairs={{1,2},{2,1},{3,4},{4,3},{5,6},{6,5},{9,10},{10,9},{11,12},{12,11},... | collective-permute-start | bytes 1376264 | tf_op jit(solution)/shard_map/ppermute | solution.py:356
  27.9 1.9 %collective-permute-start.2 = (f32[14,4,8,128]{3,2,1,0:T(8,128)S(1)}, f32[14,4,8,128]{3,2,1,0:T(8,128)S(1)}, u32[]{:S(2)}, u32[]{:S(2)}) collective-permute-start(f32[14,4,8,128]{3,2,1,0:T(8,128)S(1)} %get-tuple-element.20), channel_id=1, source_target_pairs={{0,8},{1,9},{2,10},{3,11},{4,12},{5,13},{6,14},{7,15},{8,0},{9,1},... | collective-permute-start | bytes 688136 | tf_op jit(solution)/shard_map/ppermute | solution.py:356
  29.8 0.0 copy-start.12
  29.8 6.0 %collective-permute-start.3 = (f32[14,4,8,128]{3,2,1,0:T(8,128)S(1)}, f32[14,4,8,128]{3,2,1,0:T(8,128)S(1)}, u32[]{:S(2)}, u32[]{:S(2)}) collective-permute-start(f32[14,4,8,128]{3,2,1,0:T(8,128)S(1)} %get-tuple-element.21), channel_id=1, source_target_pairs={{8,16},{9,17},{10,18},{11,19},{12,20},{13,21},{14,22},{15,23},{16,... | collective-permute-start | bytes 688136 | tf_op jit(solution)/shard_map/ppermute | solution.py:356
  35.8 2.5 %collective-permute-start.5 = (f32[14,8,4,128]{3,2,1,0:T(4,128)S(1)}, f32[14,8,4,128]{3,2,1,0:T(4,128)S(1)}, u32[]{:S(2)}, u32[]{:S(2)}) collective-permute-start(f32[14,8,4,128]{3,2,1,0:T(4,128)S(1)} %get-tuple-element.24), channel_id=1, source_target_pairs={{1,2},{2,1},{3,4},{4,3},{5,6},{6,5},{9,10},{10,9},{11,12},{12,11},... | collective-permute-start | bytes 688136 | tf_op jit(solution)/shard_map/ppermute | solution.py:356
  38.4 0.0 collective-permute-done.2.ra2
  38.4 3.7 %collective-permute-done.3.rb2 = f32[14,4,8,128]{3,2,1,0:T(8,128)S(1)} collective-permute-done((f32[14,4,8,128]{3,2,1,0:T(8,128)S(1)}, f32[14,4,8,128]{3,2,1,0:T(8,128)S(1)}, u32[]{:S(2)}, u32[]{:S(2)}) %collective-permute-start.3) | collective-permute-done | bytes 229408 | tf_op jit(solution)/shard_map/ppermute | solution.py:356
  42.1 1.1 %collective-permute-done.5.rcb = f32[14,8,4,128]{3,2,1,0:T(4,128)S(1)} collective-permute-done((f32[14,8,4,128]{3,2,1,0:T(4,128)S(1)}, f32[14,8,4,128]{3,2,1,0:T(4,128)S(1)}, u32[]{:S(2)}, u32[]{:S(2)}) %collective-permute-start.5) | collective-permute-done | bytes 229408 | tf_op jit(solution)/shard_map/ppermute | solution.py:356
  43.1 0.0 collective-permute-done.4.rb
  43.1 0.0 collective-permute-done.6.rya
  43.1 0.0 copy-done.5
  43.2 0.0 copy-done.7
  43.2 0.0 copy-done.11
  43.2 0.0 copy-done.1
  43.2 0.0 copy-done.3
  43.2 16.2 %steps.1 = (f32[3,16,16,128]{3,2,1,0:T(8,128)}, f32[3,16,16,128]{3,2,1,0:T(8,128)}, f32[3,16,16,128]{3,2,1,0:T(8,128)}, f32[3,16,16,128]{3,2,1,0:T(8,128)}, f32[8,32,128]{2,1,0:T(8,128)S(1)}) custom-call(s32[3]{0:T(128)S(1)} %pad_add_fusion.meta, f32[1,4]{1,0:T(1,128)S(1)} %copy-done.12, f32[3,16,16,128]{3,2,1,0:T(8,128)S(1)} %bitcast.11, ...), custom_call_target="tpu_custom_call" | custom-call | tf_op jit(solution)/shard_map/steps/pallas_call | solution.py:304
  59.4 20.5 %all_to_all.5.parts = f32[8,32,128]{2,1,0:T(8,128)S(1)} all-to-all(f32[8,32,128]{2,1,0:T(8,128)S(1)} %get-tuple-element.30), channel_id=1, replica_groups=mesh['wave'=8,'tile'=64] {'wave'}, dimensions={0} | all-to-all | bytes 262144 | tf_op jit(solution)/shard_map/all_to_all | solution.py:369
  79.9 0.9 %gradient.1 = f32[16,16,16]{2,1,0:T(8,128)} custom-call(f32[8,32,128]{2,1,0:T(8,128)S(1)} %all_to_all.5.parts), custom_call_target="tpu_custom_call" | custom-call | tf_op jit(solution)/shard_map/gradient/pallas_call | solution.py:335
  (14 shorter events, 0.0 us)
Async XLA Ops:
  1.4 1.0 %copy-start = (f32[1,3,16,16,128]{4,3,2,1,0:T(8,128)S(1)}, f32[1,3,16,16,128]{4,3,2,1,0:T(8,128)}, u32[]{:S(2)}) copy-start(f32[1,3,16,16,128]{4,3,2,1,0:T(8,128)} %param.8) | copy-start | bytes 1179652
  2.4 1.0 %copy-start.2 = (f32[1,3,16,16,128]{4,3,2,1,0:T(8,128)S(1)}, f32[1,3,16,16,128]{4,3,2,1,0:T(8,128)}, u32[]{:S(2)}) copy-start(f32[1,3,16,16,128]{4,3,2,1,0:T(8,128)} %param.9) | copy-start | bytes 1179652
  3.4 1.0 %copy-start.4 = (f32[1,3,16,16,128]{4,3,2,1,0:T(8,128)S(1)}, f32[1,3,16,16,128]{4,3,2,1,0:T(8,128)}, u32[]{:S(2)}) copy-start(f32[1,3,16,16,128]{4,3,2,1,0:T(8,128)} %param.10) | copy-start | bytes 1179652
  4.4 1.0 %copy-start.6 = (f32[1,3,16,16,128]{4,3,2,1,0:T(8,128)S(1)}, f32[1,3,16,16,128]{4,3,2,1,0:T(8,128)}, u32[]{:S(2)}) copy-start(f32[1,3,16,16,128]{4,3,2,1,0:T(8,128)} %param.11) | copy-start | bytes 1179652
  5.4 0.9 %copy-start.8 = (s32[16,16,128]{2,1,0:T(8,128)S(1)}, s32[16,16,128]{2,1,0:T(8,128)}, u32[]{:S(2)}) copy-start(s32[16,16,128]{2,1,0:T(8,128)} %kind.3) | copy-start | bytes 393220
  6.3 0.9 %copy-start.10 = (s32[16,16,128]{2,1,0:T(8,128)S(1)}, s32[16,16,128]{2,1,0:T(8,128)}, u32[]{:S(2)}) copy-start(s32[16,16,128]{2,1,0:T(8,128)} %depth.3) | copy-start | bytes 393220
  7.2 36.0 %copy-start.5 = (f32[1,3,16,16,128]{4,3,2,1,0:T(8,128)S(1)}, f32[1,3,16,16,128]{4,3,2,1,0:T(8,128)}, u32[]{:S(2)}) copy-start(f32[1,3,16,16,128]{4,3,2,1,0:T(8,128)} %param.10) | copy-start | bytes 1179652
  7.2 36.0 %copy-start.7 = (f32[1,3,16,16,128]{4,3,2,1,0:T(8,128)S(1)}, f32[1,3,16,16,128]{4,3,2,1,0:T(8,128)}, u32[]{:S(2)}) copy-start(f32[1,3,16,16,128]{4,3,2,1,0:T(8,128)} %param.11) | copy-start | bytes 1179652
  7.2 36.0 %copy-start.11 = (s32[16,16,128]{2,1,0:T(8,128)S(1)}, s32[16,16,128]{2,1,0:T(8,128)}, u32[]{:S(2)}) copy-start(s32[16,16,128]{2,1,0:T(8,128)} %depth.3) | copy-start | bytes 393220
  8.0 9.2 %collective-permute-start = (f32[14,4,8,128]{3,2,1,0:T(8,128)S(1)}, f32[14,4,8,128]{3,2,1,0:T(8,128)S(1)}, u32[]{:S(2)}, u32[]{:S(2)}) collective-permute-start(f32[14,4,8,128]{3,2,1,0:T(8,128)S(1)} %get-tuple-element.18), channel_id=1, source_target_pairs={{0,8},{1,9},{2,10},{3,11},{4,12},{5,13},{6,14},{7,15},{8,0},{9,1},... | collective-permute-start | bytes 688136 | tf_op jit(solution)/shard_map/ppermute | solution.py:356
  9.9 12.0 %collective-permute-start.1 = (f32[14,4,8,128]{3,2,1,0:T(8,128)S(1)}, f32[14,4,8,128]{3,2,1,0:T(8,128)S(1)}, u32[]{:S(2)}, u32[]{:S(2)}) collective-permute-start(f32[14,4,8,128]{3,2,1,0:T(8,128)S(1)} %get-tuple-element.19), channel_id=1, source_target_pairs={{8,16},{9,17},{10,18},{11,19},{12,20},{13,21},{14,22},{15,23},{16,... | collective-permute-start | bytes 688136 | tf_op jit(solution)/shard_map/ppermute | solution.py:356
  21.8 21.3 %copy-start.1 = (f32[1,3,16,16,128]{4,3,2,1,0:T(8,128)S(1)}, f32[1,3,16,16,128]{4,3,2,1,0:T(8,128)}, u32[]{:S(2)}) copy-start(f32[1,3,16,16,128]{4,3,2,1,0:T(8,128)} %param.8) | copy-start | bytes 1179652
  21.8 21.3 %copy-start.3 = (f32[1,3,16,16,128]{4,3,2,1,0:T(8,128)S(1)}, f32[1,3,16,16,128]{4,3,2,1,0:T(8,128)}, u32[]{:S(2)}) copy-start(f32[1,3,16,16,128]{4,3,2,1,0:T(8,128)} %param.9) | copy-start | bytes 1179652
  21.8 21.4 %copy-start.9 = (s32[16,16,128]{2,1,0:T(8,128)S(1)}, s32[16,16,128]{2,1,0:T(8,128)}, u32[]{:S(2)}) copy-start(s32[16,16,128]{2,1,0:T(8,128)} %kind.3) | copy-start | bytes 393220
  22.5 20.6 %collective-permute-start.6 = (f32[14,24,4,128]{3,2,1,0:T(4,128)S(1)}, f32[14,24,4,128]{3,2,1,0:T(4,128)S(1)}, u32[]{:S(2)}, u32[]{:S(2)}) collective-permute-start(f32[14,24,4,128]{3,2,1,0:T(4,128)S(1)} %get-tuple-element.25), channel_id=1, source_target_pairs={{0,1},{1,0},{2,3},{3,2},{4,5},{5,4},{6,7},{7,6},{8,9},{9,8},{10,11... | collective-permute-start | bytes 2064392 | tf_op jit(solution)/shard_map/ppermute | solution.py:356
  24.4 18.7 %collective-permute-start.4 = (f32[14,16,4,128]{3,2,1,0:T(4,128)S(1)}, f32[14,16,4,128]{3,2,1,0:T(4,128)S(1)}, u32[]{:S(2)}, u32[]{:S(2)}) collective-permute-start(f32[14,16,4,128]{3,2,1,0:T(4,128)S(1)} %get-tuple-element.22), channel_id=1, source_target_pairs={{1,2},{2,1},{3,4},{4,3},{5,6},{6,5},{9,10},{10,9},{11,12},{12,11},... | collective-permute-start | bytes 1376264 | tf_op jit(solution)/shard_map/ppermute | solution.py:356
  27.9 10.5 %collective-permute-start.2 = (f32[14,4,8,128]{3,2,1,0:T(8,128)S(1)}, f32[14,4,8,128]{3,2,1,0:T(8,128)S(1)}, u32[]{:S(2)}, u32[]{:S(2)}) collective-permute-start(f32[14,4,8,128]{3,2,1,0:T(8,128)S(1)} %get-tuple-element.20), channel_id=1, source_target_pairs={{0,8},{1,9},{2,10},{3,11},{4,12},{5,13},{6,14},{7,15},{8,0},{9,1},... | collective-permute-start | bytes 688136 | tf_op jit(solution)/shard_map/ppermute | solution.py:356
  29.8 13.4 %copy-start.12 = (f32[1,4]{1,0:T(1,128)S(1)}, f32[1,4]{1,0:T(1,128)}, u32[]{:S(2)}) copy-start(f32[1,4]{1,0:T(1,128)} %table.1) | copy-start | bytes 52
  29.8 12.3 %collective-permute-start.3 = (f32[14,4,8,128]{3,2,1,0:T(8,128)S(1)}, f32[14,4,8,128]{3,2,1,0:T(8,128)S(1)}, u32[]{:S(2)}, u32[]{:S(2)}) collective-permute-start(f32[14,4,8,128]{3,2,1,0:T(8,128)S(1)} %get-tuple-element.21), channel_id=1, source_target_pairs={{8,16},{9,17},{10,18},{11,19},{12,20},{13,21},{14,22},{15,23},{16,... | collective-permute-start | bytes 688136 | tf_op jit(solution)/shard_map/ppermute | solution.py:356
  35.8 7.3 %collective-permute-start.5 = (f32[14,8,4,128]{3,2,1,0:T(4,128)S(1)}, f32[14,8,4,128]{3,2,1,0:T(4,128)S(1)}, u32[]{:S(2)}, u32[]{:S(2)}) collective-permute-start(f32[14,8,4,128]{3,2,1,0:T(4,128)S(1)} %get-tuple-element.24), channel_id=1, source_target_pairs={{1,2},{2,1},{3,4},{4,3},{5,6},{6,5},{9,10},{10,9},{11,12},{12,11},... | collective-permute-start | bytes 688136 | tf_op jit(solution)/shard_map/ppermute | solution.py:356

commit v2 on v1

v2 whole, which is shorter than its diff:
```python
import functools

import jax
import jax.numpy as jnp
from jax import lax
from jax.experimental import pallas as pl
from jax.experimental.pallas import tpu as pltpu
from jax.sharding import PartitionSpec as P

STEPS = 4
DZ = 16
TILE_COLS = 8
HALO = STEPS
KINDS = 14
CORNER_FLOPS = 2**36

dt_step = 0.5
depth_scale = 4.0

VMEM = pl.BlockSpec(memory_space=pltpu.VMEM)
SMEM = pl.BlockSpec(memory_space=pltpu.SMEM)
HBM = pl.BlockSpec(memory_space=pltpu.HBM)


def swap_pairs(count, cols, along_x, odd):
    rows = count // cols
    pairs = []
    for row in range(rows):
        for col in range(cols):
            place, size = (row, rows) if along_x else (col, cols)
            other = place + 1 if place % 2 == odd else place - 1
            if 0 <= other < size:
                target = other * cols + col if along_x else row * cols + other
                pairs.append((row * cols + col, target))
    return pairs


def low_half(shape):
    return lax.broadcasted_iota(jnp.int32, shape, len(shape) - 2) < 4


def staggered(block, by):
    row = lax.broadcasted_iota(jnp.int32, block.shape, 0)
    for bit in range(3):
        moved = pltpu.roll(block, (by << bit) % 128, 1)
        block = jnp.where((row >> bit) % 2 == 1, moved, block)
    return block


def pack_kernel(meta, ef, hf, ea, ha, kind, depth,
                own, xa1, xb1, xa2, xb2, yb, ya, whole, sems):
    row_even = lax.rem(meta[1], 2) == 0
    col_even = lax.rem(meta[2], 2) == 0
    cells = kind.shape[0]
    at_a = jnp.where(row_even, cells - HALO, 0)
    at_b = jnp.where(row_even, 0, cells - HALO)
    low = low_half((HALO, 8, 128))

    loads = []
    for k in range(12):
        loads.append(pltpu.make_async_copy(
            (ef, hf, ea, ha)[k // 3].at[k % 3], own.at[k], sems.at[k]))
    loads.append(pltpu.make_async_copy(kind, whole.at[0], sems.at[12]))
    loads.append(pltpu.make_async_copy(depth, whole.at[1], sems.at[13]))
    for load in loads:
        load.start()

    for k in range(KINDS):
        loads[k].wait()
        if k >= 12:
            own[k] = whole[k - 12].astype(jnp.float32)
        for at, first, second in ((at_a, xa1, xa2), (at_b, xb1, xb2)):
            rows = pl.ds(at, HALO)
            t0 = own[k, rows, 0:8, :]
            t1 = own[k, rows, 8:16, :]
            first[k] = jnp.where(low, t0, t1)
            second[k] = jnp.where(low, t1, t0)

    def strips(to_a, to_b):
        for k in range(KINDS):
            ya[k] = own[k, :, to_a, :]
            yb[k] = own[k, :, to_b, :]

    @pl.when(col_even)
    def _():
        strips(slice(12, 16), slice(0, 4))

    @pl.when(jnp.logical_not(col_even))
    def _():
        strips(slice(0, 4), slice(12, 16))


def pack(meta, fields, kind, depth):
    cells = kind.shape[0]
    edge = jax.ShapeDtypeStruct((KINDS, HALO, 8, 128), jnp.float32)
    strip = jax.ShapeDtypeStruct((KINDS, cells, 4, 128), jnp.float32)
    return pl.pallas_call(
        pack_kernel,
        out_shape=(jax.ShapeDtypeStruct((KINDS, cells, cells, 128), jnp.float32),
                   edge, edge, edge, edge, strip, strip),
        in_specs=[SMEM] + [HBM] * 6,
        out_specs=[VMEM] * 7,
        scratch_shapes=[
            pltpu.VMEM((2, cells, cells, 128), jnp.int32),
            pltpu.SemaphoreType.DMA((KINDS,)),
        ],
        compiler_params=pltpu.CompilerParams(vmem_limit_bytes=16 * 2**20),
        name="pack",
    )(meta, *(pltpu.with_memory_space_constraint(value, pltpu.HBM)
             for value in (*fields, kind, depth)))


def corner_kernel(meta, ra1, rb1, ya, cb, yac):
    col_even = lax.rem(meta[2], 2) == 0
    cells = ya.shape[1]
    yac[:, 0:cells] = ya[...]

    def put(to_a, to_b):
        for k in range(KINDS):
            yac[k, cells:cells + HALO] = ra1[k, :, to_a, :]
            yac[k, cells + HALO:cells + 2 * HALO] = rb1[k, :, to_a, :]
            cb[k, 0:HALO] = ra1[k, :, to_b, :]
            cb[k, HALO:2 * HALO] = rb1[k, :, to_b, :]

    @pl.when(col_even)
    def _():
        put(slice(4, 8), slice(0, 4))

    @pl.when(jnp.logical_not(col_even))
    def _():
        put(slice(0, 4), slice(4, 8))


def corners(meta, ra1, rb1, ya):
    cells = ya.shape[1]
    return pl.pallas_call(
        corner_kernel,
        out_shape=(
            jax.ShapeDtypeStruct((KINDS, 2 * HALO, 4, 128), jnp.float32),
            jax.ShapeDtypeStruct((KINDS, cells + 2 * HALO, 4, 128), jnp.float32),
        ),
        in_specs=[SMEM] + [VMEM] * 3,
        out_specs=[VMEM] * 2,
        compiler_params=pltpu.CompilerParams(vmem_limit_bytes=16 * 2**20),
        cost_estimate=pl.CostEstimate(flops=CORNER_FLOPS, bytes_accessed=2**20, transcendentals=0),
        name="corners",
    )(meta, ra1, rb1, ya)


def coefficients(m, d, table, outside):
    eps = jnp.where(m < 0.5, table[0, 0],
                    jnp.where(m < 1.5, table[0, 1],
                              jnp.where(m < 2.5, table[0, 2], table[0, 3])))
    ramp = d / depth_scale
    sigma = ramp * ramp
    s_e = sigma * dt_step / (2.0 * eps)
    s_h = sigma * dt_step / 2.0
    return ((1.0 - s_e) / (1.0 + s_e), jnp.where(outside, 0.0, dt_step / (eps * (1.0 + s_e))),
            (1.0 - s_h) / (1.0 + s_h), jnp.where(outside, 0.0, dt_step / (1.0 + s_h)))


def outside_rows(x, cells, row, rows):
    return jnp.logical_or(jnp.logical_and(x < HALO, row == 0),
                          jnp.logical_and(x >= HALO + cells, row == rows - 1))


def halo_rows(row, cells):
    even = lax.rem(row, 2) == 0
    return jnp.where(even, HALO + cells, 0), jnp.where(even, 0, HALO + cells)


def prepare_kernel(rows, meta, table, own, ra1, rb1, ra2, rb2, field, ca, cb, da, db, matter):
    row = meta[1]
    cells = own.shape[1]
    wide = cells + 2 * HALO
    off_a, off_b = halo_rows(row, cells)
    low = low_half((HALO, 8, 128))
    for k in range(KINDS):
        to = field.at[k] if k < 12 else matter.at[k - 12]
        to[HALO:HALO + cells, 0:cells, :] = own[k]
        for off, first, second in ((off_a, ra1, ra2), (off_b, rb1, rb2)):
            here = pl.ds(off, HALO)
            edge, mid = first[k], second[k]
            to[here, 0:8, :] = jnp.where(low, edge, mid)
            to[here, 8:16, :] = jnp.where(low, mid, edge)

    def fill(x, _):
        outside = outside_rows(x, cells, row, rows)
        values = coefficients(matter[0, x], matter[1, x], table, outside)
        for plane, value in zip((ca, cb, da, db), values):
            plane[x, 0:cells, :] = value
        return 0

    lax.fori_loop(0, wide, fill, 0, unroll=2)


def prepare(rows, meta, table, own, halos):
    cells = own.shape[1]
    wide = cells + 2 * HALO
    plane = jax.ShapeDtypeStruct((wide, wide, 128), jnp.float32)
    return pl.pallas_call(
        functools.partial(prepare_kernel, rows),
        out_shape=(jax.ShapeDtypeStruct((12, wide, wide, 128), jnp.float32),
                   plane, plane, plane, plane),
        in_specs=[SMEM, SMEM] + [VMEM] * 5,
        out_specs=[VMEM] * 5,
        scratch_shapes=[pltpu.VMEM((2, wide, cells, 128), jnp.float32)],
        compiler_params=pltpu.CompilerParams(vmem_limit_bytes=16 * 2**20),
        cost_estimate=pl.CostEstimate(flops=2**36, bytes_accessed=2**22, transcendentals=0),
        name="prepare",
    )(meta, table, own, *halos)


def steps_kernel(cols, rows, meta, table, field_in, ca_in, cb_in, da_in, db_in, rb, rcb, rya,
                 ef_out, hf_out, ea_out, ha_out, send, field, ca, cb, da, db, total, matter):
    start, row, col = meta[0], meta[1], meta[2]
    col_even = lax.rem(col, 2) == 0
    cells = rb.shape[1]
    wide = cells + 2 * HALO
    own = slice(HALO, HALO + cells)
    off_a, off_b = halo_rows(row, cells)

    def columns(first_a, first_b):
        for k in range(KINDS):
            to, base = (field.at[k], cells) if k < 12 else (matter.at[k - 12], 0)
            side_a = slice(base + first_a, base + first_a + 4)
            side_b = slice(base + first_b, base + first_b + 4)
            to[own, side_a, :] = rya[k, 0:cells]
            to[pl.ds(off_a, HALO), side_a, :] = rya[k, cells:cells + HALO]
            to[pl.ds(off_b, HALO), side_a, :] = rya[k, cells + HALO:wide]
            to[own, side_b, :] = rb[k]
            to[pl.ds(off_a, HALO), side_b, :] = rcb[k, 0:HALO]
            to[pl.ds(off_b, HALO), side_b, :] = rcb[k, HALO:2 * HALO]

    @pl.when(col_even)
    def _():
        columns(0, 4)

    @pl.when(jnp.logical_not(col_even))
    def _():
        columns(4, 0)

    after = low_half((8, 128))
    outside_y = jnp.logical_or(jnp.logical_and(after, col == cols - 1),
                               jnp.logical_and(jnp.logical_not(after), col == 0))

    def fill(x, _):
        outside = jnp.logical_or(outside_y, outside_rows(x, cells, row, rows))
        values = coefficients(matter[0, x], matter[1, x], table, outside)
        for plane, value in zip((ca, cb, da, db), values):
            plane[x, cells:wide, :] = value
        return 0

    lax.fori_loop(0, wide, fill, 0, unroll=4)

    lane = lax.broadcasted_iota(jnp.int32, (wide, 128), 1)
    last_z, first_z = lane == 127, lane == 0

    def up_z(v):
        return jnp.where(last_z, 0.0, pltpu.roll(v, 127, 1))

    def down_z(v):
        return jnp.where(first_z, 0.0, pltpu.roll(v, 1, 1))

    def up_y(v):
        return pltpu.roll(v, wide - 1, 0)

    def down_y(v):
        return pltpu.roll(v, 1, 0)

    def h_new(e, h, x, dax, dbx):
        ex, ey, ez = field[e, x], field[e + 1, x], field[e + 2, x]
        ey1, ez1 = field[e + 1, x + 1], field[e + 2, x + 1]
        return (dax * field[h, x] - dbx * ((up_y(ez) - ez) - (up_z(ey) - ey)),
                dax * field[h + 1, x] - dbx * ((up_z(ex) - ex) - (ez1 - ez)),
                dax * field[h + 2, x] - dbx * ((ey1 - ey) - (up_y(ex) - ex)))

    def e_new(e, x, cax, cbx, now, before):
        hx, hy, hz = now
        hy1, hz1 = before
        return (cax * field[e, x] + cbx * ((hz - down_y(hz)) - (hy - down_z(hy))),
                cax * field[e + 1, x] + cbx * ((hx - down_z(hx)) - (hz - hz1)),
                cax * field[e + 2, x] + cbx * ((hy - hy1) - (hx - down_y(hx))))

    outs = {0: ef_out, 3: hf_out, 6: ea_out, 9: ha_out}

    def two_rows(step, i, _):
        x0 = step + 1 + 2 * i
        es = []
        for e, h in ((0, 3), (6, 9)):
            hs, news = [], []
            before = field[h + 1, x0 - 1], field[h + 2, x0 - 1]
            for u in range(2):
                x = x0 + u
                hs.append(h_new(e, h, x, da[x], db[x]))
                news.append(e_new(e, x, ca[x], cb[x], hs[-1], before))
                before = hs[-1][1:]
            for u in range(2):
                for k, new in ((h, hs[u]), (e, news[u])):
                    for n in range(3):
                        if step == STEPS - 1:
                            outs[k][n, x0 + u - HALO] = new[n][0:cells]
                            if k == h and u == 1 and n > 0:
                                field[k + n, x0 + u] = new[n]
                        else:
                            field[k + n, x0 + u] = new[n]
            es.append(news)
        for u in range(2):
            term = sum(es[0][u][n][0:cells] * es[1][u][n][0:cells] for n in range(3))
            total[x0 + u] = term if step == 0 else total[x0 + u] + term
        return 0

    for step in range(STEPS):
        for e, h in ((0, 3), (6, 9)):
            first = h_new(e, h, step, da[step], db[step])
            for n in range(3):
                field[h + n, step] = first[n]
        lax.fori_loop(0, (wide - 2 - 2 * step) // 2, functools.partial(two_rows, step), 0,
                      unroll=2)

    sub = lax.broadcasted_iota(jnp.int32, (8, 128), 0)
    mine = lax.broadcasted_iota(jnp.int32, (8, 128), 1) // DZ == sub
    for tile in range(cells * 2 // 8):
        block = jnp.zeros((8, 128), jnp.float32)
        for n in range(8):
            x, half = HALO + (tile * 8 + n) // 2, (tile * 8 + n) % 2
            moved = pltpu.roll(total[x, 8 * half:8 * half + 8, :], 128 - start, 1)
            line = jnp.sum(jnp.where(mine, staggered(moved, DZ), 0.0), axis=0, keepdims=True)
            block = jnp.where(sub == n, line, block)
        for peer in range(send.shape[0]):
            send[peer, tile * 8:tile * 8 + 8, :] = block


def all_steps(cols, rows, waves, meta, table, state, halos):
    wide = state[0].shape[1]
    cells = wide - 2 * HALO
    out = jax.ShapeDtypeStruct((3, cells, cells, 128), jnp.float32)
    plane = jax.ShapeDtypeStruct((wide, wide, 128), jnp.float32)
    return pl.pallas_call(
        functools.partial(steps_kernel, cols, rows),
        out_shape=(out, out, out, out,
                   jax.ShapeDtypeStruct((waves, cells * 2, 128), jnp.float32),
                   jax.ShapeDtypeStruct((12, wide, wide, 128), jnp.float32),
                   plane, plane, plane, plane),
        in_specs=[SMEM, SMEM] + [VMEM] * 8,
        out_specs=[VMEM] * 10,
        scratch_shapes=[
            pltpu.VMEM((wide, cells, 128), jnp.float32),
            pltpu.VMEM((2, wide, 8, 128), jnp.float32),
        ],
        input_output_aliases={2: 5, 3: 6, 4: 7, 5: 8, 6: 9},
        compiler_params=pltpu.CompilerParams(vmem_limit_bytes=16 * 2**20),
        name="steps",
    )(meta, table, *state, *halos)[:5]


def gradient_kernel(parts, out):
    waves, lines, _ = parts.shape
    whole = parts[0]
    for wave in range(1, waves):
        whole = whole + parts[wave]
    for n in range(lines):
        spread = jnp.broadcast_to(whole[n:n + 1, :], (8, 128))
        moved = staggered(spread, 128 - DZ)
        out[n // 2, 8 * (n % 2):8 * (n % 2) + 8, :] = moved[:, 0:DZ]


def gradient_of(parts):
    cells = parts.shape[1] // 2
    return pl.pallas_call(
        gradient_kernel,
        out_shape=jax.ShapeDtypeStruct((cells, cells, DZ), jnp.float32),
        in_specs=[VMEM],
        out_specs=VMEM,
        compiler_params=pltpu.CompilerParams(vmem_limit_bytes=8 * 2**20),
        name="gradient",
    )(parts)


def per_device(
    e_forward, h_forward, e_adjoint, h_adjoint, eps_table, material, pml_depth, design_start
):
    cols = TILE_COLS
    count = lax.axis_size("tile")
    rows = count // cols
    me = lax.axis_index("tile")
    meta = jnp.stack([design_start[0], me // cols, me % cols]).astype(jnp.int32)
    fields = (e_forward[0], h_forward[0], e_adjoint[0], h_adjoint[0])

    def swap(value, along_x, odd):
        return lax.ppermute(value, "tile", swap_pairs(count, cols, along_x, odd))

    own, xa1, xb1, xa2, xb2, yb, ya = pack(meta, fields, material, pml_depth)
    ra1 = swap(xa1, True, 0)
    rb1 = swap(xb1, True, 1)
    rb = swap(yb, False, 1)
    ra2 = swap(xa2, True, 0)
    rb2 = swap(xb2, True, 1)
    cb, yac = corners(meta, ra1, rb1, ya)
    rcb = swap(cb, False, 1)
    rya = swap(yac, False, 0)
    state = prepare(rows, meta, eps_table, own, (ra1, rb1, ra2, rb2))
    *outs, send = all_steps(cols, rows, lax.axis_size("wave"), meta, eps_table, state,
                            (rb, rcb, rya))
    parts = lax.all_to_all(send, "wave", 0, 0)
    gradient = gradient_of(parts)
    return tuple(out[None] for out in outs) + (gradient,)


def solution(mesh):
    return jax.shard_map(
        per_device,
        mesh=mesh,
        in_specs=(
            P("wave", None, "tile", None, None),
            P("wave", None, "tile", None, None),
            P("wave", None, "tile", None, None),
            P("wave", None, "tile", None, None),
            P("wave", None),
            P("tile", None, None),
            P("tile", None, None),
            P("tile"),
        ),
        out_specs=(
            P("wave", None, "tile", None, None),
            P("wave", None, "tile", None, None),
            P("wave", None, "tile", None, None),
            P("wave", None, "tile", None, None),
            P("tile", None, None),
        ),
        check_vma=False,
    )
```

time: 81.3 us -> 60.9 us (0.75)
  waiting for transfers between devices: 10.1 us -> 2.96 us
  Pallas kernels: 18.5 us -> 11.6 us
  local copies, waits for them, and re-layouts: 5.82 us -> 0.01 us
  blocking collectives: 20.5 us -> 19.6 us
    pallas_call x1, Pallas kernels: 16.2 us -> 6.63 us  [all_steps(): pl.pallas_call(functools.partial(steps_kernel, cols, rows), out_shape=(ou...]
    ppermute x7, waiting for transfers between devices: 10.1 us -> 2.96 us  [swap(): return lax.ppermute(value, 'tile', swap_pairs(count, cols, along_x, odd))]
    unnamed x26 -> x2, local copies, waits for them, and re-layouts: 5.82 us -> 0.01 us
    pallas_call x1 -> x2, Pallas kernels: 0.77 us -> 3.43 us  [the longest x1 2.35 us: pack(): pl.pallas_call(pack_kernel, out_shape=(jax.ShapeDtypeStruct((KINDS, cells...]
    all_to_all x1, blocking collectives: 20.5 us -> 19.6 us  [per_device(): parts = lax.all_to_all(send, 'wave', 0, 0)]
  transfers between devices with their start and end apart: 7 -> 7, of which waited for: 4 -> 1; matrix products, arithmetic and copies ran while one was open for 0% -> 0% of each run, Pallas kernels for 0% -> 3%
where the time goes in v2:
time: 60.9 us; the launch traced here: 60.6 us
  starting transfers between devices  24.9 us (41%)
  blocking collectives  19.6 us (32%)
  Pallas kernels  11.6 us (19%)
  waiting for transfers between devices  2.96 us (5%)
  between operations  1.43 us (2%)
    ppermute x7, starting transfers between devices, swap(): return lax.ppermute(value, 'tile', swap_pairs(count, cols, along_x, odd))  24.9 us
    all_to_all x1, blocking collectives, per_device(): parts = lax.all_to_all(send, 'wave', 0, 0)  19.6 us
    pallas_call x1, Pallas kernels, all_steps(): pl.pallas_call(functools.partial(steps_kernel, cols, rows), out_shape=(ou...  6.63 us
    ppermute x7, waiting for transfers between devices, swap(): return lax.ppermute(value, 'tile', swap_pairs(count, cols, along_x, odd))  2.96 us
    pallas_call x1, Pallas kernels, pack(): pl.pallas_call(pack_kernel, out_shape=(jax.ShapeDtypeStruct((KINDS, cells...  2.35 us
  transfers between devices with their start and end apart: 7, of which 1 were waited for; matrix products, arithmetic and copies ran while one was open for 0% of the time, Pallas kernels for 3%

profile of v2, /device:TPU:72, one launch (start us, length us, event | category | flops | bytes accessed | tf_op | source)
XLA Modules:
  0.0 60.6 jit_solution(17278614552726937158)
XLA Ops:
  1.3 0.1 pad_add_fusion.meta
  1.4 2.4 %pack.1 = (f32[14,16,16,128]{3,2,1,0:T(8,128)S(1)}, f32[14,4,8,128]{3,2,1,0:T(8,128)S(1)}, f32[14,4,8,128]{3,2,1,0:T(8,128)S(1)}, f32[14,4,8,128]{3,2,1,0:T(8,12...) custom-call(s32[3]{0:T(128)S(1)} %pad_add_fusion.meta, ...), custom_call_target="tpu_custom_call" | custom-call | tf_op jit(solution)/shard_map/pack/pallas_call | solution.py:97
  3.7 1.9 %collective-permute-start = (f32[14,4,8,128]{3,2,1,0:T(8,128)S(1)}, f32[14,4,8,128]{3,2,1,0:T(8,128)S(1)}, u32[]{:S(2)}, u32[]{:S(2)}) collective-permute-start(f32[14,4,8,128]{3,2,1,0:T(8,128)S(1)} %get-tuple-element.25), channel_id=1, source_target_pairs={{0,8},{1,9},{2,10},{3,11},{4,12},{5,13},{6,14},{7,15},{8,0},{9,1},... | collective-permute-start | bytes 688136 | tf_op jit(solution)/shard_map/ppermute | solution.py:391
  5.7 6.6 %collective-permute-start.1 = (f32[14,4,8,128]{3,2,1,0:T(8,128)S(1)}, f32[14,4,8,128]{3,2,1,0:T(8,128)S(1)}, u32[]{:S(2)}, u32[]{:S(2)}) collective-permute-start(f32[14,4,8,128]{3,2,1,0:T(8,128)S(1)} %get-tuple-element.26), channel_id=1, source_target_pairs={{8,16},{9,17},{10,18},{11,19},{12,20},{13,21},{14,22},{15,23},{16,... | collective-permute-start | bytes 688136 | tf_op jit(solution)/shard_map/ppermute | solution.py:391
  12.3 1.9 %collective-permute-start.2 = (f32[14,4,8,128]{3,2,1,0:T(8,128)S(1)}, f32[14,4,8,128]{3,2,1,0:T(8,128)S(1)}, u32[]{:S(2)}, u32[]{:S(2)}) collective-permute-start(f32[14,4,8,128]{3,2,1,0:T(8,128)S(1)} %get-tuple-element.27), channel_id=1, source_target_pairs={{0,8},{1,9},{2,10},{3,11},{4,12},{5,13},{6,14},{7,15},{8,0},{9,1},... | collective-permute-start | bytes 688136 | tf_op jit(solution)/shard_map/ppermute | solution.py:391
  14.2 7.0 %collective-permute-start.3 = (f32[14,4,8,128]{3,2,1,0:T(8,128)S(1)}, f32[14,4,8,128]{3,2,1,0:T(8,128)S(1)}, u32[]{:S(2)}, u32[]{:S(2)}) collective-permute-start(f32[14,4,8,128]{3,2,1,0:T(8,128)S(1)} %get-tuple-element.28), channel_id=1, source_target_pairs={{8,16},{9,17},{10,18},{11,19},{12,20},{13,21},{14,22},{15,23},{16,... | collective-permute-start | bytes 688136 | tf_op jit(solution)/shard_map/ppermute | solution.py:391
  21.2 1.9 %collective-permute-start.4 = (f32[14,16,4,128]{3,2,1,0:T(4,128)S(1)}, f32[14,16,4,128]{3,2,1,0:T(4,128)S(1)}, u32[]{:S(2)}, u32[]{:S(2)}) collective-permute-start(f32[14,16,4,128]{3,2,1,0:T(4,128)S(1)} %get-tuple-element.34), channel_id=1, source_target_pairs={{1,2},{2,1},{3,4},{4,3},{5,6},{6,5},{9,10},{10,9},{11,12},{12,11},... | collective-permute-start | bytes 1376264 | tf_op jit(solution)/shard_map/ppermute | solution.py:391
  23.1 0.0 collective-permute-done.ra1
  23.1 0.0 collective-permute-done.1.rb1
  23.1 0.0 copy-start
  23.2 0.7 %corners.1 = (f32[14,8,4,128]{3,2,1,0:T(4,128)S(1)}, f32[14,24,4,128]{3,2,1,0:T(4,128)S(1)}) custom-call(s32[3]{0:T(128)S(1)} %pad_add_fusion.meta, f32[14,4,8,128]{3,2,1,0:T(8,128)S(1)} %collective-permute-done.ra1, f32[14,4,8,128]{3,2,1,0:T(8,128)S(1)} %collective-permute-done.1.rb1, f32[14,16,4,128]{3,2,1,0:T(4,128)S(1)} %get-tuple-element.35.ya), custom_call_target="tpu_custom_call" | custom-call | flops 68719476736 | bytes 1048576 | tf_op jit(solution)/shard_map/corners/pallas_call | solution.py:136
  23.8 3.6 %collective-permute-start.5 = (f32[14,8,4,128]{3,2,1,0:T(4,128)S(1)}, f32[14,8,4,128]{3,2,1,0:T(4,128)S(1)}, u32[]{:S(2)}, u32[]{:S(2)}) collective-permute-start(f32[14,8,4,128]{3,2,1,0:T(4,128)S(1)} %get-tuple-element.36), channel_id=1, source_target_pairs={{1,2},{2,1},{3,4},{4,3},{5,6},{6,5},{9,10},{10,9},{11,12},{12,11},... | collective-permute-start | bytes 688136 | tf_op jit(solution)/shard_map/ppermute | solution.py:391
  27.5 1.9 %collective-permute-start.6 = (f32[14,24,4,128]{3,2,1,0:T(4,128)S(1)}, f32[14,24,4,128]{3,2,1,0:T(4,128)S(1)}, u32[]{:S(2)}, u32[]{:S(2)}) collective-permute-start(f32[14,24,4,128]{3,2,1,0:T(4,128)S(1)} %get-tuple-element.37), channel_id=1, source_target_pairs={{0,1},{1,0},{2,3},{3,2},{4,5},{5,4},{6,7},{7,6},{8,9},{9,8},{10,11... | collective-permute-start | bytes 2064392 | tf_op jit(solution)/shard_map/ppermute | solution.py:391
  29.4 0.0 collective-permute-done.2.ra2
  29.4 0.0 collective-permute-done.3.rb2
  29.4 0.0 copy-done
  29.4 1.1 %prepare.1 = (f32[12,24,24,128]{3,2,1,0:T(8,128)S(1)}, f32[24,24,128]{2,1,0:T(8,128)S(1)}, f32[24,24,128]{2,1,0:T(8,128)S(1)}, f32[24,24,128]{2,1,0:T(8,128)S(1)}, f32[24,24,128]{2,1,0:T(8,128)S(1)}) custom-call(s32[3]{0:T(128)S(1)} %pad_add_fusion.meta, f32[1,4]{1,0:T(1,128)S(1)} %copy-done, f32[14,16,16,128]{3,2,1,0:T(8,128)S(1)} %get-tuple-element.24.own, ...), custom_call_target="tpu_custom_call" | custom-call | flops 68719476736 | bytes 4194304 | tf_op jit(solution)/shard_map/prepare/pallas_call | solution.py:201
  30.5 2.9 %collective-permute-done.5.rcb = f32[14,8,4,128]{3,2,1,0:T(4,128)S(1)} collective-permute-done((f32[14,8,4,128]{3,2,1,0:T(4,128)S(1)}, f32[14,8,4,128]{3,2,1,0:T(4,128)S(1)}, u32[]{:S(2)}, u32[]{:S(2)}) %collective-permute-start.5) | collective-permute-done | bytes 229408 | tf_op jit(solution)/shard_map/ppermute | solution.py:391
  33.5 0.0 collective-permute-done.4.rb
  33.5 0.0 collective-permute-done.6.rya
  33.5 6.6 %steps.1 = (f32[3,16,16,128]{3,2,1,0:T(8,128)}, f32[3,16,16,128]{3,2,1,0:T(8,128)}, f32[3,16,16,128]{3,2,1,0:T(8,128)}, f32[3,16,16,128]{3,2,1,0:T(8,128)}, f32[...) custom-call(s32[3]{0:T(128)S(1)} %pad_add_fusion.meta, ...), custom_call_target="tpu_custom_call", output_to_operand_aliasing={{5}: (2, {}), {6}: (3, {}), {7}: (4, {}), {8}: (5, {}), {9}... | custom-call | tf_op jit(solution)/shard_map/steps/pallas_call | solution.py:339
  40.1 19.6 %all_to_all.5.parts = f32[8,32,128]{2,1,0:T(8,128)S(1)} all-to-all(f32[8,32,128]{2,1,0:T(8,128)S(1)} %get-tuple-element.42), channel_id=1, replica_groups=mesh['wave'=8,'tile'=64] {'wave'}, dimensions={0} | all-to-all | bytes 262144 | tf_op jit(solution)/shard_map/all_to_all | solution.py:405
  59.7 0.9 %gradient.1 = f32[16,16,16]{2,1,0:T(8,128)} custom-call(f32[8,32,128]{2,1,0:T(8,128)S(1)} %all_to_all.5.parts), custom_call_target="tpu_custom_call" | custom-call | tf_op jit(solution)/shard_map/gradient/pallas_call | solution.py:370
Async XLA Ops:
  3.7 19.4 %collective-permute-start = (f32[14,4,8,128]{3,2,1,0:T(8,128)S(1)}, f32[14,4,8,128]{3,2,1,0:T(8,128)S(1)}, u32[]{:S(2)}, u32[]{:S(2)}) collective-permute-start(f32[14,4,8,128]{3,2,1,0:T(8,128)S(1)} %get-tuple-element.25), channel_id=1, source_target_pairs={{0,8},{1,9},{2,10},{3,11},{4,12},{5,13},{6,14},{7,15},{8,0},{9,1},... | collective-permute-start | bytes 688136 | tf_op jit(solution)/shard_map/ppermute | solution.py:391
  5.7 17.5 %collective-permute-start.1 = (f32[14,4,8,128]{3,2,1,0:T(8,128)S(1)}, f32[14,4,8,128]{3,2,1,0:T(8,128)S(1)}, u32[]{:S(2)}, u32[]{:S(2)}) collective-permute-start(f32[14,4,8,128]{3,2,1,0:T(8,128)S(1)} %get-tuple-element.26), channel_id=1, source_target_pairs={{8,16},{9,17},{10,18},{11,19},{12,20},{13,21},{14,22},{15,23},{16,... | collective-permute-start | bytes 688136 | tf_op jit(solution)/shard_map/ppermute | solution.py:391
  12.3 17.1 %collective-permute-start.2 = (f32[14,4,8,128]{3,2,1,0:T(8,128)S(1)}, f32[14,4,8,128]{3,2,1,0:T(8,128)S(1)}, u32[]{:S(2)}, u32[]{:S(2)}) collective-permute-start(f32[14,4,8,128]{3,2,1,0:T(8,128)S(1)} %get-tuple-element.27), channel_id=1, source_target_pairs={{0,8},{1,9},{2,10},{3,11},{4,12},{5,13},{6,14},{7,15},{8,0},{9,1},... | collective-permute-start | bytes 688136 | tf_op jit(solution)/shard_map/ppermute | solution.py:391
  14.2 15.2 %collective-permute-start.3 = (f32[14,4,8,128]{3,2,1,0:T(8,128)S(1)}, f32[14,4,8,128]{3,2,1,0:T(8,128)S(1)}, u32[]{:S(2)}, u32[]{:S(2)}) collective-permute-start(f32[14,4,8,128]{3,2,1,0:T(8,128)S(1)} %get-tuple-element.28), channel_id=1, source_target_pairs={{8,16},{9,17},{10,18},{11,19},{12,20},{13,21},{14,22},{15,23},{16,... | collective-permute-start | bytes 688136 | tf_op jit(solution)/shard_map/ppermute | solution.py:391
  21.2 12.3 %collective-permute-start.4 = (f32[14,16,4,128]{3,2,1,0:T(4,128)S(1)}, f32[14,16,4,128]{3,2,1,0:T(4,128)S(1)}, u32[]{:S(2)}, u32[]{:S(2)}) collective-permute-start(f32[14,16,4,128]{3,2,1,0:T(4,128)S(1)} %get-tuple-element.34), channel_id=1, source_target_pairs={{1,2},{2,1},{3,4},{4,3},{5,6},{6,5},{9,10},{10,9},{11,12},{12,11},... | collective-permute-start | bytes 1376264 | tf_op jit(solution)/shard_map/ppermute | solution.py:391
  23.1 6.3 %copy-start = (f32[1,4]{1,0:T(1,128)S(1)}, f32[1,4]{1,0:T(1,128)}, u32[]{:S(2)}) copy-start(f32[1,4]{1,0:T(1,128)} %table.3) | copy-start | bytes 52
  23.8 9.6 %collective-permute-start.5 = (f32[14,8,4,128]{3,2,1,0:T(4,128)S(1)}, f32[14,8,4,128]{3,2,1,0:T(4,128)S(1)}, u32[]{:S(2)}, u32[]{:S(2)}) collective-permute-start(f32[14,8,4,128]{3,2,1,0:T(4,128)S(1)} %get-tuple-element.36), channel_id=1, source_target_pairs={{1,2},{2,1},{3,4},{4,3},{5,6},{6,5},{9,10},{10,9},{11,12},{12,11},... | collective-permute-start | bytes 688136 | tf_op jit(solution)/shard_map/ppermute | solution.py:391
  27.5 6.0 %collective-permute-start.6 = (f32[14,24,4,128]{3,2,1,0:T(4,128)S(1)}, f32[14,24,4,128]{3,2,1,0:T(4,128)S(1)}, u32[]{:S(2)}, u32[]{:S(2)}) collective-permute-start(f32[14,24,4,128]{3,2,1,0:T(4,128)S(1)} %get-tuple-element.37), channel_id=1, source_target_pairs={{0,1},{1,0},{2,3},{3,2},{4,5},{5,4},{6,7},{7,6},{8,9},{9,8},{10,11... | collective-permute-start | bytes 2064392 | tf_op jit(solution)/shard_map/ppermute | solution.py:391

commit v3 on v2

v3 whole, which is shorter than its diff:
```python
import functools

import jax
import jax.numpy as jnp
from jax import lax
from jax.experimental import pallas as pl
from jax.experimental.pallas import tpu as pltpu
from jax.sharding import PartitionSpec as P

STEPS = 4
DZ = 16
TILE_COLS = 8
HALO = STEPS
KINDS = 14
UNROLL = 5
CORNER_FLOPS = 2**36
LOAD_FLOPS = 2**30
PREPARE_FLOPS = 2**36

dt_step = 0.5
depth_scale = 4.0

VMEM = pl.BlockSpec(memory_space=pltpu.VMEM)
SMEM = pl.BlockSpec(memory_space=pltpu.SMEM)
HBM = pl.BlockSpec(memory_space=pltpu.HBM)
ANY = pl.BlockSpec(memory_space=pl.ANY)


def swap_pairs(count, cols, along_x, odd):
    rows = count // cols
    pairs = []
    for row in range(rows):
        for col in range(cols):
            place, size = (row, rows) if along_x else (col, cols)
            other = place + 1 if place % 2 == odd else place - 1
            if 0 <= other < size:
                target = other * cols + col if along_x else row * cols + other
                pairs.append((row * cols + col, target))
    return pairs


def low_half(shape):
    return lax.broadcasted_iota(jnp.int32, shape, len(shape) - 2) < 4


def staggered(block, by):
    row = lax.broadcasted_iota(jnp.int32, block.shape, 0)
    for bit in range(3):
        moved = pltpu.roll(block, (by << bit) % 128, 1)
        block = jnp.where((row >> bit) % 2 == 1, moved, block)
    return block


DEEP = (0, 1, 2, 4, 5, 6, 7, 8, 10, 11, 13)
SHALLOW = (3, 9, 12)
LAYERS = 4 * len(DEEP) + 3 * len(SHALLOW)


def layer_places():
    places = [(k, 4 * n, 4) for n, k in enumerate(DEEP)]
    return places + [(k, 4 * len(DEEP) + 3 * n, 3) for n, k in enumerate(SHALLOW)]


def tile_place(cols):
    me = lax.axis_index("tile")
    return lax.div(me, cols), lax.rem(me, cols)


def is_even(place):
    return lax.rem(place, 2) == 0


def edges_kernel(cols, ef, hf, ea, ha, kind, depth, xa, xb, whole, sems):
    row, _ = tile_place(cols)
    cells = kind.shape[0]
    sources = [(ef, hf, ea, ha)[k // 3].at[k % 3] for k in range(12)] + [kind, depth]
    loads = []
    for side, to in enumerate((xa, xb)):
        at_end = is_even(row) if side == 0 else jnp.logical_not(is_even(row))
        for k, place, count in layer_places():
            at = jnp.where(at_end, cells - count, 0)
            target = to.at[pl.ds(place, count)]
            if k >= 12:
                target = whole.at[2 * side + k - 12, pl.ds(0, count)]
            loads.append(pltpu.make_async_copy(
                sources[k].at[pl.ds(at, count)], target, sems.at[side * KINDS + k]))
            loads[-1].start()
    for load in loads:
        load.wait()
    for side, to in enumerate((xa, xb)):
        for k, place, count in layer_places():
            if k >= 12:
                to[place:place + count] = whole[2 * side + k - 12, 0:count].astype(jnp.float32)


def in_hbm(values):
    return [pltpu.with_memory_space_constraint(value, pltpu.HBM) for value in values]


def edges(cols, fields, kind, depth):
    cells = kind.shape[0]
    layers = jax.ShapeDtypeStruct((LAYERS, cells, 128), jnp.float32)
    return pl.pallas_call(
        functools.partial(edges_kernel, cols),
        out_shape=(layers, layers),
        in_specs=[HBM] * 6,
        out_specs=[VMEM] * 2,
        scratch_shapes=[
            pltpu.VMEM((4, HALO, cells, 128), jnp.int32),
            pltpu.SemaphoreType.DMA((2 * KINDS,)),
        ],
        compiler_params=pltpu.CompilerParams(vmem_limit_bytes=16 * 2**20),
        cost_estimate=pl.CostEstimate(flops=2**20, bytes_accessed=2**20, transcendentals=0),
        name="edges",
    )(*in_hbm((*fields, kind, depth)))


def load_kernel(cols, eps_table, ef, hf, ea, ha, kind, depth, after,
                field, ca, cb, da, db, ya, yb, spread, whole, few, sems):
    _, col = tile_place(cols)
    cells = kind.shape[0]
    own = pl.ds(HALO, cells)
    loads = []
    for n, k in enumerate((12, 13) + tuple(range(12))):
        source = (kind, depth)[k - 12] if k >= 12 else (ef, hf, ea, ha)[k // 3].at[k % 3]
        target = whole.at[k - 12] if k >= 12 else field.at[k, own, pl.ds(0, cells), :]
        loads.append(pltpu.make_async_copy(source, target, sems.at[k]))
        loads[-1].start()
    loads.append(pltpu.make_async_copy(eps_table, few, sems.at[KINDS]))
    loads[-1].start()
    for n in (0, 1, -1):
        loads[n].wait()
    table = [few[0, m] for m in range(spread.shape[0])]
    for m, eps in enumerate(table):
        spread[m] = jnp.full(spread.shape[1:], eps, jnp.float32)

    def fill(x, _):
        values = coefficients(whole[0, x].astype(jnp.float32), whole[1, x].astype(jnp.float32),
                              table, None)
        for plane, value in zip((ca, cb, da, db), values):
            plane[HALO + x, 0:cells, :] = value
        return 0

    lax.fori_loop(0, cells, fill, 0, unroll=4)
    for load in loads[2:-1]:
        load.wait()

    def strips(to_a, to_b):
        for k in range(KINDS):
            for out, ys in ((ya, to_a), (yb, to_b)):
                strip = (whole[k - 12, :, ys, :].astype(jnp.float32) if k >= 12
                         else field[k, own, ys, :])
                out[k * cells:(k + 1) * cells] = strip

    @pl.when(is_even(col))
    def _():
        strips(slice(12, 16), slice(0, 4))

    @pl.when(jnp.logical_not(is_even(col)))
    def _():
        strips(slice(0, 4), slice(12, 16))


def load(cols, eps_table, fields, kind, depth, after):
    cells = kind.shape[0]
    wide = cells + 2 * HALO
    plane = jax.ShapeDtypeStruct((wide, wide, 128), jnp.float32)
    return pl.pallas_call(
        functools.partial(load_kernel, cols),
        out_shape=(jax.ShapeDtypeStruct((12, wide, wide, 128), jnp.float32),
                   plane, plane, plane, plane,
                   jax.ShapeDtypeStruct((KINDS * cells + 2 * LAYERS, 4, 128), jnp.float32),
                   jax.ShapeDtypeStruct((KINDS * cells, 4, 128), jnp.float32),
                   jax.ShapeDtypeStruct((eps_table.shape[1], 8, 128), jnp.float32)),
        in_specs=[HBM] * 7 + [ANY],
        out_specs=[VMEM] * 8,
        scratch_shapes=[
            pltpu.VMEM((2, cells, cells, 128), jnp.int32),
            pltpu.SMEM(eps_table.shape, jnp.float32),
            pltpu.SemaphoreType.DMA((KINDS + 1,)),
        ],
        compiler_params=pltpu.CompilerParams(vmem_limit_bytes=16 * 2**20),
        cost_estimate=pl.CostEstimate(flops=LOAD_FLOPS, bytes_accessed=2**22, transcendentals=0),
        name="load",
    )(*in_hbm((eps_table, *fields, kind, depth)), after)


def corner_kernel(cols, ra, rb, ya_in, cb, ya):
    _, col = tile_place(cols)
    strips = ya.shape[0] - 2 * LAYERS

    def put(to_a, to_b):
        for n, source in enumerate((ra, rb)):
            cb[n * LAYERS:(n + 1) * LAYERS] = source[:, to_b, :]
            ya[strips + n * LAYERS:strips + (n + 1) * LAYERS] = source[:, to_a, :]

    @pl.when(is_even(col))
    def _():
        put(slice(12, 16), slice(0, 4))

    @pl.when(jnp.logical_not(is_even(col)))
    def _():
        put(slice(0, 4), slice(12, 16))


def corners(cols, ra, rb, ya):
    return pl.pallas_call(
        functools.partial(corner_kernel, cols),
        out_shape=(jax.ShapeDtypeStruct((2 * LAYERS, 4, 128), jnp.float32),
                   jax.ShapeDtypeStruct(ya.shape, jnp.float32)),
        in_specs=[VMEM] * 3,
        out_specs=[VMEM] * 2,
        input_output_aliases={2: 1},
        compiler_params=pltpu.CompilerParams(vmem_limit_bytes=16 * 2**20),
        cost_estimate=pl.CostEstimate(flops=CORNER_FLOPS, bytes_accessed=2**20, transcendentals=0),
        name="corners",
    )(ra, rb, ya)


def coefficients(m, d, table, outside):
    eps = jnp.where(m < 0.5, table[0],
                    jnp.where(m < 1.5, table[1], jnp.where(m < 2.5, table[2], table[3])))
    ramp = d / depth_scale
    sigma = ramp * ramp
    s_e = sigma * dt_step / (2.0 * eps)
    s_h = sigma * dt_step / 2.0
    values = ((1.0 - s_e) / (1.0 + s_e), dt_step / (eps * (1.0 + s_e)),
              (1.0 - s_h) / (1.0 + s_h), dt_step / (1.0 + s_h))
    if outside is None:
        return values
    return (values[0], jnp.where(outside, 0.0, values[1]),
            values[2], jnp.where(outside, 0.0, values[3]))


def spread_table(spread):
    return [spread[m, 0:1, :] for m in range(spread.shape[0])]


def outside_rows(x, cells, row, rows):
    return jnp.logical_or(jnp.logical_and(x < HALO, row == 0),
                          jnp.logical_and(x >= HALO + cells, row == rows - 1))


def halo_places(row, cells):
    even = is_even(row)
    after, before = HALO + cells, 0
    deep = jnp.where(even, after, before), jnp.where(even, before, after)
    shallow = jnp.where(even, after, before + 1), jnp.where(even, before + 1, after)
    return deep, shallow


def prepare_kernel(cols, rows, spread, field_in, ca_in, cb_in, da_in, db_in, ra, rb,
                   field, ca, cb, da, db, matter):
    row, _ = tile_place(cols)
    cells = ra.shape[1]
    table = spread_table(spread)
    deep, shallow = halo_places(row, cells)
    for k, place, count in layer_places():
        for side, layers in enumerate((ra, rb)):
            here = pl.ds((deep if count == HALO else shallow)[side], count)
            to = field.at[k] if k < 12 else matter.at[k - 12]
            to[here, 0:cells, :] = layers[place:place + count]

    def fill(n, _):
        x = jnp.where(n < HALO, n, n + cells)
        values = coefficients(matter[0, x], matter[1, x], table,
                              outside_rows(x, cells, row, rows))
        for plane, value in zip((ca, cb, da, db), values):
            plane[x, 0:cells, :] = value
        return 0

    lax.fori_loop(0, 2 * HALO, fill, 0, unroll=4)


def prepare(cols, rows, spread, state, ra, rb):
    cells = ra.shape[1]
    wide = cells + 2 * HALO
    return pl.pallas_call(
        functools.partial(prepare_kernel, cols, rows),
        out_shape=tuple(jax.ShapeDtypeStruct(part.shape, part.dtype) for part in state),
        in_specs=[VMEM] * 8,
        out_specs=[VMEM] * 5,
        scratch_shapes=[pltpu.VMEM((2, wide, cells, 128), jnp.float32)],
        input_output_aliases={n + 1: n for n in range(5)},
        compiler_params=pltpu.CompilerParams(vmem_limit_bytes=16 * 2**20),
        cost_estimate=pl.CostEstimate(flops=PREPARE_FLOPS, bytes_accessed=2**22, transcendentals=0),
        name="prepare",
    )(spread, *state, ra, rb)


def steps_kernel(cols, rows, first_z, spread, field_in, ca_in, cb_in, da_in, db_in, ryb, rcb, rya,
                 ef_out, hf_out, ea_out, ha_out, send, field, ca, cb, da, db, total, matter):
    start = first_z[0]
    table = spread_table(spread)
    row, col = tile_place(cols)
    wide = ca.shape[0]
    cells = wide - 2 * HALO
    own = slice(HALO, HALO + cells)
    deep, shallow = halo_places(row, cells)

    def columns(first_a, first_b):
        for k in range(KINDS):
            to, base = (field.at[k], cells) if k < 12 else (matter.at[k - 12], 0)
            to[own, base + first_a:base + first_a + 4, :] = rya[k * cells:(k + 1) * cells]
            to[own, base + first_b:base + first_b + 4, :] = ryb[k * cells:(k + 1) * cells]
        for k, place, count in layer_places():
            to, base = (field.at[k], cells) if k < 12 else (matter.at[k - 12], 0)
            for side in range(2):
                here = pl.ds((deep if count == HALO else shallow)[side], count)
                at = side * LAYERS + place
                to[here, base + first_a:base + first_a + 4, :] = (
                    rya[KINDS * cells + at:KINDS * cells + at + count])
                to[here, base + first_b:base + first_b + 4, :] = rcb[at:at + count]

    @pl.when(is_even(col))
    def _():
        columns(0, 4)

    @pl.when(jnp.logical_not(is_even(col)))
    def _():
        columns(4, 0)

    after = low_half((8, 128))
    outside_y = jnp.logical_or(jnp.logical_and(after, col == cols - 1),
                               jnp.logical_and(jnp.logical_not(after), col == 0))

    def fill(x, _):
        outside = jnp.logical_or(outside_y, outside_rows(x, cells, row, rows))
        values = coefficients(matter[0, x], matter[1, x], table, outside)
        for plane, value in zip((ca, cb, da, db), values):
            plane[x, cells:wide, :] = value
        return 0

    lax.fori_loop(0, wide, fill, 0, unroll=4)

    lane = lax.broadcasted_iota(jnp.int32, (wide, 128), 1)
    top_z, bottom_z = lane == 127, lane == 0

    def up_z(v):
        return jnp.where(top_z, 0.0, pltpu.roll(v, 127, 1))

    def down_z(v):
        return jnp.where(bottom_z, 0.0, pltpu.roll(v, 1, 1))

    def up_y(v):
        return pltpu.roll(v, wide - 1, 0)

    def down_y(v):
        return pltpu.roll(v, 1, 0)

    parts = ((0, 3), (6, 9))
    outs = {0: ef_out, 3: hf_out, 6: ea_out, 9: ha_out}

    def h_new(e, h, x):
        dax, dbx = da[x], db[x]
        ex, ey, ez = field[e, x], field[e + 1, x], field[e + 2, x]
        ey1, ez1 = field[e + 1, x + 1], field[e + 2, x + 1]
        return (dax * field[h, x] - dbx * ((up_y(ez) - ez) - (up_z(ey) - ey)),
                dax * field[h + 1, x] - dbx * ((up_z(ex) - ex) - (ez1 - ez)),
                dax * field[h + 2, x] - dbx * ((ey1 - ey) - (up_y(ex) - ex)))

    def e_new(e, h, x):
        cax, cbx = ca[x], cb[x]
        hx, hy, hz = field[h, x], field[h + 1, x], field[h + 2, x]
        hy1, hz1 = field[h + 1, x - 1], field[h + 2, x - 1]
        return (cax * field[e, x] + cbx * ((hz - down_y(hz)) - (hy - down_z(hy))),
                cax * field[e + 1, x] + cbx * ((hx - down_z(hx)) - (hz - hz1)),
                cax * field[e + 2, x] + cbx * ((hy - hy1) - (hx - down_y(hx))))

    def put(k, x, new, last):
        for n in range(3):
            if last:
                outs[k][n, x - HALO] = new[n][0:cells]
            if not last or (k in (3, 9)):
                field[k + n, x] = new[n]

    def h_rows(x0, count, last):
        news = [[h_new(e, h, x0 + u) for u in range(count)] for e, h in parts]
        for (_, h), new in zip(parts, news):
            for u in range(count):
                put(h, x0 + u, new[u], last)

    def e_rows(step, x0, count, ahead):
        last = step == STEPS - 1
        news = []
        for e, h in parts:
            es = [e_new(e, h, x0 + u) for u in range(count)]
            hs = [h_new(e, h, x0 + count + u) for u in range(count)] if ahead else []
            for u in range(count):
                put(e, x0 + u, es[u], last)
            for u in range(len(hs)):
                put(h, x0 + count + u, hs[u], last)
            news.append(es)
        for u in range(count):
            term = sum(news[0][u][n][0:cells] * news[1][u][n][0:cells] for n in range(3))
            total[x0 + u] = term if step == 0 else total[x0 + u] + term

    for step in range(STEPS):
        last = step == STEPS - 1
        pairs = (wide - 2 - 2 * step) // 2
        h_rows(step, 1, False)
        h_rows(step + 1, 2, last)

        def two_rows(i, _):
            e_rows(step, step + 1 + 2 * i, 2, True)
            return 0

        lax.fori_loop(0, pairs - 1, two_rows, 0, unroll=UNROLL)
        e_rows(step, step + 1 + 2 * (pairs - 1), 2, False)

    sub = lax.broadcasted_iota(jnp.int32, (8, 128), 0)
    mine = lax.broadcasted_iota(jnp.int32, (8, 128), 1) // DZ == sub
    for tile in range(cells * 2 // 8):
        block = jnp.zeros((8, 128), jnp.float32)
        for n in range(8):
            x, half = HALO + (tile * 8 + n) // 2, (tile * 8 + n) % 2
            moved = pltpu.roll(total[x, 8 * half:8 * half + 8, :], 128 - start, 1)
            line = jnp.sum(jnp.where(mine, staggered(moved, DZ), 0.0), axis=0, keepdims=True)
            block = jnp.where(sub == n, line, block)
        for peer in range(send.shape[0]):
            send[peer, tile * 8:tile * 8 + 8, :] = block


def all_steps(cols, rows, waves, first_z, spread, state, halos):
    wide = state[0].shape[1]
    cells = wide - 2 * HALO
    out = pltpu.VMEM((3, cells, cells, 128), jnp.float32)
    plane = jax.ShapeDtypeStruct((wide, wide, 128), jnp.float32)
    return pl.pallas_call(
        functools.partial(steps_kernel, cols, rows),
        out_shape=(out, out, out, out,
                   jax.ShapeDtypeStruct((waves, cells * 2, 128), jnp.float32),
                   jax.ShapeDtypeStruct((12, wide, wide, 128), jnp.float32),
                   plane, plane, plane, plane),
        in_specs=[SMEM] + [VMEM] * 9,
        out_specs=[VMEM] * 10,
        scratch_shapes=[
            pltpu.VMEM((wide, cells, 128), jnp.float32),
            pltpu.VMEM((2, wide, 8, 128), jnp.float32),
        ],
        input_output_aliases={2: 5, 3: 6, 4: 7, 5: 8, 6: 9},
        compiler_params=pltpu.CompilerParams(vmem_limit_bytes=16 * 2**20),
        name="steps",
    )(first_z, spread, *state, *halos)[:5]


def gradient_kernel(parts, out):
    waves, lines, _ = parts.shape
    whole = parts[0]
    for wave in range(1, waves):
        whole = whole + parts[wave]
    for n in range(lines):
        spread = jnp.broadcast_to(whole[n:n + 1, :], (8, 128))
        moved = staggered(spread, 128 - DZ)
        out[n // 2, 8 * (n % 2):8 * (n % 2) + 8, :] = moved[:, 0:DZ]


def gradient_of(parts):
    cells = parts.shape[1] // 2
    return pl.pallas_call(
        gradient_kernel,
        out_shape=jax.ShapeDtypeStruct((cells, cells, DZ), jnp.float32),
        in_specs=[VMEM],
        out_specs=VMEM,
        compiler_params=pltpu.CompilerParams(vmem_limit_bytes=8 * 2**20),
        name="gradient",
    )(parts)


def per_device(
    e_forward, h_forward, e_adjoint, h_adjoint, eps_table, material, pml_depth, design_start
):
    cols = TILE_COLS
    count = lax.axis_size("tile")
    rows = count // cols
    fields = (e_forward[0], h_forward[0], e_adjoint[0], h_adjoint[0])

    def swap(value, along_x, odd):
        return lax.ppermute(value, "tile", swap_pairs(count, cols, along_x, odd))

    xa, xb = edges(cols, fields, material, pml_depth)
    ra = swap(xa, True, 0)
    rb = swap(xb, True, 1)
    *state, ya, yb, spread = load(cols, eps_table, fields, material, pml_depth, xa)
    ryb = swap(yb, False, 1)
    cb, ya = corners(cols, ra, rb, ya)
    rcb = swap(cb, False, 1)
    rya = swap(ya, False, 0)
    state = prepare(cols, rows, spread, state, ra, rb)
    *outs, send = all_steps(cols, rows, lax.axis_size("wave"), design_start, spread, state,
                            (ryb, rcb, rya))
    parts = lax.all_to_all(send, "wave", 0, 0)
    gradient = gradient_of(parts)
    return tuple(out[None] for out in outs) + (gradient,)


def solution(mesh):
    return jax.shard_map(
        per_device,
        mesh=mesh,
        in_specs=(
            P("wave", None, "tile", None, None),
            P("wave", None, "tile", None, None),
            P("wave", None, "tile", None, None),
            P("wave", None, "tile", None, None),
            P("wave", None),
            P("tile", None, None),
            P("tile", None, None),
            P("tile"),
        ),
        out_specs=(
            P("wave", None, "tile", None, None),
            P("wave", None, "tile", None, None),
            P("wave", None, "tile", None, None),
            P("wave", None, "tile", None, None),
            P("tile", None, None),
        ),
        check_vma=False,
    )
```

time: 60.9 us -> 55.7 us (0.915)
  the two profiles are of different devices: /device:TPU:72 before, /device:TPU:136 now
where the time goes in v3:
time: 55.7 us; the launch traced here: 55.3 us
  starting transfers between devices  25.8 us (46%)
  waiting for transfers between devices  15 us (27%)
  Pallas kernels  10.1 us (18%)
  local copies, waits for them, and re-layouts  2.98 us (5%)
  between operations  1.37 us (2%)
    ppermute x5, starting transfers between devices, swap(): return lax.ppermute(value, 'tile', swap_pairs(count, cols, along_x, odd))  17.2 us
    all_to_all x1, starting transfers between devices, per_device(): parts = lax.all_to_all(send, 'wave', 0, 0)  8.62 us
    all_to_all x1, waiting for transfers between devices, per_device(): parts = lax.all_to_all(send, 'wave', 0, 0)  8.15 us
    ppermute x5, waiting for transfers between devices, swap(): return lax.ppermute(value, 'tile', swap_pairs(count, cols, along_x, odd))  6.84 us
    pallas_call x1, Pallas kernels, all_steps(): pl.pallas_call(functools.partial(steps_kernel, cols, rows), out_shape=(ou...  5.81 us
    unnamed x4, local copies, waits for them, and re-layouts  2.98 us
    pallas_call x1, Pallas kernels, load(): pl.pallas_call(functools.partial(load_kernel, cols), out_shape=(jax.Shape...  1.82 us
    pallas_call x1, Pallas kernels, edges(): pl.pallas_call(functools.partial(edges_kernel, cols), out_shape=(layers,...  1.36 us
  transfers between devices with their start and end apart: 6, of which 3 were waited for; matrix products, arithmetic and copies ran while one was open for 5% of the time, Pallas kernels for 4%

profile of v3, /device:TPU:136, one launch (start us, length us, event | category | flops | bytes accessed | tf_op | source)
XLA Modules:
  0.0 55.3 jit_solution(5165377156306518150)
XLA Ops:
  0.6 1.4 %edges.1 = (f32[53,16,128]{2,1,0:T(8,128)S(1)}, f32[53,16,128]{2,1,0:T(8,128)S(1)}) custom-call(f32[3,16,16,128]{3,2,1,0:T(8,128)} %bitcast.12, f32[3,16,16,128]{3,2,1,0:T(8,128)} %bitcast.14, f32[3,16,16,128]{3,2,1,0:T(8,128)} %bitcast.16, f32[3,16,16,128]{3,2,1,0:T(8,128)} %bitcast.18, s32[16,16,128]{2,1,0:T(8,128)} %kind.3, s32[16,16,128]{2,1,0:T(8,128)} %depth.3), custom_call_target="tpu_custom_call" | custom-call | flops 1048576 | bytes 1048576 | tf_op jit(solution)/shard_map/edges/pallas_call | solution.py:103
  2.0 1.9 %collective-permute-start.1 = (f32[53,16,128]{2,1,0:T(8,128)S(1)}, f32[53,16,128]{2,1,0:T(8,128)S(1)}, u32[]{:S(2)}, u32[]{:S(2)}) collective-permute-start(f32[53,16,128]{2,1,0:T(8,128)S(1)} %get-tuple-element.34), channel_id=1, source_target_pairs={{8,16},{9,17},{10,18},{11,19},{12,20},{13,21},{14,22},{15,23},{16,... | collective-permute-start | bytes 1302536 | tf_op jit(solution)/shard_map/ppermute | solution.py:479
  3.9 7.9 %collective-permute-start = (f32[53,16,128]{2,1,0:T(8,128)S(1)}, f32[53,16,128]{2,1,0:T(8,128)S(1)}, u32[]{:S(2)}, u32[]{:S(2)}) collective-permute-start(f32[53,16,128]{2,1,0:T(8,128)S(1)} %get-tuple-element.27.after), channel_id=1, source_target_pairs={{0,8},{1,9},{2,10},{3,11},{4,12},{5,13},{6,14},{7,15},{8,0},{9,1},... | collective-permute-start | bytes 1302536 | tf_op jit(solution)/shard_map/ppermute | solution.py:479
  11.8 1.8 %load.1 = (f32[12,24,24,128]{3,2,1,0:T(8,128)S(1)}, f32[24,24,128]{2,1,0:T(8,128)S(1)}, f32[24,24,128]{2,1,0:T(8,128)S(1)}, f32[24,24,128]{2,1,0:T(8,128)S(1)}, ...) custom-call(f32[1,4]{1,0:T(1,128)} %eps_table.1, ...), custom_call_target="tpu_custom_call" | custom-call | flops 1073741824 | bytes 4194304 | tf_op jit(solution)/shard_map/load/pallas_call | solution.py:168
  13.6 1.9 %collective-permute-start.2 = (f32[224,4,128]{2,1,0:T(4,128)S(1)}, f32[224,4,128]{2,1,0:T(4,128)S(1)}, u32[]{:S(2)}, u32[]{:S(2)}) collective-permute-start(f32[224,4,128]{2,1,0:T(4,128)S(1)} %get-tuple-element.40), channel_id=1, source_target_pairs={{1,2},{2,1},{3,4},{4,3},{5,6},{6,5},{9,10},{10,9},{11,12},{12,11},... | collective-permute-start | bytes 1376264 | tf_op jit(solution)/shard_map/ppermute | solution.py:479
  16.2 0.0 collective-permute-done.1.rb
  16.2 5.3 %collective-permute-done.ra = f32[53,16,128]{2,1,0:T(8,128)S(1)} collective-permute-done((f32[53,16,128]{2,1,0:T(8,128)S(1)}, f32[53,16,128]{2,1,0:T(8,128)S(1)}, u32[]{:S(2)}, u32[]{:S(2)}) %collective-permute-start) | collective-permute-done | bytes 434208 | tf_op jit(solution)/shard_map/ppermute | solution.py:479
  21.5 0.1 corners.1
  21.6 1.9 %collective-permute-start.3 = (f32[106,4,128]{2,1,0:T(4,128)S(1)}, f32[106,4,128]{2,1,0:T(4,128)S(1)}, u32[]{:S(2)}, u32[]{:S(2)}) collective-permute-start(f32[106,4,128]{2,1,0:T(4,128)S(1)} %get-tuple-element.42), channel_id=1, source_target_pairs={{1,2},{2,1},{3,4},{4,3},{5,6},{6,5},{9,10},{10,9},{11,12},{12,11},... | collective-permute-start | bytes 651272 | tf_op jit(solution)/shard_map/ppermute | solution.py:479
  23.5 3.6 %collective-permute-start.4 = (f32[330,4,128]{2,1,0:T(4,128)S(1)}, f32[330,4,128]{2,1,0:T(4,128)S(1)}, u32[]{:S(2)}, u32[]{:S(2)}) collective-permute-start(f32[330,4,128]{2,1,0:T(4,128)S(1)} %get-tuple-element.43), channel_id=1, source_target_pairs={{0,1},{1,0},{2,3},{3,2},{4,5},{5,4},{6,7},{7,6},{8,9},{9,8},{10,11... | collective-permute-start | bytes 2027528 | tf_op jit(solution)/shard_map/ppermute | solution.py:479
  27.1 0.2 prepare.1
  27.3 0.0 collective-permute-done.2.ryb
  27.3 1.5 %collective-permute-done.3.rcb = f32[106,4,128]{2,1,0:T(4,128)S(1)} collective-permute-done((f32[106,4,128]{2,1,0:T(4,128)S(1)}, f32[106,4,128]{2,1,0:T(4,128)S(1)}, u32[]{:S(2)}, u32[]{:S(2)}) %collective-permute-start.3) | collective-permute-done | bytes 217120 | tf_op jit(solution)/shard_map/ppermute | solution.py:479
  28.8 0.0 collective-permute-done.4.rya
  28.8 5.8 %steps.1 = (f32[3,16,16,128]{3,2,1,0:T(8,128)S(1)}, f32[3,16,16,128]{3,2,1,0:T(8,128)S(1)}, f32[3,16,16,128]{3,2,1,0:T(8,128)S(1)}, f32[3,16,16,128]{3,2,1,0:T(8...) custom-call(s32[1]{0:T(128)S(6)} %copy.39.first_z, ...), custom_call_target="tpu_custom_call", output_to_operand_aliasing={{5}: (2, {}), {6}: (3, {}), {7}: (4, {}), {8}: (5, {}), {9}... | custom-call | tf_op jit(solution)/shard_map/steps/pallas_call | solution.py:429
  34.6 8.6 %all-to-all-start = ((f32[8,32,128]{2,1,0:T(8,128)}), f32[8,32,128]{2,1,0:T(8,128)S(1)}, u32[]{:S(2)}, u32[]{:S(2)}) async-start(f32[8,32,128]{2,1,0:T(8,128)} %get-tuple-element.48), calls=%async_computation | async-start | bytes 262144 | tf_op jit(solution)/shard_map/all_to_all | solution.py:492
  43.3 0.7 %copy.35 = f32[1,3,16,16,128]{4,3,2,1,0:T(8,128)} copy(f32[1,3,16,16,128]{4,3,2,1,0:T(8,128)S(1)} %bitcast.11) | data formatting | bytes 786432
  44.0 0.7 %copy.36 = f32[1,3,16,16,128]{4,3,2,1,0:T(8,128)} copy(f32[1,3,16,16,128]{4,3,2,1,0:T(8,128)S(1)} %bitcast.10) | data formatting | bytes 786432
  44.7 0.7 %copy.37 = f32[1,3,16,16,128]{4,3,2,1,0:T(8,128)} copy(f32[1,3,16,16,128]{4,3,2,1,0:T(8,128)S(1)} %bitcast.9) | data formatting | bytes 786432
  45.5 0.7 %copy.38 = f32[1,3,16,16,128]{4,3,2,1,0:T(8,128)} copy(f32[1,3,16,16,128]{4,3,2,1,0:T(8,128)S(1)} %bitcast.8) | data formatting | bytes 786432
  46.2 8.1 %all-to-all-done.parts = f32[8,32,128]{2,1,0:T(8,128)S(1)} async-done(((f32[8,32,128]{2,1,0:T(8,128)}), f32[8,32,128]{2,1,0:T(8,128)S(1)}, u32[]{:S(2)}, u32[]{:S(2)}) %all-to-all-start) | async-done | bytes 131104 | tf_op jit(solution)/shard_map/all_to_all | solution.py:492
  54.4 0.9 %gradient.1 = f32[16,16,16]{2,1,0:T(8,128)} custom-call(f32[8,32,128]{2,1,0:T(8,128)S(1)} %all-to-all-done.parts), custom_call_target="tpu_custom_call" | custom-call | tf_op jit(solution)/shard_map/gradient/pallas_call | solution.py:460
Async XLA Ops:
  2.0 14.2 %collective-permute-start.1 = (f32[53,16,128]{2,1,0:T(8,128)S(1)}, f32[53,16,128]{2,1,0:T(8,128)S(1)}, u32[]{:S(2)}, u32[]{:S(2)}) collective-permute-start(f32[53,16,128]{2,1,0:T(8,128)S(1)} %get-tuple-element.34), channel_id=1, source_target_pairs={{8,16},{9,17},{10,18},{11,19},{12,20},{13,21},{14,22},{15,23},{16,... | collective-permute-start | bytes 1302536 | tf_op jit(solution)/shard_map/ppermute | solution.py:479
  3.9 17.6 %collective-permute-start = (f32[53,16,128]{2,1,0:T(8,128)S(1)}, f32[53,16,128]{2,1,0:T(8,128)S(1)}, u32[]{:S(2)}, u32[]{:S(2)}) collective-permute-start(f32[53,16,128]{2,1,0:T(8,128)S(1)} %get-tuple-element.27.after), channel_id=1, source_target_pairs={{0,8},{1,9},{2,10},{3,11},{4,12},{5,13},{6,14},{7,15},{8,0},{9,1},... | collective-permute-start | bytes 1302536 | tf_op jit(solution)/shard_map/ppermute | solution.py:479
  13.6 13.7 %collective-permute-start.2 = (f32[224,4,128]{2,1,0:T(4,128)S(1)}, f32[224,4,128]{2,1,0:T(4,128)S(1)}, u32[]{:S(2)}, u32[]{:S(2)}) collective-permute-start(f32[224,4,128]{2,1,0:T(4,128)S(1)} %get-tuple-element.40), channel_id=1, source_target_pairs={{1,2},{2,1},{3,4},{4,3},{5,6},{6,5},{9,10},{10,9},{11,12},{12,11},... | collective-permute-start | bytes 1376264 | tf_op jit(solution)/shard_map/ppermute | solution.py:479
  21.6 7.2 %collective-permute-start.3 = (f32[106,4,128]{2,1,0:T(4,128)S(1)}, f32[106,4,128]{2,1,0:T(4,128)S(1)}, u32[]{:S(2)}, u32[]{:S(2)}) collective-permute-start(f32[106,4,128]{2,1,0:T(4,128)S(1)} %get-tuple-element.42), channel_id=1, source_target_pairs={{1,2},{2,1},{3,4},{4,3},{5,6},{6,5},{9,10},{10,9},{11,12},{12,11},... | collective-permute-start | bytes 651272 | tf_op jit(solution)/shard_map/ppermute | solution.py:479
  23.5 5.3 %collective-permute-start.4 = (f32[330,4,128]{2,1,0:T(4,128)S(1)}, f32[330,4,128]{2,1,0:T(4,128)S(1)}, u32[]{:S(2)}, u32[]{:S(2)}) collective-permute-start(f32[330,4,128]{2,1,0:T(4,128)S(1)} %get-tuple-element.43), channel_id=1, source_target_pairs={{0,1},{1,0},{2,3},{3,2},{4,5},{5,4},{6,7},{7,6},{8,9},{9,8},{10,11... | collective-permute-start | bytes 2027528 | tf_op jit(solution)/shard_map/ppermute | solution.py:479
  34.6 19.8 %all-to-all-start = ((f32[8,32,128]{2,1,0:T(8,128)}), f32[8,32,128]{2,1,0:T(8,128)S(1)}, u32[]{:S(2)}, u32[]{:S(2)}) async-start(f32[8,32,128]{2,1,0:T(8,128)} %get-tuple-element.48), calls=%async_computation | async-start | bytes 262144 | tf_op jit(solution)/shard_map/all_to_all | solution.py:492

commit v4 on v3

--- a/solution.py
+++ b/solution.py
@@ -169,7 +169,7 @@
         functools.partial(load_kernel, cols),
         out_shape=(jax.ShapeDtypeStruct((12, wide, wide, 128), jnp.float32),
                    plane, plane, plane, plane,
-                   jax.ShapeDtypeStruct((KINDS * cells + 2 * LAYERS, 4, 128), jnp.float32),
+                   jax.ShapeDtypeStruct((KINDS * cells, 4, 128), jnp.float32),
                    jax.ShapeDtypeStruct((KINDS * cells, 4, 128), jnp.float32),
                    jax.ShapeDtypeStruct((eps_table.shape[1], 8, 128), jnp.float32)),
         in_specs=[HBM] * 7 + [ANY],
@@ -185,14 +185,13 @@
     )(*in_hbm((eps_table, *fields, kind, depth)), after)
 
 
-def corner_kernel(cols, ra, rb, ya_in, cb, ya):
+def corner_kernel(cols, ra, rb, ca, cb):
     _, col = tile_place(cols)
-    strips = ya.shape[0] - 2 * LAYERS
 
     def put(to_a, to_b):
         for n, source in enumerate((ra, rb)):
             cb[n * LAYERS:(n + 1) * LAYERS] = source[:, to_b, :]
-            ya[strips + n * LAYERS:strips + (n + 1) * LAYERS] = source[:, to_a, :]
+            ca[n * LAYERS:(n + 1) * LAYERS] = source[:, to_a, :]
 
     @pl.when(is_even(col))
     def _():
@@ -203,18 +202,17 @@
         put(slice(0, 4), slice(12, 16))
 
 
-def corners(cols, ra, rb, ya):
+def corners(cols, ra, rb):
+    corner = jax.ShapeDtypeStruct((2 * LAYERS, HALO, 128), jnp.float32)
     return pl.pallas_call(
         functools.partial(corner_kernel, cols),
-        out_shape=(jax.ShapeDtypeStruct((2 * LAYERS, 4, 128), jnp.float32),
-                   jax.ShapeDtypeStruct(ya.shape, jnp.float32)),
-        in_specs=[VMEM] * 3,
+        out_shape=(corner, corner),
+        in_specs=[VMEM] * 2,
         out_specs=[VMEM] * 2,
-        input_output_aliases={2: 1},
         compiler_params=pltpu.CompilerParams(vmem_limit_bytes=16 * 2**20),
         cost_estimate=pl.CostEstimate(flops=CORNER_FLOPS, bytes_accessed=2**20, transcendentals=0),
         name="corners",
-    )(ra, rb, ya)
+    )(ra, rb)
 
 
 def coefficients(m, d, table, outside):
@@ -249,10 +247,53 @@
     return deep, shallow
 
 
-def prepare_kernel(cols, rows, spread, field_in, ca_in, cb_in, da_in, db_in, ra, rb,
-                   field, ca, cb, da, db, matter):
-    row, _ = tile_place(cols)
+def sides(col, put):
+    @pl.when(is_even(col))
+    def _():
+        put(0, HALO)
+
+    @pl.when(jnp.logical_not(is_even(col)))
+    def _():
+        put(HALO, 0)
+
+
+def fill_columns(cols, table, matter, planes, row_of, count, outside):
+    _, col = tile_place(cols)
+    cells = planes[0].shape[0] - 2 * HALO
+    after = low_half((8, 128))
+    outside_y = jnp.logical_or(jnp.logical_and(after, col == cols - 1),
+                               jnp.logical_and(jnp.logical_not(after), col == 0))
+
+    def fill(n, _):
+        x = row_of(n)
+        values = coefficients(matter[0, x], matter[1, x], table,
+                              jnp.logical_or(outside_y, outside(x)) if outside else outside_y)
+        for plane, value in zip(planes, values):
+            plane[x, cells:cells + 8, :] = value
+        return 0
+
+    lax.fori_loop(0, count, fill, 0, unroll=4)
+
+
+def rim_row(cells):
+    return lambda n: jnp.where(n < HALO, n, n + cells)
+
+
+def prepare_kernel(cols, rows, spread, field_in, ca_in, cb_in, da_in, db_in, ra, rb, ryb, rya,
+                   field, ca, cb, da, db, matter, strip):
+    row, col = tile_place(cols)
     cells = ra.shape[1]
+    own = slice(HALO, HALO + cells)
+
+    def columns(first_a, first_b):
+        for k in range(KINDS):
+            to, base = (field.at[k], cells) if k < 12 else (strip.at[k - 12], 0)
+            to[own, base + first_a:base + first_a + 4, :] = rya[k * cells:(k + 1) * cells]
+            to[own, base + first_b:base + first_b + 4, :] = ryb[k * cells:(k + 1) * cells]
+
+    sides(col, columns)
+    fill_columns(cols, spread_table(spread), strip, (ca, cb, da, db), lambda n: n + HALO, cells,
+                 None)
     table = spread_table(spread)
     deep, shallow = halo_places(row, cells)
     for k, place, count in layer_places():
@@ -262,7 +303,7 @@
             to[here, 0:cells, :] = layers[place:place + count]
 
     def fill(n, _):
-        x = jnp.where(n < HALO, n, n + cells)
+        x = rim_row(cells)(n)
         values = coefficients(matter[0, x], matter[1, x], table,
                               outside_rows(x, cells, row, rows))
         for plane, value in zip((ca, cb, da, db), values):
@@ -272,66 +313,44 @@
     lax.fori_loop(0, 2 * HALO, fill, 0, unroll=4)
 
 
-def prepare(cols, rows, spread, state, ra, rb):
+def prepare(cols, rows, spread, state, ra, rb, ryb, rya):
     cells = ra.shape[1]
     wide = cells + 2 * HALO
     return pl.pallas_call(
         functools.partial(prepare_kernel, cols, rows),
         out_shape=tuple(jax.ShapeDtypeStruct(part.shape, part.dtype) for part in state),
-        in_specs=[VMEM] * 8,
+        in_specs=[VMEM] * 10,
         out_specs=[VMEM] * 5,
-        scratch_shapes=[pltpu.VMEM((2, wide, cells, 128), jnp.float32)],
+        scratch_shapes=[pltpu.VMEM((2, wide, cells, 128), jnp.float32),
+                        pltpu.VMEM((2, wide, 8, 128), jnp.float32)],
         input_output_aliases={n + 1: n for n in range(5)},
         compiler_params=pltpu.CompilerParams(vmem_limit_bytes=16 * 2**20),
         cost_estimate=pl.CostEstimate(flops=PREPARE_FLOPS, bytes_accessed=2**22, transcendentals=0),
         name="prepare",
-    )(spread, *state, ra, rb)
-
-
-def steps_kernel(cols, rows, first_z, spread, field_in, ca_in, cb_in, da_in, db_in, ryb, rcb, rya,
+    )(spread, *state, ra, rb, ryb, rya)
+
+
+def steps_kernel(cols, rows, first_z, spread, field_in, ca_in, cb_in, da_in, db_in, rcb, rca,
                  ef_out, hf_out, ea_out, ha_out, send, field, ca, cb, da, db, total, matter):
     start = first_z[0]
     table = spread_table(spread)
     row, col = tile_place(cols)
     wide = ca.shape[0]
     cells = wide - 2 * HALO
-    own = slice(HALO, HALO + cells)
     deep, shallow = halo_places(row, cells)
 
     def columns(first_a, first_b):
-        for k in range(KINDS):
-            to, base = (field.at[k], cells) if k < 12 else (matter.at[k - 12], 0)
-            to[own, base + first_a:base + first_a + 4, :] = rya[k * cells:(k + 1) * cells]
-            to[own, base + first_b:base + first_b + 4, :] = ryb[k * cells:(k + 1) * cells]
         for k, place, count in layer_places():
             to, base = (field.at[k], cells) if k < 12 else (matter.at[k - 12], 0)
             for side in range(2):
                 here = pl.ds((deep if count == HALO else shallow)[side], count)
                 at = side * LAYERS + place
-                to[here, base + first_a:base + first_a + 4, :] = (
-                    rya[KINDS * cells + at:KINDS * cells + at + count])
+                to[here, base + first_a:base + first_a + 4, :] = rca[at:at + count]
                 to[here, base + first_b:base + first_b + 4, :] = rcb[at:at + count]
 
-    @pl.when(is_even(col))
-    def _():
-        columns(0, 4)
-
-    @pl.when(jnp.logical_not(is_even(col)))
-    def _():
-        columns(4, 0)
-
-    after = low_half((8, 128))
-    outside_y = jnp.logical_or(jnp.logical_and(after, col == cols - 1),
-                               jnp.logical_and(jnp.logical_not(after), col == 0))
-
-    def fill(x, _):
-        outside = jnp.logical_or(outside_y, outside_rows(x, cells, row, rows))
-        values = coefficients(matter[0, x], matter[1, x], table, outside)
-        for plane, value in zip((ca, cb, da, db), values):
-            plane[x, cells:wide, :] = value
-        return 0
-
-    lax.fori_loop(0, wide, fill, 0, unroll=4)
+    sides(col, columns)
+    fill_columns(cols, table, matter, (ca, cb, da, db), rim_row(cells), 2 * HALO,
+                 lambda x: outside_rows(x, cells, row, rows))
 
     lane = lax.broadcasted_iota(jnp.int32, (wide, 128), 1)
     top_z, bottom_z = lane == 127, lane == 0
@@ -432,7 +451,7 @@
                    jax.ShapeDtypeStruct((waves, cells * 2, 128), jnp.float32),
                    jax.ShapeDtypeStruct((12, wide, wide, 128), jnp.float32),
                    plane, plane, plane, plane),
-        in_specs=[SMEM] + [VMEM] * 9,
+        in_specs=[SMEM] + [VMEM] * 8,
         out_specs=[VMEM] * 10,
         scratch_shapes=[
             pltpu.VMEM((wide, cells, 128), jnp.float32),
@@ -483,12 +502,13 @@
     rb = swap(xb, True, 1)
     *state, ya, yb, spread = load(cols, eps_table, fields, material, pml_depth, xa)
     ryb = swap(yb, False, 1)
-    cb, ya = corners(cols, ra, rb, ya)
+    rya = swap(ya, False, 0)
+    ca, cb = corners(cols, ra, rb)
     rcb = swap(cb, False, 1)
-    rya = swap(ya, False, 0)
-    state = prepare(cols, rows, spread, state, ra, rb)
+    rca = swap(ca, False, 0)
+    state = prepare(cols, rows, spread, state, ra, rb, ryb, rya)
     *outs, send = all_steps(cols, rows, lax.axis_size("wave"), design_start, spread, state,
-                            (ryb, rcb, rya))
+                            (rcb, rca))
     parts = lax.all_to_all(send, "wave", 0, 0)
     gradient = gradient_of(parts)
     return tuple(out[None] for out in outs) + (gradient,)

time: 55.7 us -> 54.5 us (0.978)
  the two profiles are of different devices: /device:TPU:136 before, /device:TPU:200 now
where the time goes in v4:
time: 54.5 us; the launch traced here: 54 us
  starting transfers between devices  28.6 us (52%)
  waiting for transfers between devices  11.1 us (20%)
  Pallas kernels  10 us (18%)
  local copies, waits for them, and re-layouts  2.98 us (5%)
  between operations  1.39 us (3%)
    ppermute x6, starting transfers between devices, swap(): return lax.ppermute(value, 'tile', swap_pairs(count, cols, along_x, odd))  19.9 us
    all_to_all x1, starting transfers between devices, per_device(): parts = lax.all_to_all(send, 'wave', 0, 0)  8.66 us
    all_to_all x1, waiting for transfers between devices, per_device(): parts = lax.all_to_all(send, 'wave', 0, 0)  8.15 us
    pallas_call x1, Pallas kernels, all_steps(): pl.pallas_call(functools.partial(steps_kernel, cols, rows), out_shape=(ou...  5.43 us
    unnamed x4, local copies, waits for them, and re-layouts  2.98 us
    ppermute x6, waiting for transfers between devices, swap(): return lax.ppermute(value, 'tile', swap_pairs(count, cols, along_x, odd))  2.92 us
    pallas_call x1, Pallas kernels, load(): pl.pallas_call(functools.partial(load_kernel, cols), out_shape=(jax.Shape...  1.82 us
    pallas_call x1, Pallas kernels, edges(): pl.pallas_call(functools.partial(edges_kernel, cols), out_shape=(layers,...  1.36 us
  transfers between devices with their start and end apart: 7, of which 3 were waited for; matrix products, arithmetic and copies ran while one was open for 6% of the time, Pallas kernels for 4%

profile of v4, /device:TPU:200, one launch (start us, length us, event | category | flops | bytes accessed | tf_op | source)
XLA Modules:
  0.0 54.0 jit_solution(17169073064433387282)
XLA Ops:
  0.6 1.4 %edges.1 = (f32[53,16,128]{2,1,0:T(8,128)S(1)}, f32[53,16,128]{2,1,0:T(8,128)S(1)}) custom-call(f32[3,16,16,128]{3,2,1,0:T(8,128)} %bitcast.12, f32[3,16,16,128]{3,2,1,0:T(8,128)} %bitcast.14, f32[3,16,16,128]{3,2,1,0:T(8,128)} %bitcast.16, f32[3,16,16,128]{3,2,1,0:T(8,128)} %bitcast.18, s32[16,16,128]{2,1,0:T(8,128)} %kind.3, s32[16,16,128]{2,1,0:T(8,128)} %depth.3), custom_call_target="tpu_custom_call" | custom-call | flops 1048576 | bytes 1048576 | tf_op jit(solution)/shard_map/edges/pallas_call | solution.py:103
  2.0 1.9 %collective-permute-start = (f32[53,16,128]{2,1,0:T(8,128)S(1)}, f32[53,16,128]{2,1,0:T(8,128)S(1)}, u32[]{:S(2)}, u32[]{:S(2)}) collective-permute-start(f32[53,16,128]{2,1,0:T(8,128)S(1)} %get-tuple-element.27.after), channel_id=1, source_target_pairs={{0,8},{1,9},{2,10},{3,11},{4,12},{5,13},{6,14},{7,15},{8,0},{9,1},... | collective-permute-start | bytes 1302536 | tf_op jit(solution)/shard_map/ppermute | solution.py:498
  3.9 7.0 %collective-permute-start.1 = (f32[53,16,128]{2,1,0:T(8,128)S(1)}, f32[53,16,128]{2,1,0:T(8,128)S(1)}, u32[]{:S(2)}, u32[]{:S(2)}) collective-permute-start(f32[53,16,128]{2,1,0:T(8,128)S(1)} %get-tuple-element.34), channel_id=1, source_target_pairs={{8,16},{9,17},{10,18},{11,19},{12,20},{13,21},{14,22},{15,23},{16,... | collective-permute-start | bytes 1302536 | tf_op jit(solution)/shard_map/ppermute | solution.py:498
  10.9 1.8 %load.1 = (f32[12,24,24,128]{3,2,1,0:T(8,128)S(1)}, f32[24,24,128]{2,1,0:T(8,128)S(1)}, f32[24,24,128]{2,1,0:T(8,128)S(1)}, f32[24,24,128]{2,1,0:T(8,128)S(1)}, ...) custom-call(f32[1,4]{1,0:T(1,128)} %eps_table.1, ...), custom_call_target="tpu_custom_call" | custom-call | flops 1073741824 | bytes 4194304 | tf_op jit(solution)/shard_map/load/pallas_call | solution.py:168
  12.7 1.9 %collective-permute-start.2 = (f32[224,4,128]{2,1,0:T(4,128)S(1)}, f32[224,4,128]{2,1,0:T(4,128)S(1)}, u32[]{:S(2)}, u32[]{:S(2)}) collective-permute-start(f32[224,4,128]{2,1,0:T(4,128)S(1)} %get-tuple-element.35), channel_id=1, source_target_pairs={{1,2},{2,1},{3,4},{4,3},{5,6},{6,5},{9,10},{10,9},{11,12},{12,11},... | collective-permute-start | bytes 1376264 | tf_op jit(solution)/shard_map/ppermute | solution.py:498
  14.6 3.6 %collective-permute-start.3 = (f32[224,4,128]{2,1,0:T(4,128)S(1)}, f32[224,4,128]{2,1,0:T(4,128)S(1)}, u32[]{:S(2)}, u32[]{:S(2)}) collective-permute-start(f32[224,4,128]{2,1,0:T(4,128)S(1)} %get-tuple-element.36), channel_id=1, source_target_pairs={{0,1},{1,0},{2,3},{3,2},{4,5},{5,4},{6,7},{7,6},{8,9},{9,8},{10,11... | collective-permute-start | bytes 1376264 | tf_op jit(solution)/shard_map/ppermute | solution.py:498
  18.9 0.0 collective-permute-done.ra
  18.9 1.7 %collective-permute-done.1.rb = f32[53,16,128]{2,1,0:T(8,128)S(1)} collective-permute-done((f32[53,16,128]{2,1,0:T(8,128)S(1)}, f32[53,16,128]{2,1,0:T(8,128)S(1)}, u32[]{:S(2)}, u32[]{:S(2)}) %collective-permute-start.1) | collective-permute-done | bytes 434208 | tf_op jit(solution)/shard_map/ppermute | solution.py:498
  20.6 0.1 corners.1
  20.7 1.9 %collective-permute-start.4 = (f32[106,4,128]{2,1,0:T(4,128)S(1)}, f32[106,4,128]{2,1,0:T(4,128)S(1)}, u32[]{:S(2)}, u32[]{:S(2)}) collective-permute-start(f32[106,4,128]{2,1,0:T(4,128)S(1)} %get-tuple-element.42), channel_id=1, source_target_pairs={{1,2},{2,1},{3,4},{4,3},{5,6},{6,5},{9,10},{10,9},{11,12},{12,11},... | collective-permute-start | bytes 651272 | tf_op jit(solution)/shard_map/ppermute | solution.py:498
  22.6 3.6 %collective-permute-start.5 = (f32[106,4,128]{2,1,0:T(4,128)S(1)}, f32[106,4,128]{2,1,0:T(4,128)S(1)}, u32[]{:S(2)}, u32[]{:S(2)}) collective-permute-start(f32[106,4,128]{2,1,0:T(4,128)S(1)} %get-tuple-element.43), channel_id=1, source_target_pairs={{0,1},{1,0},{2,3},{3,2},{4,5},{5,4},{6,7},{7,6},{8,9},{9,8},{10,11... | collective-permute-start | bytes 651272 | tf_op jit(solution)/shard_map/ppermute | solution.py:498
  26.2 0.0 collective-permute-done.2.ryb
  26.2 0.0 collective-permute-done.3.rya
  26.2 0.4 prepare.1
  26.7 1.2 %collective-permute-done.4.rcb = f32[106,4,128]{2,1,0:T(4,128)S(1)} collective-permute-done((f32[106,4,128]{2,1,0:T(4,128)S(1)}, f32[106,4,128]{2,1,0:T(4,128)S(1)}, u32[]{:S(2)}, u32[]{:S(2)}) %collective-permute-start.4) | collective-permute-done | bytes 217120 | tf_op jit(solution)/shard_map/ppermute | solution.py:498
  27.9 0.0 collective-permute-done.5.rca
  27.9 5.4 %steps.1 = (f32[3,16,16,128]{3,2,1,0:T(8,128)S(1)}, f32[3,16,16,128]{3,2,1,0:T(8,128)S(1)}, f32[3,16,16,128]{3,2,1,0:T(8,128)S(1)}, f32[3,16,16,128]{3,2,1,0:T(8...) custom-call(s32[1]{0:T(128)S(6)} %copy.37.first_z, ...), custom_call_target="tpu_custom_call", output_to_operand_aliasing={{5}: (2, {}), {6}: (3, {}), {7}: (4, {}), {8}: (5, {}), {9}... | custom-call | tf_op jit(solution)/shard_map/steps/pallas_call | solution.py:448
  33.3 8.7 %all-to-all-start = ((f32[8,32,128]{2,1,0:T(8,128)}), f32[8,32,128]{2,1,0:T(8,128)S(1)}, u32[]{:S(2)}, u32[]{:S(2)}) async-start(f32[8,32,128]{2,1,0:T(8,128)} %get-tuple-element.48), calls=%async_computation | async-start | bytes 262144 | tf_op jit(solution)/shard_map/all_to_all | solution.py:512
  42.0 0.7 %copy.33 = f32[1,3,16,16,128]{4,3,2,1,0:T(8,128)} copy(f32[1,3,16,16,128]{4,3,2,1,0:T(8,128)S(1)} %bitcast.11) | data formatting | bytes 786432
  42.7 0.7 %copy.34 = f32[1,3,16,16,128]{4,3,2,1,0:T(8,128)} copy(f32[1,3,16,16,128]{4,3,2,1,0:T(8,128)S(1)} %bitcast.10) | data formatting | bytes 786432
  43.5 0.7 %copy.35 = f32[1,3,16,16,128]{4,3,2,1,0:T(8,128)} copy(f32[1,3,16,16,128]{4,3,2,1,0:T(8,128)S(1)} %bitcast.9) | data formatting | bytes 786432
  44.2 0.7 %copy.36 = f32[1,3,16,16,128]{4,3,2,1,0:T(8,128)} copy(f32[1,3,16,16,128]{4,3,2,1,0:T(8,128)S(1)} %bitcast.8) | data formatting | bytes 786432
  45.0 8.1 %all-to-all-done.parts = f32[8,32,128]{2,1,0:T(8,128)S(1)} async-done(((f32[8,32,128]{2,1,0:T(8,128)}), f32[8,32,128]{2,1,0:T(8,128)S(1)}, u32[]{:S(2)}, u32[]{:S(2)}) %all-to-all-start) | async-done | bytes 131104 | tf_op jit(solution)/shard_map/all_to_all | solution.py:512
  53.1 0.9 %gradient.1 = f32[16,16,16]{2,1,0:T(8,128)} custom-call(f32[8,32,128]{2,1,0:T(8,128)S(1)} %all-to-all-done.parts), custom_call_target="tpu_custom_call" | custom-call | tf_op jit(solution)/shard_map/gradient/pallas_call | solution.py:479
Async XLA Ops:
  2.0 16.9 %collective-permute-start = (f32[53,16,128]{2,1,0:T(8,128)S(1)}, f32[53,16,128]{2,1,0:T(8,128)S(1)}, u32[]{:S(2)}, u32[]{:S(2)}) collective-permute-start(f32[53,16,128]{2,1,0:T(8,128)S(1)} %get-tuple-element.27.after), channel_id=1, source_target_pairs={{0,8},{1,9},{2,10},{3,11},{4,12},{5,13},{6,14},{7,15},{8,0},{9,1},... | collective-permute-start | bytes 1302536 | tf_op jit(solution)/shard_map/ppermute | solution.py:498
  3.9 16.7 %collective-permute-start.1 = (f32[53,16,128]{2,1,0:T(8,128)S(1)}, f32[53,16,128]{2,1,0:T(8,128)S(1)}, u32[]{:S(2)}, u32[]{:S(2)}) collective-permute-start(f32[53,16,128]{2,1,0:T(8,128)S(1)} %get-tuple-element.34), channel_id=1, source_target_pairs={{8,16},{9,17},{10,18},{11,19},{12,20},{13,21},{14,22},{15,23},{16,... | collective-permute-start | bytes 1302536 | tf_op jit(solution)/shard_map/ppermute | solution.py:498
  12.7 13.5 %collective-permute-start.2 = (f32[224,4,128]{2,1,0:T(4,128)S(1)}, f32[224,4,128]{2,1,0:T(4,128)S(1)}, u32[]{:S(2)}, u32[]{:S(2)}) collective-permute-start(f32[224,4,128]{2,1,0:T(4,128)S(1)} %get-tuple-element.35), channel_id=1, source_target_pairs={{1,2},{2,1},{3,4},{4,3},{5,6},{6,5},{9,10},{10,9},{11,12},{12,11},... | collective-permute-start | bytes 1376264 | tf_op jit(solution)/shard_map/ppermute | solution.py:498
  14.6 11.6 %collective-permute-start.3 = (f32[224,4,128]{2,1,0:T(4,128)S(1)}, f32[224,4,128]{2,1,0:T(4,128)S(1)}, u32[]{:S(2)}, u32[]{:S(2)}) collective-permute-start(f32[224,4,128]{2,1,0:T(4,128)S(1)} %get-tuple-element.36), channel_id=1, source_target_pairs={{0,1},{1,0},{2,3},{3,2},{4,5},{5,4},{6,7},{7,6},{8,9},{9,8},{10,11... | collective-permute-start | bytes 1376264 | tf_op jit(solution)/shard_map/ppermute | solution.py:498
  20.7 7.2 %collective-permute-start.4 = (f32[106,4,128]{2,1,0:T(4,128)S(1)}, f32[106,4,128]{2,1,0:T(4,128)S(1)}, u32[]{:S(2)}, u32[]{:S(2)}) collective-permute-start(f32[106,4,128]{2,1,0:T(4,128)S(1)} %get-tuple-element.42), channel_id=1, source_target_pairs={{1,2},{2,1},{3,4},{4,3},{5,6},{6,5},{9,10},{10,9},{11,12},{12,11},... | collective-permute-start | bytes 651272 | tf_op jit(solution)/shard_map/ppermute | solution.py:498
  22.6 5.3 %collective-permute-start.5 = (f32[106,4,128]{2,1,0:T(4,128)S(1)}, f32[106,4,128]{2,1,0:T(4,128)S(1)}, u32[]{:S(2)}, u32[]{:S(2)}) collective-permute-start(f32[106,4,128]{2,1,0:T(4,128)S(1)} %get-tuple-element.43), channel_id=1, source_target_pairs={{0,1},{1,0},{2,3},{3,2},{4,5},{5,4},{6,7},{7,6},{8,9},{9,8},{10,11... | collective-permute-start | bytes 651272 | tf_op jit(solution)/shard_map/ppermute | solution.py:498
  33.3 19.8 %all-to-all-start = ((f32[8,32,128]{2,1,0:T(8,128)}), f32[8,32,128]{2,1,0:T(8,128)S(1)}, u32[]{:S(2)}, u32[]{:S(2)}) async-start(f32[8,32,128]{2,1,0:T(8,128)} %get-tuple-element.48), calls=%async_computation | async-start | bytes 262144 | tf_op jit(solution)/shard_map/all_to_all | solution.py:512

commit v5 on v4

--- a/solution.py
+++ b/solution.py
@@ -41,14 +41,6 @@
 
 def low_half(shape):
     return lax.broadcasted_iota(jnp.int32, shape, len(shape) - 2) < 4
-
-
-def staggered(block, by):
-    row = lax.broadcasted_iota(jnp.int32, block.shape, 0)
-    for bit in range(3):
-        moved = pltpu.roll(block, (by << bit) % 128, 1)
-        block = jnp.where((row >> bit) % 2 == 1, moved, block)
-    return block
 
 
 DEEP = (0, 1, 2, 4, 5, 6, 7, 8, 10, 11, 13)
@@ -359,7 +351,7 @@
         return jnp.where(top_z, 0.0, pltpu.roll(v, 127, 1))
 
     def down_z(v):
-        return jnp.where(bottom_z, 0.0, pltpu.roll(v, 1, 1))
+        return jnp.where(bottom_z[0:v.shape[0]], 0.0, pltpu.roll(v, 1, 1))
 
     def up_y(v):
         return pltpu.roll(v, wide - 1, 0)
@@ -378,13 +370,15 @@
                 dax * field[h + 1, x] - dbx * ((up_z(ex) - ex) - (ez1 - ez)),
                 dax * field[h + 2, x] - dbx * ((ey1 - ey) - (up_y(ex) - ex)))
 
-    def e_new(e, h, x):
-        cax, cbx = ca[x], cb[x]
-        hx, hy, hz = field[h, x], field[h + 1, x], field[h + 2, x]
-        hy1, hz1 = field[h + 1, x - 1], field[h + 2, x - 1]
-        return (cax * field[e, x] + cbx * ((hz - down_y(hz)) - (hy - down_z(hy))),
-                cax * field[e + 1, x] + cbx * ((hx - down_z(hx)) - (hz - hz1)),
-                cax * field[e + 2, x] + cbx * ((hy - hy1) - (hx - down_y(hx))))
+    def e_new(e, h, x, last):
+        ys = cells if last else wide
+        cax, cbx = ca[x, 0:ys], cb[x, 0:ys]
+        all_hx, hy, all_hz = field[h, x], field[h + 1, x, 0:ys], field[h + 2, x]
+        hx, hz = all_hx[0:ys], all_hz[0:ys]
+        hy1, hz1 = field[h + 1, x - 1, 0:ys], field[h + 2, x - 1, 0:ys]
+        return (cax * field[e, x, 0:ys] + cbx * ((hz - down_y(all_hz)[0:ys]) - (hy - down_z(hy))),
+                cax * field[e + 1, x, 0:ys] + cbx * ((hx - down_z(hx)) - (hz - hz1)),
+                cax * field[e + 2, x, 0:ys] + cbx * ((hy - hy1) - (hx - down_y(all_hx)[0:ys])))
 
     def put(k, x, new, last):
         for n in range(3):
@@ -403,7 +397,7 @@
         last = step == STEPS - 1
         news = []
         for e, h in parts:
-            es = [e_new(e, h, x0 + u) for u in range(count)]
+            es = [e_new(e, h, x0 + u, last) for u in range(count)]
             hs = [h_new(e, h, x0 + count + u) for u in range(count)] if ahead else []
             for u in range(count):
                 put(e, x0 + u, es[u], last)
@@ -427,17 +421,15 @@
         lax.fori_loop(0, pairs - 1, two_rows, 0, unroll=UNROLL)
         e_rows(step, step + 1 + 2 * (pairs - 1), 2, False)
 
-    sub = lax.broadcasted_iota(jnp.int32, (8, 128), 0)
-    mine = lax.broadcasted_iota(jnp.int32, (8, 128), 1) // DZ == sub
-    for tile in range(cells * 2 // 8):
-        block = jnp.zeros((8, 128), jnp.float32)
+    group = lax.broadcasted_iota(jnp.int32, (8, 128), 1) // DZ
+    for line in range(cells * 2 // 8):
+        packed = jnp.zeros((8, 128), jnp.float32)
         for n in range(8):
-            x, half = HALO + (tile * 8 + n) // 2, (tile * 8 + n) % 2
-            moved = pltpu.roll(total[x, 8 * half:8 * half + 8, :], 128 - start, 1)
-            line = jnp.sum(jnp.where(mine, staggered(moved, DZ), 0.0), axis=0, keepdims=True)
-            block = jnp.where(sub == n, line, block)
+            x, half = HALO + (8 * line + n) // 2, n % 2
+            moved = pltpu.roll(total[x, 8 * half:8 * half + 8, :], lax.rem(128 - start + DZ * n, 128), 1)
+            packed = jnp.where(group == n, moved, packed)
         for peer in range(send.shape[0]):
-            send[peer, tile * 8:tile * 8 + 8, :] = block
+            send[peer, 8 * line:8 * line + 8, :] = packed
 
 
 def all_steps(cols, rows, waves, first_z, spread, state, halos):
@@ -468,10 +460,13 @@
     whole = parts[0]
     for wave in range(1, waves):
         whole = whole + parts[wave]
-    for n in range(lines):
-        spread = jnp.broadcast_to(whole[n:n + 1, :], (8, 128))
-        moved = staggered(spread, 128 - DZ)
-        out[n // 2, 8 * (n % 2):8 * (n % 2) + 8, :] = moved[:, 0:DZ]
+    for line in range(lines // 8):
+        for n in range(8):
+            x, half = (8 * line + n) // 2, n % 2
+            block = whole[8 * line:8 * line + 8, :]
+            if n:
+                block = pltpu.roll(block, 128 - DZ * n, 1)
+            out[x, 8 * half:8 * half + 8, :] = block[:, 0:DZ]
 
 
 def gradient_of(parts):

time: 54.5 us -> 54.1 us (level)
  no operation moved by 1% of the time
where the time goes in v5:
time: 54.1 us; the launch traced here: 53.6 us
  starting transfers between devices  28.6 us (53%)
  waiting for transfers between devices  11.1 us (21%)
  Pallas kernels  9.66 us (18%)
  local copies, waits for them, and re-layouts  2.98 us (6%)
  between operations  1.39 us (3%)
    ppermute x6, starting transfers between devices, swap(): return lax.ppermute(value, 'tile', swap_pairs(count, cols, along_x, odd))  19.9 us
    all_to_all x1, starting transfers between devices, per_device(): parts = lax.all_to_all(send, 'wave', 0, 0)  8.66 us
    all_to_all x1, waiting for transfers between devices, per_device(): parts = lax.all_to_all(send, 'wave', 0, 0)  8.15 us
    pallas_call x1, Pallas kernels, all_steps(): pl.pallas_call(functools.partial(steps_kernel, cols, rows), out_shape=(ou...  5.21 us
    unnamed x4, local copies, waits for them, and re-layouts  2.98 us
    ppermute x6, waiting for transfers between devices, swap(): return lax.ppermute(value, 'tile', swap_pairs(count, cols, along_x, odd))  2.92 us
    pallas_call x1, Pallas kernels, load(): pl.pallas_call(functools.partial(load_kernel, cols), out_shape=(jax.Shape...  1.82 us
    pallas_call x1, Pallas kernels, edges(): pl.pallas_call(functools.partial(edges_kernel, cols), out_shape=(layers,...  1.36 us
  transfers between devices with their start and end apart: 7, of which 3 were waited for; matrix products, arithmetic and copies ran while one was open for 6% of the time, Pallas kernels for 4%

profile of v5, /device:TPU:200, one launch (start us, length us, event | category | flops | bytes accessed | tf_op | source)
XLA Modules:
  0.0 53.6 jit_solution(2981964990176580625)
XLA Ops:
  0.6 1.4 %edges.1 = (f32[53,16,128]{2,1,0:T(8,128)S(1)}, f32[53,16,128]{2,1,0:T(8,128)S(1)}) custom-call(f32[3,16,16,128]{3,2,1,0:T(8,128)} %bitcast.12, f32[3,16,16,128]{3,2,1,0:T(8,128)} %bitcast.14, f32[3,16,16,128]{3,2,1,0:T(8,128)} %bitcast.16, f32[3,16,16,128]{3,2,1,0:T(8,128)} %bitcast.18, s32[16,16,128]{2,1,0:T(8,128)} %kind.3, s32[16,16,128]{2,1,0:T(8,128)} %depth.3), custom_call_target="tpu_custom_call" | custom-call | flops 1048576 | bytes 1048576 | tf_op jit(solution)/shard_map/edges/pallas_call | solution.py:95
  2.0 1.9 %collective-permute-start = (f32[53,16,128]{2,1,0:T(8,128)S(1)}, f32[53,16,128]{2,1,0:T(8,128)S(1)}, u32[]{:S(2)}, u32[]{:S(2)}) collective-permute-start(f32[53,16,128]{2,1,0:T(8,128)S(1)} %get-tuple-element.27.after), channel_id=1, source_target_pairs={{0,8},{1,9},{2,10},{3,11},{4,12},{5,13},{6,14},{7,15},{8,0},{9,1},... | collective-permute-start | bytes 1302536 | tf_op jit(solution)/shard_map/ppermute | solution.py:493
  3.9 7.0 %collective-permute-start.1 = (f32[53,16,128]{2,1,0:T(8,128)S(1)}, f32[53,16,128]{2,1,0:T(8,128)S(1)}, u32[]{:S(2)}, u32[]{:S(2)}) collective-permute-start(f32[53,16,128]{2,1,0:T(8,128)S(1)} %get-tuple-element.34), channel_id=1, source_target_pairs={{8,16},{9,17},{10,18},{11,19},{12,20},{13,21},{14,22},{15,23},{16,... | collective-permute-start | bytes 1302536 | tf_op jit(solution)/shard_map/ppermute | solution.py:493
  10.9 1.8 %load.1 = (f32[12,24,24,128]{3,2,1,0:T(8,128)S(1)}, f32[24,24,128]{2,1,0:T(8,128)S(1)}, f32[24,24,128]{2,1,0:T(8,128)S(1)}, f32[24,24,128]{2,1,0:T(8,128)S(1)}, ...) custom-call(f32[1,4]{1,0:T(1,128)} %eps_table.1, ...), custom_call_target="tpu_custom_call" | custom-call | flops 1073741824 | bytes 4194304 | tf_op jit(solution)/shard_map/load/pallas_call | solution.py:160
  12.7 1.9 %collective-permute-start.2 = (f32[224,4,128]{2,1,0:T(4,128)S(1)}, f32[224,4,128]{2,1,0:T(4,128)S(1)}, u32[]{:S(2)}, u32[]{:S(2)}) collective-permute-start(f32[224,4,128]{2,1,0:T(4,128)S(1)} %get-tuple-element.35), channel_id=1, source_target_pairs={{1,2},{2,1},{3,4},{4,3},{5,6},{6,5},{9,10},{10,9},{11,12},{12,11},... | collective-permute-start | bytes 1376264 | tf_op jit(solution)/shard_map/ppermute | solution.py:493
  14.6 3.6 %collective-permute-start.3 = (f32[224,4,128]{2,1,0:T(4,128)S(1)}, f32[224,4,128]{2,1,0:T(4,128)S(1)}, u32[]{:S(2)}, u32[]{:S(2)}) collective-permute-start(f32[224,4,128]{2,1,0:T(4,128)S(1)} %get-tuple-element.36), channel_id=1, source_target_pairs={{0,1},{1,0},{2,3},{3,2},{4,5},{5,4},{6,7},{7,6},{8,9},{9,8},{10,11... | collective-permute-start | bytes 1376264 | tf_op jit(solution)/shard_map/ppermute | solution.py:493
  18.9 0.0 collective-permute-done.ra
  18.9 1.7 %collective-permute-done.1.rb = f32[53,16,128]{2,1,0:T(8,128)S(1)} collective-permute-done((f32[53,16,128]{2,1,0:T(8,128)S(1)}, f32[53,16,128]{2,1,0:T(8,128)S(1)}, u32[]{:S(2)}, u32[]{:S(2)}) %collective-permute-start.1) | collective-permute-done | bytes 434208 | tf_op jit(solution)/shard_map/ppermute | solution.py:493
  20.6 0.1 corners.1
  20.7 1.9 %collective-permute-start.4 = (f32[106,4,128]{2,1,0:T(4,128)S(1)}, f32[106,4,128]{2,1,0:T(4,128)S(1)}, u32[]{:S(2)}, u32[]{:S(2)}) collective-permute-start(f32[106,4,128]{2,1,0:T(4,128)S(1)} %get-tuple-element.42), channel_id=1, source_target_pairs={{1,2},{2,1},{3,4},{4,3},{5,6},{6,5},{9,10},{10,9},{11,12},{12,11},... | collective-permute-start | bytes 651272 | tf_op jit(solution)/shard_map/ppermute | solution.py:493
  22.6 3.6 %collective-permute-start.5 = (f32[106,4,128]{2,1,0:T(4,128)S(1)}, f32[106,4,128]{2,1,0:T(4,128)S(1)}, u32[]{:S(2)}, u32[]{:S(2)}) collective-permute-start(f32[106,4,128]{2,1,0:T(4,128)S(1)} %get-tuple-element.43), channel_id=1, source_target_pairs={{0,1},{1,0},{2,3},{3,2},{4,5},{5,4},{6,7},{7,6},{8,9},{9,8},{10,11... | collective-permute-start | bytes 651272 | tf_op jit(solution)/shard_map/ppermute | solution.py:493
  26.2 0.0 collective-permute-done.2.ryb
  26.2 0.0 collective-permute-done.3.rya
  26.2 0.4 prepare.1
  26.7 1.2 %collective-permute-done.4.rcb = f32[106,4,128]{2,1,0:T(4,128)S(1)} collective-permute-done((f32[106,4,128]{2,1,0:T(4,128)S(1)}, f32[106,4,128]{2,1,0:T(4,128)S(1)}, u32[]{:S(2)}, u32[]{:S(2)}) %collective-permute-start.4) | collective-permute-done | bytes 217120 | tf_op jit(solution)/shard_map/ppermute | solution.py:493
  27.9 0.0 collective-permute-done.5.rca
  27.9 5.2 %steps.1 = (f32[3,16,16,128]{3,2,1,0:T(8,128)S(1)}, f32[3,16,16,128]{3,2,1,0:T(8,128)S(1)}, f32[3,16,16,128]{3,2,1,0:T(8,128)S(1)}, f32[3,16,16,128]{3,2,1,0:T(8...) custom-call(s32[1]{0:T(128)S(6)} %copy.37.first_z, ...), custom_call_target="tpu_custom_call", output_to_operand_aliasing={{5}: (2, {}), {6}: (3, {}), {7}: (4, {}), {8}: (5, {}), {9}... | custom-call | tf_op jit(solution)/shard_map/steps/pallas_call | solution.py:440
  33.1 8.7 %all-to-all-start = ((f32[8,32,128]{2,1,0:T(8,128)}), f32[8,32,128]{2,1,0:T(8,128)S(1)}, u32[]{:S(2)}, u32[]{:S(2)}) async-start(f32[8,32,128]{2,1,0:T(8,128)} %get-tuple-element.48), calls=%async_computation | async-start | bytes 262144 | tf_op jit(solution)/shard_map/all_to_all | solution.py:507
  41.8 0.7 %copy.33 = f32[1,3,16,16,128]{4,3,2,1,0:T(8,128)} copy(f32[1,3,16,16,128]{4,3,2,1,0:T(8,128)S(1)} %bitcast.11) | data formatting | bytes 786432
  42.5 0.7 %copy.34 = f32[1,3,16,16,128]{4,3,2,1,0:T(8,128)} copy(f32[1,3,16,16,128]{4,3,2,1,0:T(8,128)S(1)} %bitcast.10) | data formatting | bytes 786432
  43.2 0.7 %copy.35 = f32[1,3,16,16,128]{4,3,2,1,0:T(8,128)} copy(f32[1,3,16,16,128]{4,3,2,1,0:T(8,128)S(1)} %bitcast.9) | data formatting | bytes 786432
  44.0 0.7 %copy.36 = f32[1,3,16,16,128]{4,3,2,1,0:T(8,128)} copy(f32[1,3,16,16,128]{4,3,2,1,0:T(8,128)S(1)} %bitcast.8) | data formatting | bytes 786432
  44.7 8.1 %all-to-all-done.parts = f32[8,32,128]{2,1,0:T(8,128)S(1)} async-done(((f32[8,32,128]{2,1,0:T(8,128)}), f32[8,32,128]{2,1,0:T(8,128)S(1)}, u32[]{:S(2)}, u32[]{:S(2)}) %all-to-all-start) | async-done | bytes 131104 | tf_op jit(solution)/shard_map/all_to_all | solution.py:507
  52.9 0.8 %gradient.1 = f32[16,16,16]{2,1,0:T(8,128)} custom-call(f32[8,32,128]{2,1,0:T(8,128)S(1)} %all-to-all-done.parts), custom_call_target="tpu_custom_call" | custom-call | tf_op jit(solution)/shard_map/gradient/pallas_call | solution.py:474
Async XLA Ops:
  2.0 16.9 %collective-permute-start = (f32[53,16,128]{2,1,0:T(8,128)S(1)}, f32[53,16,128]{2,1,0:T(8,128)S(1)}, u32[]{:S(2)}, u32[]{:S(2)}) collective-permute-start(f32[53,16,128]{2,1,0:T(8,128)S(1)} %get-tuple-element.27.after), channel_id=1, source_target_pairs={{0,8},{1,9},{2,10},{3,11},{4,12},{5,13},{6,14},{7,15},{8,0},{9,1},... | collective-permute-start | bytes 1302536 | tf_op jit(solution)/shard_map/ppermute | solution.py:493
  3.9 16.7 %collective-permute-start.1 = (f32[53,16,128]{2,1,0:T(8,128)S(1)}, f32[53,16,128]{2,1,0:T(8,128)S(1)}, u32[]{:S(2)}, u32[]{:S(2)}) collective-permute-start(f32[53,16,128]{2,1,0:T(8,128)S(1)} %get-tuple-element.34), channel_id=1, source_target_pairs={{8,16},{9,17},{10,18},{11,19},{12,20},{13,21},{14,22},{15,23},{16,... | collective-permute-start | bytes 1302536 | tf_op jit(solution)/shard_map/ppermute | solution.py:493
  12.7 13.5 %collective-permute-start.2 = (f32[224,4,128]{2,1,0:T(4,128)S(1)}, f32[224,4,128]{2,1,0:T(4,128)S(1)}, u32[]{:S(2)}, u32[]{:S(2)}) collective-permute-start(f32[224,4,128]{2,1,0:T(4,128)S(1)} %get-tuple-element.35), channel_id=1, source_target_pairs={{1,2},{2,1},{3,4},{4,3},{5,6},{6,5},{9,10},{10,9},{11,12},{12,11},... | collective-permute-start | bytes 1376264 | tf_op jit(solution)/shard_map/ppermute | solution.py:493
  14.6 11.6 %collective-permute-start.3 = (f32[224,4,128]{2,1,0:T(4,128)S(1)}, f32[224,4,128]{2,1,0:T(4,128)S(1)}, u32[]{:S(2)}, u32[]{:S(2)}) collective-permute-start(f32[224,4,128]{2,1,0:T(4,128)S(1)} %get-tuple-element.36), channel_id=1, source_target_pairs={{0,1},{1,0},{2,3},{3,2},{4,5},{5,4},{6,7},{7,6},{8,9},{9,8},{10,11... | collective-permute-start | bytes 1376264 | tf_op jit(solution)/shard_map/ppermute | solution.py:493
  20.7 7.2 %collective-permute-start.4 = (f32[106,4,128]{2,1,0:T(4,128)S(1)}, f32[106,4,128]{2,1,0:T(4,128)S(1)}, u32[]{:S(2)}, u32[]{:S(2)}) collective-permute-start(f32[106,4,128]{2,1,0:T(4,128)S(1)} %get-tuple-element.42), channel_id=1, source_target_pairs={{1,2},{2,1},{3,4},{4,3},{5,6},{6,5},{9,10},{10,9},{11,12},{12,11},... | collective-permute-start | bytes 651272 | tf_op jit(solution)/shard_map/ppermute | solution.py:493
  22.6 5.3 %collective-permute-start.5 = (f32[106,4,128]{2,1,0:T(4,128)S(1)}, f32[106,4,128]{2,1,0:T(4,128)S(1)}, u32[]{:S(2)}, u32[]{:S(2)}) collective-permute-start(f32[106,4,128]{2,1,0:T(4,128)S(1)} %get-tuple-element.43), channel_id=1, source_target_pairs={{0,1},{1,0},{2,3},{3,2},{4,5},{5,4},{6,7},{7,6},{8,9},{9,8},{10,11... | collective-permute-start | bytes 651272 | tf_op jit(solution)/shard_map/ppermute | solution.py:493
  33.1 19.8 %all-to-all-start = ((f32[8,32,128]{2,1,0:T(8,128)}), f32[8,32,128]{2,1,0:T(8,128)S(1)}, u32[]{:S(2)}, u32[]{:S(2)}) async-start(f32[8,32,128]{2,1,0:T(8,128)} %get-tuple-element.48), calls=%async_computation | async-start | bytes 262144 | tf_op jit(solution)/shard_map/all_to_all | solution.py:507

commit v6 on v5

--- a/solution.py
+++ b/solution.py
@@ -12,7 +12,7 @@
 TILE_COLS = 8
 HALO = STEPS
 KINDS = 14
-UNROLL = 5
+UNROLL = 4
 CORNER_FLOPS = 2**36
 LOAD_FLOPS = 2**30
 PREPARE_FLOPS = 2**36
@@ -387,6 +387,12 @@
             if not last or (k in (3, 9)):
                 field[k + n, x] = new[n]
 
+    def before_first(x):
+        for e, h in parts:
+            new = h_new(e, h, x)
+            for n in (1, 2):
+                field[h + n, x] = new[n]
+
     def h_rows(x0, count, last):
         news = [[h_new(e, h, x0 + u) for u in range(count)] for e, h in parts]
         for (_, h), new in zip(parts, news):
@@ -411,7 +417,7 @@
     for step in range(STEPS):
         last = step == STEPS - 1
         pairs = (wide - 2 - 2 * step) // 2
-        h_rows(step, 1, False)
+        before_first(step)
         h_rows(step + 1, 2, last)
 
         def two_rows(i, _):

time: 54.1 us -> 54 us (level)
  no operation moved by 1% of the time
where the time goes in v6:
time: 54 us; the launch traced here: 53.5 us
  starting transfers between devices  28.6 us (53%)
  waiting for transfers between devices  11.1 us (21%)
  Pallas kernels  9.53 us (18%)
  local copies, waits for them, and re-layouts  2.98 us (6%)
  between operations  1.39 us (3%)
    ppermute x6, starting transfers between devices, swap(): return lax.ppermute(value, 'tile', swap_pairs(count, cols, along_x, odd))  19.9 us
    all_to_all x1, starting transfers between devices, per_device(): parts = lax.all_to_all(send, 'wave', 0, 0)  8.66 us
    all_to_all x1, waiting for transfers between devices, per_device(): parts = lax.all_to_all(send, 'wave', 0, 0)  8.15 us
    pallas_call x1, Pallas kernels, all_steps(): pl.pallas_call(functools.partial(steps_kernel, cols, rows), out_shape=(ou...  5.08 us
    unnamed x4, local copies, waits for them, and re-layouts  2.98 us
    ppermute x6, waiting for transfers between devices, swap(): return lax.ppermute(value, 'tile', swap_pairs(count, cols, along_x, odd))  2.92 us
    pallas_call x1, Pallas kernels, load(): pl.pallas_call(functools.partial(load_kernel, cols), out_shape=(jax.Shape...  1.82 us
    pallas_call x1, Pallas kernels, edges(): pl.pallas_call(functools.partial(edges_kernel, cols), out_shape=(layers,...  1.36 us
  transfers between devices with their start and end apart: 7, of which 3 were waited for; matrix products, arithmetic and copies ran while one was open for 6% of the time, Pallas kernels for 4%

profile of v6, /device:TPU:200, one launch (start us, length us, event | category | flops | bytes accessed | tf_op | source)
XLA Modules:
  0.0 53.5 jit_solution(679835292331951950)
XLA Ops:
  0.6 1.4 %edges.1 = (f32[53,16,128]{2,1,0:T(8,128)S(1)}, f32[53,16,128]{2,1,0:T(8,128)S(1)}) custom-call(f32[3,16,16,128]{3,2,1,0:T(8,128)} %bitcast.12, f32[3,16,16,128]{3,2,1,0:T(8,128)} %bitcast.14, f32[3,16,16,128]{3,2,1,0:T(8,128)} %bitcast.16, f32[3,16,16,128]{3,2,1,0:T(8,128)} %bitcast.18, s32[16,16,128]{2,1,0:T(8,128)} %kind.3, s32[16,16,128]{2,1,0:T(8,128)} %depth.3), custom_call_target="tpu_custom_call" | custom-call | flops 1048576 | bytes 1048576 | tf_op jit(solution)/shard_map/edges/pallas_call | solution.py:95
  2.0 1.9 %collective-permute-start = (f32[53,16,128]{2,1,0:T(8,128)S(1)}, f32[53,16,128]{2,1,0:T(8,128)S(1)}, u32[]{:S(2)}, u32[]{:S(2)}) collective-permute-start(f32[53,16,128]{2,1,0:T(8,128)S(1)} %get-tuple-element.27.after), channel_id=1, source_target_pairs={{0,8},{1,9},{2,10},{3,11},{4,12},{5,13},{6,14},{7,15},{8,0},{9,1},... | collective-permute-start | bytes 1302536 | tf_op jit(solution)/shard_map/ppermute | solution.py:499
  3.9 7.0 %collective-permute-start.1 = (f32[53,16,128]{2,1,0:T(8,128)S(1)}, f32[53,16,128]{2,1,0:T(8,128)S(1)}, u32[]{:S(2)}, u32[]{:S(2)}) collective-permute-start(f32[53,16,128]{2,1,0:T(8,128)S(1)} %get-tuple-element.34), channel_id=1, source_target_pairs={{8,16},{9,17},{10,18},{11,19},{12,20},{13,21},{14,22},{15,23},{16,... | collective-permute-start | bytes 1302536 | tf_op jit(solution)/shard_map/ppermute | solution.py:499
  10.9 1.8 %load.1 = (f32[12,24,24,128]{3,2,1,0:T(8,128)S(1)}, f32[24,24,128]{2,1,0:T(8,128)S(1)}, f32[24,24,128]{2,1,0:T(8,128)S(1)}, f32[24,24,128]{2,1,0:T(8,128)S(1)}, ...) custom-call(f32[1,4]{1,0:T(1,128)} %eps_table.1, ...), custom_call_target="tpu_custom_call" | custom-call | flops 1073741824 | bytes 4194304 | tf_op jit(solution)/shard_map/load/pallas_call | solution.py:160
  12.7 1.9 %collective-permute-start.2 = (f32[224,4,128]{2,1,0:T(4,128)S(1)}, f32[224,4,128]{2,1,0:T(4,128)S(1)}, u32[]{:S(2)}, u32[]{:S(2)}) collective-permute-start(f32[224,4,128]{2,1,0:T(4,128)S(1)} %get-tuple-element.35), channel_id=1, source_target_pairs={{1,2},{2,1},{3,4},{4,3},{5,6},{6,5},{9,10},{10,9},{11,12},{12,11},... | collective-permute-start | bytes 1376264 | tf_op jit(solution)/shard_map/ppermute | solution.py:499
  14.6 3.6 %collective-permute-start.3 = (f32[224,4,128]{2,1,0:T(4,128)S(1)}, f32[224,4,128]{2,1,0:T(4,128)S(1)}, u32[]{:S(2)}, u32[]{:S(2)}) collective-permute-start(f32[224,4,128]{2,1,0:T(4,128)S(1)} %get-tuple-element.36), channel_id=1, source_target_pairs={{0,1},{1,0},{2,3},{3,2},{4,5},{5,4},{6,7},{7,6},{8,9},{9,8},{10,11... | collective-permute-start | bytes 1376264 | tf_op jit(solution)/shard_map/ppermute | solution.py:499
  18.9 0.0 collective-permute-done.ra
  18.9 1.7 %collective-permute-done.1.rb = f32[53,16,128]{2,1,0:T(8,128)S(1)} collective-permute-done((f32[53,16,128]{2,1,0:T(8,128)S(1)}, f32[53,16,128]{2,1,0:T(8,128)S(1)}, u32[]{:S(2)}, u32[]{:S(2)}) %collective-permute-start.1) | collective-permute-done | bytes 434208 | tf_op jit(solution)/shard_map/ppermute | solution.py:499
  20.6 0.1 corners.1
  20.7 1.9 %collective-permute-start.4 = (f32[106,4,128]{2,1,0:T(4,128)S(1)}, f32[106,4,128]{2,1,0:T(4,128)S(1)}, u32[]{:S(2)}, u32[]{:S(2)}) collective-permute-start(f32[106,4,128]{2,1,0:T(4,128)S(1)} %get-tuple-element.42), channel_id=1, source_target_pairs={{1,2},{2,1},{3,4},{4,3},{5,6},{6,5},{9,10},{10,9},{11,12},{12,11},... | collective-permute-start | bytes 651272 | tf_op jit(solution)/shard_map/ppermute | solution.py:499
  22.6 3.6 %collective-permute-start.5 = (f32[106,4,128]{2,1,0:T(4,128)S(1)}, f32[106,4,128]{2,1,0:T(4,128)S(1)}, u32[]{:S(2)}, u32[]{:S(2)}) collective-permute-start(f32[106,4,128]{2,1,0:T(4,128)S(1)} %get-tuple-element.43), channel_id=1, source_target_pairs={{0,1},{1,0},{2,3},{3,2},{4,5},{5,4},{6,7},{7,6},{8,9},{9,8},{10,11... | collective-permute-start | bytes 651272 | tf_op jit(solution)/shard_map/ppermute | solution.py:499
  26.2 0.0 collective-permute-done.2.ryb
  26.2 0.0 collective-permute-done.3.rya
  26.2 0.4 prepare.1
  26.7 1.2 %collective-permute-done.4.rcb = f32[106,4,128]{2,1,0:T(4,128)S(1)} collective-permute-done((f32[106,4,128]{2,1,0:T(4,128)S(1)}, f32[106,4,128]{2,1,0:T(4,128)S(1)}, u32[]{:S(2)}, u32[]{:S(2)}) %collective-permute-start.4) | collective-permute-done | bytes 217120 | tf_op jit(solution)/shard_map/ppermute | solution.py:499
  27.9 0.0 collective-permute-done.5.rca
  27.9 5.1 %steps.1 = (f32[3,16,16,128]{3,2,1,0:T(8,128)S(1)}, f32[3,16,16,128]{3,2,1,0:T(8,128)S(1)}, f32[3,16,16,128]{3,2,1,0:T(8,128)S(1)}, f32[3,16,16,128]{3,2,1,0:T(8...) custom-call(s32[1]{0:T(128)S(6)} %copy.37.first_z, ...), custom_call_target="tpu_custom_call", output_to_operand_aliasing={{5}: (2, {}), {6}: (3, {}), {7}: (4, {}), {8}: (5, {}), {9}... | custom-call | tf_op jit(solution)/shard_map/steps/pallas_call | solution.py:446
  33.0 8.7 %all-to-all-start = ((f32[8,32,128]{2,1,0:T(8,128)}), f32[8,32,128]{2,1,0:T(8,128)S(1)}, u32[]{:S(2)}, u32[]{:S(2)}) async-start(f32[8,32,128]{2,1,0:T(8,128)} %get-tuple-element.48), calls=%async_computation | async-start | bytes 262144 | tf_op jit(solution)/shard_map/all_to_all | solution.py:513
  41.6 0.7 %copy.33 = f32[1,3,16,16,128]{4,3,2,1,0:T(8,128)} copy(f32[1,3,16,16,128]{4,3,2,1,0:T(8,128)S(1)} %bitcast.11) | data formatting | bytes 786432
  42.4 0.7 %copy.34 = f32[1,3,16,16,128]{4,3,2,1,0:T(8,128)} copy(f32[1,3,16,16,128]{4,3,2,1,0:T(8,128)S(1)} %bitcast.10) | data formatting | bytes 786432
  43.1 0.7 %copy.35 = f32[1,3,16,16,128]{4,3,2,1,0:T(8,128)} copy(f32[1,3,16,16,128]{4,3,2,1,0:T(8,128)S(1)} %bitcast.9) | data formatting | bytes 786432
  43.9 0.7 %copy.36 = f32[1,3,16,16,128]{4,3,2,1,0:T(8,128)} copy(f32[1,3,16,16,128]{4,3,2,1,0:T(8,128)S(1)} %bitcast.8) | data formatting | bytes 786432
  44.6 8.1 %all-to-all-done.parts = f32[8,32,128]{2,1,0:T(8,128)S(1)} async-done(((f32[8,32,128]{2,1,0:T(8,128)}), f32[8,32,128]{2,1,0:T(8,128)S(1)}, u32[]{:S(2)}, u32[]{:S(2)}) %all-to-all-start) | async-done | bytes 131104 | tf_op jit(solution)/shard_map/all_to_all | solution.py:513
  52.8 0.8 %gradient.1 = f32[16,16,16]{2,1,0:T(8,128)} custom-call(f32[8,32,128]{2,1,0:T(8,128)S(1)} %all-to-all-done.parts), custom_call_target="tpu_custom_call" | custom-call | tf_op jit(solution)/shard_map/gradient/pallas_call | solution.py:480
Async XLA Ops:
  2.0 16.9 %collective-permute-start = (f32[53,16,128]{2,1,0:T(8,128)S(1)}, f32[53,16,128]{2,1,0:T(8,128)S(1)}, u32[]{:S(2)}, u32[]{:S(2)}) collective-permute-start(f32[53,16,128]{2,1,0:T(8,128)S(1)} %get-tuple-element.27.after), channel_id=1, source_target_pairs={{0,8},{1,9},{2,10},{3,11},{4,12},{5,13},{6,14},{7,15},{8,0},{9,1},... | collective-permute-start | bytes 1302536 | tf_op jit(solution)/shard_map/ppermute | solution.py:499
  3.9 16.7 %collective-permute-start.1 = (f32[53,16,128]{2,1,0:T(8,128)S(1)}, f32[53,16,128]{2,1,0:T(8,128)S(1)}, u32[]{:S(2)}, u32[]{:S(2)}) collective-permute-start(f32[53,16,128]{2,1,0:T(8,128)S(1)} %get-tuple-element.34), channel_id=1, source_target_pairs={{8,16},{9,17},{10,18},{11,19},{12,20},{13,21},{14,22},{15,23},{16,... | collective-permute-start | bytes 1302536 | tf_op jit(solution)/shard_map/ppermute | solution.py:499
  12.7 13.5 %collective-permute-start.2 = (f32[224,4,128]{2,1,0:T(4,128)S(1)}, f32[224,4,128]{2,1,0:T(4,128)S(1)}, u32[]{:S(2)}, u32[]{:S(2)}) collective-permute-start(f32[224,4,128]{2,1,0:T(4,128)S(1)} %get-tuple-element.35), channel_id=1, source_target_pairs={{1,2},{2,1},{3,4},{4,3},{5,6},{6,5},{9,10},{10,9},{11,12},{12,11},... | collective-permute-start | bytes 1376264 | tf_op jit(solution)/shard_map/ppermute | solution.py:499
  14.6 11.6 %collective-permute-start.3 = (f32[224,4,128]{2,1,0:T(4,128)S(1)}, f32[224,4,128]{2,1,0:T(4,128)S(1)}, u32[]{:S(2)}, u32[]{:S(2)}) collective-permute-start(f32[224,4,128]{2,1,0:T(4,128)S(1)} %get-tuple-element.36), channel_id=1, source_target_pairs={{0,1},{1,0},{2,3},{3,2},{4,5},{5,4},{6,7},{7,6},{8,9},{9,8},{10,11... | collective-permute-start | bytes 1376264 | tf_op jit(solution)/shard_map/ppermute | solution.py:499
  20.7 7.2 %collective-permute-start.4 = (f32[106,4,128]{2,1,0:T(4,128)S(1)}, f32[106,4,128]{2,1,0:T(4,128)S(1)}, u32[]{:S(2)}, u32[]{:S(2)}) collective-permute-start(f32[106,4,128]{2,1,0:T(4,128)S(1)} %get-tuple-element.42), channel_id=1, source_target_pairs={{1,2},{2,1},{3,4},{4,3},{5,6},{6,5},{9,10},{10,9},{11,12},{12,11},... | collective-permute-start | bytes 651272 | tf_op jit(solution)/shard_map/ppermute | solution.py:499
  22.6 5.3 %collective-permute-start.5 = (f32[106,4,128]{2,1,0:T(4,128)S(1)}, f32[106,4,128]{2,1,0:T(4,128)S(1)}, u32[]{:S(2)}, u32[]{:S(2)}) collective-permute-start(f32[106,4,128]{2,1,0:T(4,128)S(1)} %get-tuple-element.43), channel_id=1, source_target_pairs={{0,1},{1,0},{2,3},{3,2},{4,5},{5,4},{6,7},{7,6},{8,9},{9,8},{10,11... | collective-permute-start | bytes 651272 | tf_op jit(solution)/shard_map/ppermute | solution.py:499
  33.0 19.8 %all-to-all-start = ((f32[8,32,128]{2,1,0:T(8,128)}), f32[8,32,128]{2,1,0:T(8,128)S(1)}, u32[]{:S(2)}, u32[]{:S(2)}) async-start(f32[8,32,128]{2,1,0:T(8,128)} %get-tuple-element.48), calls=%async_computation | async-start | bytes 262144 | tf_op jit(solution)/shard_map/all_to_all | solution.py:513
